TPU v7x, 32 devices: a whole 2x2x4 slice. The times are simulated.
32 devices in a mesh: wa: 8 (over z, x), ha: 4 (over y, core).
Axes of the slice: x: 2, y: 2, z: 4, core: 2. Of those that a mesh axis runs over, the one named last changes fastest.
Arguments:
- tokens: bfloat16 [256, 16384], P('ha', 'wa'), may hold values from -100 to 100, as said below
- norm_gain: float32 [16384], P('wa'), may hold values from 0.5 to 1.5
- gate_weight: bfloat16 [16384, 26624], P('wa', 'ha'), may hold values from -0.046875 to 0.046875
- up_weight: bfloat16 [16384, 26624], P('wa', 'ha'), may hold values from -0.046875 to 0.046875
- down_weight: bfloat16 [26624, 16384], P('ha', 'wa'), may hold values from -0.0390625 to 0.0390625
Outputs:
- mixed: bfloat16 [256, 16384], P('ha', 'wa')
Inputs may be any that keep to these rules, and one draw needn't show every extreme that they name: `tokens`: real-valued activations.
All inputs are finite; a program needn't handle non-finite values.
Results may differ from a plain program's by a relative error of at most 0.0064.
Values may be sent and summed in bfloat16 or wider, within the bound.
No kernel may reach another device: no remote copies, remote signals or barrier semaphores. Data moves between devices by JAX's collectives and lax.ppermute only.
A program may use at most 192 MiB of HBM per device.

v0:
```python
import jax
import jax.numpy as jnp
from jax import lax
from jax.sharding import PartitionSpec as P


def apply_norm(own_values, squares, norm_gain):
    model_width = own_values.shape[1] * lax.axis_size("wa")
    mean_square = squares[:, None] / model_width
    return (own_values * lax.rsqrt(mean_square + 1e-05) * norm_gain[None, :]).astype(jnp.bfloat16)


def activate(summed, hidden_width):
    gate = summed[:, :hidden_width]
    up = summed[:, hidden_width:]
    return (jax.nn.silu(gate) * up).astype(jnp.bfloat16)


def body(tokens, norm_gain, gate_weight, up_weight, down_weight):
    gathered = lax.all_gather(tokens, "ha", axis=0, tiled=True)
    own_values = gathered.astype(jnp.float32)
    squares = lax.psum(jnp.sum(own_values * own_values, axis=1), "wa")
    normed = apply_norm(own_values, squares, norm_gain)
    hidden_width = gate_weight.shape[1]
    gate_part = jnp.dot(normed, gate_weight, preferred_element_type=jnp.float32)
    up_part = jnp.dot(normed, up_weight, preferred_element_type=jnp.float32)
    summed = lax.psum_scatter(
        jnp.concatenate([gate_part, up_part], axis=1), "wa", scatter_dimension=0, tiled=True
    )
    hidden = activate(summed, hidden_width)
    partial_out = jnp.dot(
        lax.all_gather(hidden, "wa", axis=0, tiled=True),
        down_weight,
        preferred_element_type=jnp.float32,
    )
    mixed_out = lax.psum_scatter(partial_out, "ha", scatter_dimension=0, tiled=True)
    return mixed_out.astype(jnp.bfloat16)


def solution(mesh):
    placed = (P("ha", "wa"), P("wa"), P("wa", "ha"), P("wa", "ha"), P("ha", "wa"))
    return jax.shard_map(body, mesh=mesh, in_specs=placed, out_specs=P("ha", "wa"), check_vma=False)
```

profile of v0, /device:TPU:0, one launch (start us, length us, event | category | flops | bytes accessed | tf_op | source)
XLA Modules:
  0.0 418.5 jit_solution(10641940589857782830)
XLA Ops:
  6.5 0.0 all-gather.3.cloned.1.call-start
  6.5 0.7 all-gather.3.cloned.1.call-update
  7.3 0.0 reduce-scatter.3.cloned.1.call-start
  7.3 21.1 %all-gather.3.cloned.1.call-done = bf16[256,2048]{1,0:T(8,128)(2,1)} async-done(((bf16[64,2048]{1,0:T(8,128)(2,1)}), bf16[256,2048]{1,0:T(8,128)(2,1)}) %all-gather.3.cloned.1.call-update) | async-done | bytes 1048592 | tf_op jit(solution)/shard_map/all_gather | solution.py:20
  28.4 1.5 fusion
  29.9 21.4 %psum.7 = f32[256]{0:T(256)S(1)} all-reduce(f32[256]{0:T(256)S(1)} %fusion), channel_id=1, replica_groups=mesh['wa'=8,'ha'=4] {'wa'}, use_global_device_ids=true, to_apply=%region_1.0 | all-reduce | flops 256 | bytes 2048 | tf_op jit(solution)/shard_map/psum | solution.py:22
  51.2 0.0 copy-start
  51.2 0.0 copy-start.1
  51.3 13.0 %fusion.4 = f32[256,6656]{1,0:T(8,128)S(1)} fusion(bf16[2048,6656]{1,0:T(8,128)(2,1)} %param.8, bf16[256,2048]{1,0:T(8,128)(2,1)} %all-gather.3.cloned.1.call-done, f32[2048]{0:T(1024)} %param.6, f32[256]{0:T(256)S(1)} %add_rsqrt_fusion), kind=kOutput, calls=%fused_computation.8 | convolution fusion | flops 6981419008 | bytes 35136512 | tf_op jit(solution)/shard_map/dot_general | solution.py:26
  64.2 0.0 copy-done
  64.2 0.0 copy-done.1
  64.2 12.6 %fusion.6 = f32[256,6656]{1,0:T(8,128)S(1)} fusion(bf16[2048,6656]{1,0:T(8,128)(2,1)} %param.7, bf16[256,2048]{1,0:T(8,128)(2,1)S(1)} %copy-done, f32[2048]{0:T(1024)S(1)} %copy-done.1, f32[256]{0:T(256)S(1)} %add_rsqrt_fusion), kind=kOutput, calls=%fused_computation.9 | convolution fusion | flops 6981419008 | bytes 35136512 | tf_op jit(solution)/shard_map/dot_general | solution.py:25
  76.8 5.3 %pad_maximum_fusion = f32[256,13312]{1,0:T(8,128)} fusion(f32[256,6656]{1,0:T(8,128)S(1)} %fusion.4, f32[256,6656]{1,0:T(8,128)S(1)} %fusion.6), kind=kLoop, calls=%fused_computation | loop fusion | flops 3407872 | bytes 27262976 | tf_op jit(solution)/shard_map/concatenate | solution.py:28
  82.1 0.0 reduce-scatter.3.cloned.1.call-update
  82.1 0.0 all-gather.5.cloned.1.call-start
  82.2 218.2 %reduce-scatter.3.cloned.1.call-done = f32[32,13312]{1,0:T(8,128)} async-done(((f32[256,13312]{1,0:T(8,128)}), f32[32,13312]{1,0:T(8,128)}) %reduce-scatter.3.cloned.1.call-update) | async-done | bytes 1703952 | tf_op jit(solution)/shard_map/reduce_scatter | solution.py:27
  300.4 2.4 fusion.3
  302.8 0.0 all-gather.5.cloned.1.call-update
  302.8 0.0 reduce-scatter.5.cloned.1.call-start
  302.9 62.8 %all-gather.5.cloned.1.call-done = bf16[256,6656]{1,0:T(8,128)(2,1)} async-done(((bf16[32,6656]{1,0:T(8,128)(2,1)}), bf16[256,6656]{1,0:T(8,128)(2,1)}) %all-gather.5.cloned.1.call-update) | async-done | bytes 3407888 | tf_op jit(solution)/shard_map/all_gather | solution.py:32
  365.6 14.4 %fusion.8 = f32[256,2048]{1,0:T(8,128)} fusion(bf16[256,6656]{1,0:T(8,128)(2,1)} %all-gather.5.cloned.1.call-done, bf16[6656,2048]{1,0:T(8,128)(2,1)} %param.9), kind=kOutput, calls=%fused_computation.11 | convolution fusion | flops 6979321856 | bytes 32768000 | tf_op jit(solution)/shard_map/dot_general | solution.py:31
  380.1 0.0 reduce-scatter.5.cloned.1.call-update
  380.1 30.1 %reduce-scatter.5.cloned.1.call-done = f32[64,2048]{1,0:T(8,128)} async-done(((f32[256,2048]{1,0:T(8,128)}), f32[64,2048]{1,0:T(8,128)}) %reduce-scatter.5.cloned.1.call-update) | async-done | bytes 524304 | tf_op jit(solution)/shard_map/reduce_scatter | solution.py:36
  410.2 1.8 convert_element_type.15
  (1 shorter events, 0.0 us)
Async XLA Ops:
  6.5 21.8 %all-gather.3.cloned.1.call-start = ((), (), s32[]{:S(2)}) async-start(), calls=%async_computation.2 | async-start | bytes 1310720 | tf_op jit(solution)/shard_map/all_gather | solution.py:20
  7.3 293.1 %reduce-scatter.3.cloned.1.call-start = ((), (), s32[]{:S(2)}) async-start(), calls=%async_computation.3 | async-start | bytes 15335424 | tf_op jit(solution)/shard_map/reduce_scatter | solution.py:27
  51.2 13.0 %copy-start = (bf16[256,2048]{1,0:T(8,128)(2,1)S(1)}, bf16[256,2048]{1,0:T(8,128)(2,1)}, u32[]{:S(2)}) copy-start(bf16[256,2048]{1,0:T(8,128)(2,1)} %all-gather.3.cloned.1.call-done) | copy-start | bytes 3145732
  51.2 13.0 %copy-start.1 = (f32[2048]{0:T(1024)S(1)}, f32[2048]{0:T(1024)}, u32[]{:S(2)}) copy-start(f32[2048]{0:T(1024)} %param.6) | copy-start | bytes 24580
  82.1 283.5 %all-gather.5.cloned.1.call-start = ((), (), s32[]{:S(2)}) async-start(), calls=%async_computation.4 | async-start | bytes 3833856 | tf_op jit(solution)/shard_map/all_gather | solution.py:32
  302.8 107.4 %reduce-scatter.5.cloned.1.call-start = ((), (), s32[]{:S(2)}) async-start(), calls=%async_computation.5 | async-start | bytes 2621440 | tf_op jit(solution)/shard_map/reduce_scatter | solution.py:36
Sparse Core Ops, SparseCore 0:
  8.9 19.4 all-gather.2
  82.2 218.0 reduce-scatter.2
  302.9 62.6 all-gather.4
  380.2 29.9 reduce-scatter.4
where the time goes:
time: 419 us; the launch traced here: 418 us
  waiting for transfers between devices  333 us (79%)
  matrix products  40 us (10%)
  blocking collectives  21.4 us (5%)
  between operations  13.2 us (3%)
  other arithmetic  11 us (3%)
    reduce_scatter x1, waiting for transfers between devices, body(): lax.psum_scatter(jnp.concatenate([gate_part, up_part], axis=1), 'wa', sca...  218 us
    all_gather x1, waiting for transfers between devices, body(): lax.all_gather(hidden, 'wa', axis=0, tiled=True)  62.8 us
    reduce_scatter x1, waiting for transfers between devices, body(): lax.psum_scatter(partial_out, 'ha', scatter_dimension=0, tiled=True)  30.1 us
    psum x1, blocking collectives, body(): squares = lax.psum(jnp.sum(own_values * own_values, axis=1), 'wa')  21.4 us
    all_gather x1, waiting for transfers between devices, body(): gathered = lax.all_gather(tokens, 'ha', axis=0, tiled=True)  21.1 us
    dot_general x1, matrix products, body(): jnp.dot(lax.all_gather(hidden, 'wa', axis=0, tiled=True), down_weight, pr...  14.4 us
    dot_general x1, matrix products, body(): up_part = jnp.dot(normed, up_weight, preferred_element_type=jnp.float32)  13 us
    dot_general x1, matrix products, body(): gate_part = jnp.dot(normed, gate_weight, preferred_element_type=jnp.float32)  12.6 us
  transfers between devices with their start and end apart: 4, of which 4 were waited for; matrix products, arithmetic and copies ran while one was open for 0% of the time, Pallas kernels for 0%

commit v1 on v0

v1 whole, which is shorter than its diff:
```python
import functools

import jax
import jax.numpy as jnp
from jax import lax
from jax.experimental import pallas as pl
from jax.experimental.pallas import tpu as pltpu
from jax.sharding import PartitionSpec as P

F32, BF16 = jnp.float32, jnp.bfloat16
EPS = 1e-05
VMEM_LIMIT = 48 * 1024 * 1024

X_SWAP = [(i, i ^ 1) for i in range(8)]
Z_SWAP = [(i, i ^ 2) for i in range(8)]
Z_CROSS = [(i, 6 - (i & 6) + (i & 1)) for i in range(8)]
Z_IN = [(0, 2), (1, 3), (6, 4), (7, 5)]
Z_OUT = [(2, 0), (3, 1), (4, 6), (5, 7)]
Z_MID = [(2, 4), (3, 5), (4, 2), (5, 3)]
X_MID = [(2, 3), (3, 2), (4, 5), (5, 4)]
Y_SWAP = [(i, i ^ 2) for i in range(4)]
CORE_SWAP = [(i, i ^ 1) for i in range(4)]


def any_spec():
    return pl.BlockSpec(memory_space=pl.ANY)


class Chain:
    def __init__(self):
        self.token = None

    def call(self, kernel, args, out_shape, *, grid=(), in_specs=None, out_specs=None, scratch=(), aliases=None, flops=1, name=None):
        args = list(args)
        if in_specs is None:
            in_specs = [pl.BlockSpec(memory_space=pltpu.VMEM)] * len(args)
        if out_specs is None:
            out_specs = [pl.BlockSpec(memory_space=pltpu.VMEM)] * len(out_shape)
        n_in = len(args)
        extra = 0
        if self.token is not None:
            args.append(self.token)
            in_specs = list(in_specs) + [any_spec()]
            extra = 1

        def run(*refs):
            kernel(*refs[:n_in], *refs[n_in + extra:])

        outs = pl.pallas_call(
            run,
            out_shape=tuple(out_shape),
            grid=grid,
            in_specs=in_specs,
            out_specs=tuple(out_specs),
            scratch_shapes=scratch,
            input_output_aliases=aliases or {},
            compiler_params=pltpu.CompilerParams(vmem_limit_bytes=VMEM_LIMIT),
            cost_estimate=pl.CostEstimate(flops=flops, bytes_accessed=1024, transcendentals=0),
            name=name,
        )(*args)
        self.token = outs[0]
        return outs


def shape(dims, dtype):
    return jax.ShapeDtypeStruct(tuple(dims), dtype)


def base_block():
    place = lax.axis_index("wa")
    return 2 * lax.rem(place, 2) + jnp.where(place >= 4, 1, 0)


def swap_bits(b):
    return 2 * lax.rem(b, 2) + b // 2


def xor(a, b):
    return lax.bitwise_xor(a, b)


def squares_kernel(t_ref, o_ref):
    v = t_ref[...].astype(F32)
    total = jnp.sum(v * v, axis=1, keepdims=True)
    o_ref[...] = jnp.broadcast_to(total, o_ref.shape)


def add_kernel(a_ref, b_ref, o_ref):
    o_ref[...] = a_ref[...] + b_ref[...]


def rows_at(position, rows):
    return pl.ds(pl.multiple_of(position * rows, rows), rows)


def arrange_kernel(t0, t2, t1, t3, g_ref, o_ref):
    rows = t0.shape[0]
    first = xor(lax.axis_index("ha"), base_block())
    for flip, t in ((0, t0), (2, t2), (1, t1), (3, t3)):
        o_ref[rows_at(xor(first, flip), rows), :] = (t[...].astype(F32) * g_ref[...]).astype(BF16)


def norm_kernel(width, t0, t2, t1, t3, s0, s2, s1, s3, g_ref, o_ref, r_ref):
    rows = t0.shape[0]
    first = xor(lax.axis_index("ha"), base_block())
    for flip, t, s in ((0, t0, s0), (2, t2, s2), (1, t1, s1), (3, t3, s3)):
        factor = lax.rsqrt(s[...] / width + EPS)
        at = rows_at(xor(first, flip), rows)
        o_ref[at, :] = (t[...].astype(F32) * factor[:, :1] * g_ref[...]).astype(BF16)
        r_ref[at, :] = factor


def project_kernel(lhs_ref, g_ref, u_ref, keep_ref, send_ref):
    half = lhs_ref.shape[0] // 2
    for i, w in enumerate((g_ref, u_ref)):
        total = jnp.dot(lhs_ref[...], w[...], preferred_element_type=F32)
        keep_ref[i] = total[:half]
        send_ref[i] = total[half:].astype(BF16)


def inward_kernel(keep_ref, x_ref, o_ref):
    o_ref[...] = (keep_ref[...] + x_ref[...].astype(F32)).astype(BF16)


def middle_kernel(keep_ref, x_ref, in_ref, o_ref):
    o_ref[...] = (keep_ref[...] + x_ref[...].astype(F32) + in_ref[...].astype(F32)).astype(BF16)


def activate_kernel(scaled, keep_ref, x_ref, in_ref, mid_ref, r_ref, o_ref):
    total = keep_ref[...] + x_ref[...].astype(F32) + in_ref[...].astype(F32) + mid_ref[...].astype(F32)
    if scaled:
        total = total * r_ref[...][None, :, :1]
    gate, up = total[0], total[1]
    o_ref[...] = (gate / (1.0 + jnp.exp(-gate)) * up).astype(BF16)


def join_kernel(a_ref, b_ref, o_ref):
    rows = a_ref.shape[0]
    o_ref[:rows, :] = a_ref[...]
    o_ref[rows:, :] = b_ref[...]


def pass_kernel(a_ref, o_ref):
    del a_ref, o_ref


def down_kernel(first, last, *refs):
    refs = list(refs)
    own_ref, mid_ref, out1_ref, out2_ref, w_ref = refs[:5]
    refs = refs[5:]
    if not first:
        acc_ref = refs.pop(0)
    hid_ref = refs[-1]
    half = own_ref.shape[0]

    @pl.when(pl.program_id(0) == 0)
    def _():
        place = lax.axis_index("wa")
        end = jnp.logical_or(place < 2, place >= 6)

        @pl.when(end)
        def _():
            hid_ref[:half, :] = out1_ref[...]
            hid_ref[half:, :] = out2_ref[...]

        @pl.when(jnp.logical_not(end))
        def _():
            hid_ref[:half, :] = own_ref[...]
            hid_ref[half:, :] = mid_ref[...]

    total = jnp.dot(hid_ref[...], w_ref[...], preferred_element_type=F32)
    if not first:
        total = total + acc_ref[...]
    if not last:
        refs[0][...] = total
        return
    keep_ref, send_ref, total_ref = refs[:3]
    total_ref[...] = total
    rows = half // 2
    here = xor(lax.axis_index("ha"), base_block())
    for flip, ref, at in ((0, keep_ref, 0), (2, keep_ref, 1), (1, send_ref, 0), (3, send_ref, 1)):
        part = total_ref[rows_at(swap_bits(xor(here, flip)), rows), :]
        ref[at * rows:(at + 1) * rows, :] = part.astype(ref.dtype)


def send_y_kernel(keep_ref, core_ref, o_ref):
    o_ref[...] = (keep_ref[...] + core_ref[...].astype(F32)).astype(BF16)


def final_kernel(keep_ref, core_ref, y_ref, o_ref):
    o_ref[...] = (keep_ref[...] + core_ref[...].astype(F32) + y_ref[...].astype(F32)).astype(BF16)


def chunk_units(units):
    shares = (5, 5, 5, 4, 4, 3)
    total, done, cuts = sum(shares), 0, [0]
    for s in shares:
        done += s
        cuts.append(units * done // total)
    return cuts


def planned(tokens, norm_gain, gate_weight, up_weight, down_weight):
    rows, width = tokens.shape
    hidden = gate_weight.shape[1]
    out_width = down_weight.shape[1]
    tile = 256
    cuts = [c * tile for c in chunk_units(hidden // tile)]
    n_chunks = len(cuts) - 1
    gain = norm_gain[None, :]
    chain = Chain()
    swap = lambda a, axis, pairs: lax.ppermute(a, axis, pairs)

    (sq,) = chain.call(squares_kernel, [tokens], [shape((rows, 128), F32)], name="squares")
    t2 = swap(tokens, "ha", Y_SWAP)
    t1 = swap(tokens, "ha", CORE_SWAP)
    t3 = swap(t2, "ha", CORE_SWAP)
    for pairs in (X_SWAP, Z_SWAP):
        (sq,) = chain.call(add_kernel, [sq, swap(sq, "wa", pairs)], [shape((rows, 128), F32)], name="squares_add")
    sq_cross = swap(sq, "wa", Z_CROSS)
    (lhs_raw,) = chain.call(arrange_kernel, [tokens, t2, t1, t3, gain], [shape((4 * rows, width), BF16)], name="arrange")

    def project(k, lhs):
        n = cuts[k + 1] - cuts[k]
        first = cuts[k] // tile
        return chain.call(
            project_kernel,
            [lhs, gate_weight, up_weight],
            [shape((2, 2 * rows, n), F32), shape((2, 2 * rows, n), BF16)],
            grid=(n // tile,),
            in_specs=[
                pl.BlockSpec((4 * rows, width), lambda i: (0, 0)),
                pl.BlockSpec((width, tile), lambda i: (0, first + i)),
                pl.BlockSpec((width, tile), lambda i: (0, first + i)),
            ],
            out_specs=[pl.BlockSpec((2, 2 * rows, tile), lambda i: (0, 0, i))] * 2,
            name="project",
        )

    state = [dict() for _ in range(n_chunks)]
    env = {"acc": None, "lhs": None, "r": None, "sq": sq, "sq_cross": sq_cross}

    def stage_q(k):
        (s0,) = chain.call(add_kernel, [env["sq"], env["sq_cross"]], [shape((rows, 128), F32)], name="squares_add")
        s2 = swap(s0, "ha", Y_SWAP)
        s1 = swap(s0, "ha", CORE_SWAP)
        s3 = swap(s2, "ha", CORE_SWAP)
        env["s"] = (s0, s2, s1, s3)

    def stage_n(k):
        env["lhs"], env["r"] = chain.call(
            functools.partial(norm_kernel, width * lax.axis_size("wa")),
            [tokens, t2, t1, t3, *env["s"], gain],
            [shape((4 * rows, width), BF16), shape((4 * rows, 128), F32)],
            name="norm",
        )

    def stage_m(k):
        s = state[k]
        s["scaled"] = env["lhs"] is None
        s["keep"], send = project(k, lhs_raw if s["scaled"] else env["lhs"])
        s["x"] = swap(send, "wa", X_SWAP)

    def part(n, at):
        return pl.BlockSpec((2, rows, n), lambda i: (0, at, 0))

    def width_of(k):
        return cuts[k + 1] - cuts[k]

    def stage_i(k):
        s = state[k]
        n = width_of(k)
        (send,) = chain.call(inward_kernel, [s["keep"], s["x"]], [shape((2, 2 * rows, n), BF16)], name="inward")
        s["in"] = swap(send, "wa", Z_IN)

    def stage_j(k):
        s = state[k]
        n = width_of(k)
        (send,) = chain.call(
            middle_kernel, [s["keep"], s["x"], s["in"]], [shape((2, rows, n), BF16)],
            grid=(1,), in_specs=[part(n, 1)] * 3, out_specs=[part(n, 0)], name="middle",
        )
        s["mid"] = swap(send, "wa", Z_MID)

    def stage_h(k):
        s = state[k]
        n = width_of(k)
        r = env["r"]
        (s["h"],) = chain.call(
            functools.partial(activate_kernel, s["scaled"]),
            [s["keep"], s["x"], s["in"], s["mid"], r],
            [shape((rows, n), BF16)],
            grid=(1,),
            in_specs=[part(n, 0)] * 4 + [pl.BlockSpec((rows, 128), lambda i: (0, 0))],
            out_specs=[pl.BlockSpec((rows, n), lambda i: (0, 0))],
            name="activate",
        )
        s["hx"] = swap(s["h"], "wa", X_MID)

    def stage_g(k):
        s = state[k]
        n = width_of(k)
        (s["own"],) = chain.call(join_kernel, [s["h"], s["hx"]], [shape((2 * rows, n), BF16)], name="join")
        s["hm"] = swap(s["own"], "wa", Z_MID)
        s["o1"] = swap(s["own"], "wa", Z_OUT)

    def stage_r(k):
        s = state[k]
        n = width_of(k)
        (s["hm"],) = chain.call(
            pass_kernel, [s["hm"]], [shape((2 * rows, n), BF16)],
            in_specs=[any_spec()], out_specs=[any_spec()], aliases={0: 0}, name="pass",
        )
        s["o2"] = swap(s["hm"], "wa", Z_OUT)

    def stage_w(k):
        s = state[k]
        n = width_of(k)
        first, last = k == 0, k == n_chunks - 1
        cols = 512
        whole = pl.BlockSpec((2 * rows, n), lambda i: (0, 0))
        args = [s["own"], s["hm"], s["o1"], s["o2"], lax.slice(down_weight, (cuts[k], 0), (cuts[k + 1], out_width))]
        args[4] = down_weight
        at = cuts[k]
        in_specs = [whole] * 4 + [pl.BlockSpec((pl.Element(n), pl.Element(cols)), lambda i: (at, i * cols))]
        if not first:
            args.append(env["acc"])
            in_specs.append(pl.BlockSpec((4 * rows, cols), lambda i: (0, i)))
        if last:
            out_shape = [shape((2 * rows, out_width), F32), shape((2 * rows, out_width), BF16)]
            out_specs = [pl.BlockSpec((2 * rows, cols), lambda i: (0, i))] * 2
            scratch = [pltpu.VMEM((4 * rows, cols), F32), pltpu.VMEM((4 * rows, n), BF16)]
        else:
            out_shape = [shape((4 * rows, out_width), F32)]
            out_specs = [pl.BlockSpec((4 * rows, cols), lambda i: (0, i))]
            scratch = [pltpu.VMEM((4 * rows, n), BF16)]
        outs = chain.call(
            functools.partial(down_kernel, first, last), args, out_shape,
            grid=(out_width // cols,), in_specs=in_specs, out_specs=out_specs, scratch=scratch, name="down",
        )
        env["acc"] = outs[0]
        env["last"] = outs

    stages = dict(m=stage_m, i=stage_i, j=stage_j, h=stage_h, g=stage_g, r=stage_r, w=stage_w, q=stage_q, n=stage_n)
    for step in ORDER:
        stages[step[0]](int(step[1:] or 0))

    keep, send = env["last"]
    core = swap(send, "ha", CORE_SWAP)
    block = lambda at: pl.BlockSpec((rows, out_width), lambda i: (at, 0))
    (send_y,) = chain.call(
        send_y_kernel, [keep, core], [shape((rows, out_width), BF16)],
        grid=(1,), in_specs=[block(1), block(1)], out_specs=[block(0)], name="send_y",
    )
    y = swap(send_y, "ha", Y_SWAP)
    (out,) = chain.call(
        final_kernel, [keep, core, y], [shape((rows, out_width), BF16)],
        grid=(1,), in_specs=[block(0)] * 3, out_specs=[block(0)], name="final",
    )
    return out


ORDER = (
    "m0", "q", "m1", "n", "i0", "m2", "j0", "i1", "h0", "m3", "g0", "j1",
    "i2", "r0", "h1", "m4", "g1", "j2", "w0", "i3", "r1", "h2", "m5", "g2",
    "j3", "w1", "i4", "r2", "h3", "g3", "j4", "w2", "i5", "r3", "h4", "g4",
    "j5", "w3", "r4", "h5", "g5", "w4", "r5", "w5",
)


def general(tokens, norm_gain, gate_weight, up_weight, down_weight):
    gathered = lax.all_gather(tokens, "ha", axis=0, tiled=True).astype(F32)
    squares = lax.psum(jnp.sum(gathered * gathered, axis=1), "wa")
    mean_square = squares[:, None] / (gathered.shape[1] * lax.axis_size("wa"))
    normed = (gathered * lax.rsqrt(mean_square + EPS) * norm_gain[None, :]).astype(BF16)
    hidden = gate_weight.shape[1]
    gate = jnp.dot(normed, gate_weight, preferred_element_type=F32)
    up = jnp.dot(normed, up_weight, preferred_element_type=F32)
    summed = lax.psum_scatter(jnp.concatenate([gate, up], axis=1), "wa", scatter_dimension=0, tiled=True)
    mixed = (jax.nn.silu(summed[:, :hidden]) * summed[:, hidden:]).astype(BF16)
    out = jnp.dot(lax.all_gather(mixed, "wa", axis=0, tiled=True), down_weight, preferred_element_type=F32)
    return lax.psum_scatter(out, "ha", scatter_dimension=0, tiled=True).astype(BF16)


def solution(mesh):
    body = planned if (mesh.shape["wa"], mesh.shape["ha"]) == (8, 4) else general
    placed = (P("ha", "wa"), P("wa"), P("wa", "ha"), P("wa", "ha"), P("ha", "wa"))
    return jax.shard_map(body, mesh=mesh, in_specs=placed, out_specs=P("ha", "wa"), check_vma=False)
```

time: 419 us -> 238 us (0.57)
  waiting for transfers between devices: 333 us -> 83.2 us
  starting transfers between devices: 0.13 us -> 82.7 us
  Pallas kernels: 0 us -> 66.8 us
  matrix products: 40 us -> 0 us
  blocking collectives: 21.4 us -> 0 us
  between operations: 13.2 us -> 0.83 us
  other arithmetic: 11 us -> 0 us
    reduce_scatter x2 -> x0, waiting for transfers between devices: 248 us -> none  [the longest x1 218 us: body(): lax.psum_scatter(jnp.concatenate([gate_part, up_part], axis=1), 'wa', sca...]
    all_gather x2 -> x0, waiting for transfers between devices: 83.8 us -> none  [the longest x1 62.8 us: body(): lax.all_gather(hidden, 'wa', axis=0, tiled=True)]
    ppermute x0 -> x53, waiting for transfers between devices: none -> 83.2 us  [planned(): swap = lambda a, axis, pairs: lax.ppermute(a, axis, pairs)]
    ppermute x0 -> x53, starting transfers between devices: none -> 82.7 us  [planned(): swap = lambda a, axis, pairs: lax.ppermute(a, axis, pairs)]
    pallas_call x0 -> x50, Pallas kernels: none -> 66.8 us  [call(): pl.pallas_call(run, out_shape=tuple(out_shape), grid=grid, in_specs=in_sp...]
    dot_general x3 -> x0, matrix products: 40 us -> none  [the longest x1 14.4 us: body(): jnp.dot(lax.all_gather(hidden, 'wa', axis=0, tiled=True), down_weight, pr...]
    psum x1 -> x0, blocking collectives: 21.4 us -> none  [body(): squares = lax.psum(jnp.sum(own_values * own_values, axis=1), 'wa')]
    concatenate x1 -> x0, other arithmetic: 5.25 us -> none  [body(): jnp.concatenate([gate_part, up_part], axis=1)]
  transfers between devices with their start and end apart: 4 -> 53, of which waited for: 4 -> 25; matrix products, arithmetic and copies ran while one was open for 0% -> 0% of each run, Pallas kernels for 0% -> 23%
where the time goes in v1:
time: 238 us; the launch traced here: 236 us
  waiting for transfers between devices  83.2 us (35%)
  starting transfers between devices  82.7 us (35%)
  Pallas kernels  66.8 us (28%)
  local copies, waits for them, and re-layouts  2.6 us (1%)
    ppermute x53, waiting for transfers between devices, planned(): swap = lambda a, axis, pairs: lax.ppermute(a, axis, pairs)  83.2 us
    ppermute x53, starting transfers between devices, planned(): swap = lambda a, axis, pairs: lax.ppermute(a, axis, pairs)  82.7 us
    pallas_call x50, Pallas kernels, call(): pl.pallas_call(run, out_shape=tuple(out_shape), grid=grid, in_specs=in_sp...  66.8 us
  transfers between devices with their start and end apart: 53, of which 25 were waited for; matrix products, arithmetic and copies ran while one was open for 0% of the time, Pallas kernels for 23%

profile of v1, /device:TPU:0, one launch (start us, length us, event | category | flops | bytes accessed | tf_op | source)
XLA Modules:
  0.0 236.2 jit_solution(5345247176456099322)
XLA Ops:
  0.0 3.0 %collective-permute-start = (bf16[64,2048]{1,0:T(8,128)(2,1)}, bf16[64,2048]{1,0:T(8,128)(2,1)S(1)}, u32[]{:S(2)}, u32[]{:S(2)}) collective-permute-start(bf16[64,2048]{1,0:T(8,128)(2,1)} %refs_0_.5), channel_id=1, source_target_pairs={{0,2},{1,3},{2,0},{3,1},{4,6},{5,7},{6,4},{7,5},{8,10},{9,11},{10,... | collective-permute-start | bytes 786440 | tf_op jit(solution)/shard_map/ppermute | solution.py:212
  3.0 6.5 %collective-permute-done.refs_1_ = bf16[64,2048]{1,0:T(8,128)(2,1)S(1)} collective-permute-done((bf16[64,2048]{1,0:T(8,128)(2,1)}, bf16[64,2048]{1,0:T(8,128)(2,1)S(1)}, u32[]{:S(2)}, u32[]{:S(2)}) %collective-permute-start) | collective-permute-done | bytes 262176 | tf_op jit(solution)/shard_map/ppermute | solution.py:212
  10.6 1.7 collective-permute-start.3
  12.3 2.2 collective-permute-done.3.refs_1_
  14.5 1.8 collective-permute-start.4
  16.3 2.1 collective-permute-done.4.refs_1_
  20.4 6.9 %project.6 = (f32[2,128,1280]{2,1,0:T(8,128)S(1)}, bf16[2,128,1280]{2,1,0:T(8,128)(2,1)S(1)}) custom-call(bf16[256,2048]{1,0:T(8,128)(2,1)S(1)} %arrange.1.refs_0_.refs_3_, bf16[2048,6656]{1,0:T(8,128)(2,1)} %refs_1_.11, bf16[2048,6656]{1,0:T(8,128)(2,1)} %refs_2_.11, bf16[256,2048]{1,0:T(8,128)(2,1)S(1)} %arrange.1.refs_0_.refs_3_), custom_call_target="tpu_custom_call" | custom-call | flops 1 | bytes 1024 | tf_op jit(solution)/shard_map/project/pallas_call | solution.py:49
  27.3 1.8 collective-permute-start.9
  29.1 3.6 %collective-permute-start.5 = (f32[64,128]{1,0:T(8,128)S(1)}, f32[64,128]{1,0:T(8,128)S(1)}, u32[]{:S(2)}, u32[]{:S(2)}) collective-permute-start(f32[64,128]{1,0:T(8,128)S(1)} %squares_add.4.refs_5_.refs_0_), channel_id=1, source_target_pairs={{0,24},{4,28},{8,16},{12,20},{16,8},{20,12},{24,0},{28,4},{1,25},{... | collective-permute-start | bytes 98312 | tf_op jit(solution)/shard_map/ppermute | solution.py:212
  32.7 2.1 collective-permute-done.5.refs_1_
  34.8 1.6 collective-permute-start.6
  36.4 2.4 %collective-permute-done.6.refs_5_ = f32[64,128]{1,0:T(8,128)S(1)} collective-permute-done((f32[64,128]{1,0:T(8,128)S(1)}, f32[64,128]{1,0:T(8,128)S(1)}, u32[]{:S(2)}, u32[]{:S(2)}) %collective-permute-start.6) | collective-permute-done | bytes 32800 | tf_op jit(solution)/shard_map/ppermute | solution.py:212
  38.8 6.9 %project.7 = (f32[2,128,1280]{2,1,0:T(8,128)S(1)}, bf16[2,128,1280]{2,1,0:T(8,128)(2,1)S(1)}) custom-call(bf16[256,2048]{1,0:T(8,128)(2,1)S(1)} %arrange.1.refs_0_.refs_3_, bf16[2048,6656]{1,0:T(8,128)(2,1)} %refs_1_.11, bf16[2048,6656]{1,0:T(8,128)(2,1)} %refs_2_.11, f32[64,128]{1,0:T(8,128)S(1)} %squares_add.5.refs_3_.refs_4_), custom_call_target="tpu_custom_call" | custom-call | flops 1 | bytes 1024 | tf_op jit(solution)/shard_map/project/pallas_call | solution.py:49
  46.2 1.7 collective-permute-start.12
  48.5 6.9 %project.8 = (f32[2,128,1280]{2,1,0:T(8,128)S(1)}, bf16[2,128,1280]{2,1,0:T(8,128)(2,1)S(1)}) custom-call(bf16[256,2048]{1,0:T(8,128)(2,1)S(1)} %get-tuple-element.23.refs_2_.refs_0_, bf16[2048,6656]{1,0:T(8,128)(2,1)} %refs_1_.11, bf16[2048,6656]{1,0:T(8,128)(2,1)} %refs_2_.11, bf16[2,128,1280]{2,1,0:T(8,128)(2,1)S(1)} %inward.6.refs_3_), custom_call_target="tpu_custom_call" | custom-call | flops 1 | bytes 1024 | tf_op jit(solution)/shard_map/project/pallas_call | solution.py:49
  55.5 7.1 %collective-permute-done.12.refs_2_ = bf16[2,128,1280]{2,1,0:T(8,128)(2,1)S(1)} collective-permute-done((bf16[2,128,1280]{2,1,0:T(8,128)(2,1)S(1)}, bf16[2,128,1280]{2,1,0:T(8,128)(2,1)S(1)}, u32[]{:S(2)}, u32[]{:S(2)}) %collective-permute-start.12) | collective-permute-done | bytes 655392 | tf_op jit(solution)/shard_map/ppermute | solution.py:212
  62.6 2.2 collective-permute-done.11.refs_1_
  65.0 2.2 collective-permute-start.13
  69.5 5.5 %project.9 = (f32[2,128,1024]{2,1,0:T(8,128)S(1)}, bf16[2,128,1024]{2,1,0:T(8,128)(2,1)S(1)}) custom-call(bf16[256,2048]{1,0:T(8,128)(2,1)S(1)} %get-tuple-element.23.refs_2_.refs_0_, bf16[2048,6656]{1,0:T(8,128)(2,1)} %refs_1_.11, bf16[2048,6656]{1,0:T(8,128)(2,1)} %refs_2_.11, bf16[64,1280]{1,0:T(8,128)(2,1)S(1)} %activate.6.refs_3_.refs_0_), custom_call_target="tpu_custom_call" | custom-call | flops 1 | bytes 1024 | tf_op jit(solution)/shard_map/project/pallas_call | solution.py:49
  75.1 5.9 %collective-permute-done.13.refs_2_ = bf16[2,128,1280]{2,1,0:T(8,128)(2,1)S(1)} collective-permute-done((bf16[2,128,1280]{2,1,0:T(8,128)(2,1)S(1)}, bf16[2,128,1280]{2,1,0:T(8,128)(2,1)S(1)}, u32[]{:S(2)}, u32[]{:S(2)}) %collective-permute-start.13) | collective-permute-done | bytes 655392 | tf_op jit(solution)/shard_map/ppermute | solution.py:212
  81.1 2.2 collective-permute-done.10.refs_1_
  83.5 7.2 %collective-permute-start.16 = (bf16[2,128,1280]{2,1,0:T(8,128)(2,1)S(1)}, bf16[2,128,1280]{2,1,0:T(8,128)(2,1)S(1)}, u32[]{:S(2)}, u32[]{:S(2)}) collective-permute-start(bf16[2,128,1280]{2,1,0:T(8,128)(2,1)S(1)} %inward.8.refs_1_), channel_id=1, source_target_pairs={{0,8},{4,12},{24,16},{28,20},{1,9},{5,13},{25,17},{29,21},{2,10},{... | collective-permute-start | bytes 1966088 | tf_op jit(solution)/shard_map/ppermute | solution.py:212
  96.3 6.2 %project.10 = (f32[2,128,1024]{2,1,0:T(8,128)S(1)}, bf16[2,128,1024]{2,1,0:T(8,128)(2,1)}) custom-call(bf16[256,2048]{1,0:T(8,128)(2,1)S(1)} %get-tuple-element.23.refs_2_.refs_0_, bf16[2048,6656]{1,0:T(8,128)(2,1)} %refs_1_.11, bf16[2048,6656]{1,0:T(8,128)(2,1)} %refs_2_.11, bf16[64,1280]{1,0:T(8,128)(2,1)S(1)} %activate.7.refs_3_.refs_0_), custom_call_target="tpu_custom_call" | custom-call | flops 1 | bytes 1024 | tf_op jit(solution)/shard_map/project/pallas_call | solution.py:49
  104.4 2.0 collective-permute-done.23.refs_2_
  106.4 4.2 %collective-permute-done.24.refs_3_ = bf16[128,1280]{1,0:T(8,128)(2,1)S(1)} collective-permute-done((bf16[128,1280]{1,0:T(8,128)(2,1)S(1)}, bf16[128,1280]{1,0:T(8,128)(2,1)S(1)}, u32[]{:S(2)}, u32[]{:S(2)}) %collective-permute-start.24) | collective-permute-done | bytes 327712 | tf_op jit(solution)/shard_map/ppermute | solution.py:212
  110.6 4.4 %down.6.refs_2_.refs_5_ = f32[256,2048]{1,0:T(8,128)S(1)} custom-call(bf16[128,1280]{1,0:T(8,128)(2,1)S(1)} %join.6.refs_3_.refs_0_, bf16[128,1280]{1,0:T(8,128)(2,1)S(1)} %pass.6.refs_5_.refs_1_, bf16[128,1280]{1,0:T(8,128)(2,1)S(1)} %collective-permute-done.23.refs_2_, bf16[128,1280]{1,0:T(8,128)(2,1)S(1)} %collective-permute-done.24.refs_3_, ...), custom_call_target="tpu_custom_call" | custom-call | flops 1 | bytes 1024 | tf_op jit(solution)/shard_map/down/pallas_call | solution.py:49
  115.2 13.7 %collective-permute-start.31 = (bf16[2,128,1024]{2,1,0:T(8,128)(2,1)S(1)}, bf16[2,128,1024]{2,1,0:T(8,128)(2,1)S(1)}, u32[]{:S(2)}, u32[]{:S(2)}) collective-permute-start(bf16[2,128,1024]{2,1,0:T(8,128)(2,1)S(1)} %inward.9.refs_1_), channel_id=1, source_target_pairs={{0,8},{4,12},{24,16},{28,20},{1,9},{5,13},{25,17},{29,21},{2,10},{... | collective-permute-start | bytes 1572872 | tf_op jit(solution)/shard_map/ppermute | solution.py:212
  128.9 1.6 collective-permute-start.28
  134.0 4.7 %project.11 = (f32[2,128,768]{2,1,0:T(8,128)S(1)}, bf16[2,128,768]{2,1,0:T(8,128)(2,1)S(1)}) custom-call(bf16[256,2048]{1,0:T(8,128)(2,1)S(1)} %get-tuple-element.23.refs_2_.refs_0_, bf16[2048,6656]{1,0:T(8,128)(2,1)} %refs_1_.11, bf16[2048,6656]{1,0:T(8,128)(2,1)} %refs_2_.11, bf16[64,1280]{1,0:T(8,128)(2,1)S(1)} %activate.8.refs_3_.refs_0_), custom_call_target="tpu_custom_call" | custom-call | flops 1 | bytes 1024 | tf_op jit(solution)/shard_map/project/pallas_call | solution.py:49
  139.6 2.4 %collective-permute-done.29.refs_2_ = bf16[128,1280]{1,0:T(8,128)(2,1)S(1)} collective-permute-done((bf16[128,1280]{1,0:T(8,128)(2,1)S(1)}, bf16[128,1280]{1,0:T(8,128)(2,1)S(1)}, u32[]{:S(2)}, u32[]{:S(2)}) %collective-permute-start.29) | collective-permute-done | bytes 327712 | tf_op jit(solution)/shard_map/ppermute | solution.py:212
  141.9 3.5 %collective-permute-done.30.refs_3_ = bf16[128,1280]{1,0:T(8,128)(2,1)S(1)} collective-permute-done((bf16[128,1280]{1,0:T(8,128)(2,1)S(1)}, bf16[128,1280]{1,0:T(8,128)(2,1)S(1)}, u32[]{:S(2)}, u32[]{:S(2)}) %collective-permute-start.30) | collective-permute-done | bytes 327712 | tf_op jit(solution)/shard_map/ppermute | solution.py:212
  145.4 4.5 %down.7.refs_2_.refs_5_ = f32[256,2048]{1,0:T(8,128)S(1)} custom-call(bf16[128,1280]{1,0:T(8,128)(2,1)S(1)} %join.7.refs_3_.refs_0_, bf16[128,1280]{1,0:T(8,128)(2,1)S(1)} %pass.7.refs_5_.refs_1_, bf16[128,1280]{1,0:T(8,128)(2,1)S(1)} %collective-permute-done.29.refs_2_, bf16[128,1280]{1,0:T(8,128)(2,1)S(1)} %collective-permute-done.30.refs_3_, ...), custom_call_target="tpu_custom_call" | custom-call | flops 1 | bytes 1024 | tf_op jit(solution)/shard_map/down/pallas_call | solution.py:49
  150.1 3.2 %collective-permute-start.34 = (bf16[2,128,1024]{2,1,0:T(8,128)(2,1)S(1)}, bf16[2,128,1024]{2,1,0:T(8,128)(2,1)S(1)}, u32[]{:S(2)}, u32[]{:S(2)}) collective-permute-start(bf16[2,128,1024]{2,1,0:T(8,128)(2,1)S(1)} %inward.10.refs_1_), channel_id=1, source_target_pairs={{0,8},{4,12},{24,16},{28,20},{1,9},{5,13},{25,17},{29,21},{2,10},{... | collective-permute-start | bytes 1572872 | tf_op jit(solution)/shard_map/ppermute | solution.py:212
  161.9 3.7 %collective-permute-done.32.refs_2_ = bf16[128,1280]{1,0:T(8,128)(2,1)S(1)} collective-permute-done((bf16[128,1280]{1,0:T(8,128)(2,1)S(1)}, bf16[128,1280]{1,0:T(8,128)(2,1)S(1)}, u32[]{:S(2)}, u32[]{:S(2)}) %collective-permute-start.32) | collective-permute-done | bytes 327712 | tf_op jit(solution)/shard_map/ppermute | solution.py:212
  165.5 3.5 %collective-permute-done.33.refs_3_ = bf16[128,1280]{1,0:T(8,128)(2,1)S(1)} collective-permute-done((bf16[128,1280]{1,0:T(8,128)(2,1)S(1)}, bf16[128,1280]{1,0:T(8,128)(2,1)S(1)}, u32[]{:S(2)}, u32[]{:S(2)}) %collective-permute-start.33) | collective-permute-done | bytes 327712 | tf_op jit(solution)/shard_map/ppermute | solution.py:212
  169.0 4.5 %down.8.refs_2_.refs_5_ = f32[256,2048]{1,0:T(8,128)S(1)} custom-call(bf16[128,1280]{1,0:T(8,128)(2,1)S(1)} %join.8.refs_3_.refs_0_, bf16[128,1280]{1,0:T(8,128)(2,1)S(1)} %pass.8.refs_5_.refs_1_, bf16[128,1280]{1,0:T(8,128)(2,1)S(1)} %collective-permute-done.32.refs_2_, bf16[128,1280]{1,0:T(8,128)(2,1)S(1)} %collective-permute-done.33.refs_3_, ...), custom_call_target="tpu_custom_call" | custom-call | flops 1 | bytes 1024 | tf_op jit(solution)/shard_map/down/pallas_call | solution.py:49
  173.6 6.8 %collective-permute-start.37 = (bf16[2,128,768]{2,1,0:T(8,128)(2,1)S(1)}, bf16[2,128,768]{2,1,0:T(8,128)(2,1)S(1)}, u32[]{:S(2)}, u32[]{:S(2)}) collective-permute-start(bf16[2,128,768]{2,1,0:T(8,128)(2,1)S(1)} %inward.11.refs_1_), channel_id=1, source_target_pairs={{0,8},{4,12},{24,16},{28,20},{1,9},{5,13},{25,17},{29,21},{2,10},{... | collective-permute-start | bytes 1179656 | tf_op jit(solution)/shard_map/ppermute | solution.py:212
  186.5 3.2 %collective-permute-done.43.refs_2_ = bf16[128,1024]{1,0:T(8,128)(2,1)S(1)} collective-permute-done((bf16[128,1024]{1,0:T(8,128)(2,1)S(1)}, bf16[128,1024]{1,0:T(8,128)(2,1)S(1)}, u32[]{:S(2)}, u32[]{:S(2)}) %collective-permute-start.43) | collective-permute-done | bytes 262176 | tf_op jit(solution)/shard_map/ppermute | solution.py:212
  189.6 2.8 %collective-permute-done.44.refs_3_ = bf16[128,1024]{1,0:T(8,128)(2,1)S(1)} collective-permute-done((bf16[128,1024]{1,0:T(8,128)(2,1)S(1)}, bf16[128,1024]{1,0:T(8,128)(2,1)S(1)}, u32[]{:S(2)}, u32[]{:S(2)}) %collective-permute-start.44) | collective-permute-done | bytes 262176 | tf_op jit(solution)/shard_map/ppermute | solution.py:212
  192.4 4.1 %down.9.refs_1_.refs_5_ = f32[256,2048]{1,0:T(8,128)S(1)} custom-call(bf16[128,1024]{1,0:T(8,128)(2,1)S(1)} %join.9.refs_3_.refs_0_, bf16[128,1024]{1,0:T(8,128)(2,1)S(1)} %pass.9.refs_5_.refs_1_, bf16[128,1024]{1,0:T(8,128)(2,1)S(1)} %collective-permute-done.43.refs_2_, bf16[128,1024]{1,0:T(8,128)(2,1)S(1)} %collective-permute-done.44.refs_3_, ...), custom_call_target="tpu_custom_call" | custom-call | flops 1 | bytes 1024 | tf_op jit(solution)/shard_map/down/pallas_call | solution.py:49
  202.0 4.7 %collective-permute-done.47.refs_2_ = bf16[128,1024]{1,0:T(8,128)(2,1)S(1)} collective-permute-done((bf16[128,1024]{1,0:T(8,128)(2,1)S(1)}, bf16[128,1024]{1,0:T(8,128)(2,1)S(1)}, u32[]{:S(2)}, u32[]{:S(2)}) %collective-permute-start.47) | collective-permute-done | bytes 262176 | tf_op jit(solution)/shard_map/ppermute | solution.py:212
  206.7 2.8 %collective-permute-done.48.refs_3_ = bf16[128,1024]{1,0:T(8,128)(2,1)S(1)} collective-permute-done((bf16[128,1024]{1,0:T(8,128)(2,1)S(1)}, bf16[128,1024]{1,0:T(8,128)(2,1)S(1)}, u32[]{:S(2)}, u32[]{:S(2)}) %collective-permute-start.48) | collective-permute-done | bytes 262176 | tf_op jit(solution)/shard_map/ppermute | solution.py:212
  209.5 4.1 %down.10.refs_1_.refs_5_ = f32[256,2048]{1,0:T(8,128)S(1)} custom-call(bf16[128,1024]{1,0:T(8,128)(2,1)S(1)} %join.10.refs_3_.refs_0_, bf16[128,1024]{1,0:T(8,128)(2,1)S(1)} %pass.10.refs_5_.refs_1_, bf16[128,1024]{1,0:T(8,128)(2,1)S(1)} %collective-permute-done.47.refs_2_, bf16[128,1024]{1,0:T(8,128)(2,1)S(1)} %collective-permute-done.48.refs_3_, ...), custom_call_target="tpu_custom_call" | custom-call | flops 1 | bytes 1024 | tf_op jit(solution)/shard_map/down/pallas_call | solution.py:49
  214.9 6.3 %collective-permute-done.50.refs_3_ = bf16[128,768]{1,0:T(8,128)(2,1)S(1)} collective-permute-done((bf16[128,768]{1,0:T(8,128)(2,1)S(1)}, bf16[128,768]{1,0:T(8,128)(2,1)S(1)}, u32[]{:S(2)}, u32[]{:S(2)}) %collective-permute-start.50) | collective-permute-done | bytes 196640 | tf_op jit(solution)/shard_map/ppermute | solution.py:212
  221.2 3.8 %down.11 = (f32[128,2048]{1,0:T(8,128)S(1)}, bf16[128,2048]{1,0:T(8,128)(2,1)S(1)}) custom-call(bf16[128,768]{1,0:T(8,128)(2,1)S(1)} %join.11.refs_6_.refs_0_, bf16[128,768]{1,0:T(8,128)(2,1)S(1)} %pass.11.refs_1_.refs_6_, bf16[128,768]{1,0:T(8,128)(2,1)S(1)} %collective-permute-done.49.refs_2_, bf16[128,768]{1,0:T(8,128)(2,1)S(1)} %collective-permute-done.50.refs_3_, ...), custom_call_target="tpu_custom_call" | custom-call | flops 1 | bytes 1024 | tf_op jit(solution)/shard_map/down/pallas_call | solution.py:49
  225.0 1.9 collective-permute-done.51.refs_1_
  227.0 1.6 collective-permute-start.52
  228.5 6.8 %collective-permute-done.52.refs_2_ = bf16[64,2048]{1,0:T(8,128)(2,1)S(1)} collective-permute-done((bf16[64,2048]{1,0:T(8,128)(2,1)S(1)}, bf16[64,2048]{1,0:T(8,128)(2,1)S(1)}, u32[]{:S(2)}, u32[]{:S(2)}) %collective-permute-start.52) | collective-permute-done | bytes 262176 | tf_op jit(solution)/shard_map/ppermute | solution.py:212
  (116 shorter events, 40.7 us)
Async XLA Ops:
  0.0 9.5 %collective-permute-start = (bf16[64,2048]{1,0:T(8,128)(2,1)}, bf16[64,2048]{1,0:T(8,128)(2,1)S(1)}, u32[]{:S(2)}, u32[]{:S(2)}) collective-permute-start(bf16[64,2048]{1,0:T(8,128)(2,1)} %refs_0_.5), channel_id=1, source_target_pairs={{0,2},{1,3},{2,0},{3,1},{4,6},{5,7},{6,4},{7,5},{8,10},{9,11},{10,... | collective-permute-start | bytes 786440 | tf_op jit(solution)/shard_map/ppermute | solution.py:212
  3.0 15.5 %collective-permute-start.1 = (bf16[64,2048]{1,0:T(8,128)(2,1)}, bf16[64,2048]{1,0:T(8,128)(2,1)S(1)}, u32[]{:S(2)}, u32[]{:S(2)}) collective-permute-start(bf16[64,2048]{1,0:T(8,128)(2,1)} %refs_0_.5), channel_id=1, source_target_pairs={{0,1},{1,0},{2,3},{3,2},{4,5},{5,4},{6,7},{7,6},{8,9},{9,8},{10,11... | collective-permute-start | bytes 786440 | tf_op jit(solution)/shard_map/ppermute | solution.py:212
  9.5 9.0 %collective-permute-start.2 = (bf16[64,2048]{1,0:T(8,128)(2,1)S(1)}, bf16[64,2048]{1,0:T(8,128)(2,1)S(1)}, u32[]{:S(2)}, u32[]{:S(2)}) collective-permute-start(bf16[64,2048]{1,0:T(8,128)(2,1)S(1)} %collective-permute-done.refs_1_), channel_id=1, source_target_pairs={{0,1},{1,0},{2,3},{3,2},{4,5},{5,4},{6,7},{7,6},{8,9},{9,8},{10,11... | collective-permute-start | bytes 786440 | tf_op jit(solution)/shard_map/ppermute | solution.py:212
  10.6 3.9 %collective-permute-start.3 = (f32[64,128]{1,0:T(8,128)S(1)}, f32[64,128]{1,0:T(8,128)S(1)}, u32[]{:S(2)}, u32[]{:S(2)}) collective-permute-start(f32[64,128]{1,0:T(8,128)S(1)} %squares.1.refs_0_.refs_2_), channel_id=1, source_target_pairs={{0,4},{4,0},{8,12},{12,8},{16,20},{20,16},{24,28},{28,24},{1,5},{5... | collective-permute-start | bytes 98312 | tf_op jit(solution)/shard_map/ppermute | solution.py:212
  14.5 3.9 %collective-permute-start.4 = (f32[64,128]{1,0:T(8,128)S(1)}, f32[64,128]{1,0:T(8,128)S(1)}, u32[]{:S(2)}, u32[]{:S(2)}) collective-permute-start(f32[64,128]{1,0:T(8,128)S(1)} %squares_add.3.refs_0_.refs_2_), channel_id=1, source_target_pairs={{0,8},{4,12},{8,0},{12,4},{16,24},{20,28},{24,16},{28,20},{1,9},{5... | collective-permute-start | bytes 98312 | tf_op jit(solution)/shard_map/ppermute | solution.py:212
  27.3 18.8 %collective-permute-start.9 = (bf16[2,128,1280]{2,1,0:T(8,128)(2,1)S(1)}, bf16[2,128,1280]{2,1,0:T(8,128)(2,1)S(1)}, u32[]{:S(2)}, u32[]{:S(2)}) collective-permute-start(bf16[2,128,1280]{2,1,0:T(8,128)(2,1)S(1)} %get-tuple-element.24), channel_id=1, source_target_pairs={{0,4},{4,0},{8,12},{12,8},{16,20},{20,16},{24,28},{28,24},{1,5},{5... | collective-permute-start | bytes 1966088 | tf_op jit(solution)/shard_map/ppermute | solution.py:212
  29.1 5.7 %collective-permute-start.5 = (f32[64,128]{1,0:T(8,128)S(1)}, f32[64,128]{1,0:T(8,128)S(1)}, u32[]{:S(2)}, u32[]{:S(2)}) collective-permute-start(f32[64,128]{1,0:T(8,128)S(1)} %squares_add.4.refs_5_.refs_0_), channel_id=1, source_target_pairs={{0,24},{4,28},{8,16},{12,20},{16,8},{20,12},{24,0},{28,4},{1,25},{... | collective-permute-start | bytes 98312 | tf_op jit(solution)/shard_map/ppermute | solution.py:212
  34.8 4.0 %collective-permute-start.6 = (f32[64,128]{1,0:T(8,128)S(1)}, f32[64,128]{1,0:T(8,128)S(1)}, u32[]{:S(2)}, u32[]{:S(2)}) collective-permute-start(f32[64,128]{1,0:T(8,128)S(1)} %squares_add.5.refs_3_.refs_4_), channel_id=1, source_target_pairs={{0,2},{1,3},{2,0},{3,1},{4,6},{5,7},{6,4},{7,5},{8,10},{9,11},{10,... | collective-permute-start | bytes 98312 | tf_op jit(solution)/shard_map/ppermute | solution.py:212
  36.4 9.3 %collective-permute-start.7 = (f32[64,128]{1,0:T(8,128)S(1)}, f32[64,128]{1,0:T(8,128)S(1)}, u32[]{:S(2)}, u32[]{:S(2)}) collective-permute-start(f32[64,128]{1,0:T(8,128)S(1)} %squares_add.5.refs_3_.refs_4_), channel_id=1, source_target_pairs={{0,1},{1,0},{2,3},{3,2},{4,5},{5,4},{6,7},{7,6},{8,9},{9,8},{10,11... | collective-permute-start | bytes 98312 | tf_op jit(solution)/shard_map/ppermute | solution.py:212
  38.8 6.9 %collective-permute-start.8 = (f32[64,128]{1,0:T(8,128)S(1)}, f32[64,128]{1,0:T(8,128)S(1)}, u32[]{:S(2)}, u32[]{:S(2)}) collective-permute-start(f32[64,128]{1,0:T(8,128)S(1)} %collective-permute-done.6.refs_5_), channel_id=1, source_target_pairs={{0,1},{1,0},{2,3},{3,2},{4,5},{5,4},{6,7},{7,6},{8,9},{9,8},{10,11... | collective-permute-start | bytes 98312 | tf_op jit(solution)/shard_map/ppermute | solution.py:212
  46.2 16.3 %collective-permute-start.12 = (bf16[2,128,1280]{2,1,0:T(8,128)(2,1)S(1)}, bf16[2,128,1280]{2,1,0:T(8,128)(2,1)S(1)}, u32[]{:S(2)}, u32[]{:S(2)}) collective-permute-start(bf16[2,128,1280]{2,1,0:T(8,128)(2,1)S(1)} %inward.6.refs_3_), channel_id=1, source_target_pairs={{0,8},{4,12},{24,16},{28,20},{1,9},{5,13},{25,17},{29,21},{2,10},{... | collective-permute-start | bytes 1966088 | tf_op jit(solution)/shard_map/ppermute | solution.py:212
  47.9 16.9 %collective-permute-start.11 = (bf16[2,128,1280]{2,1,0:T(8,128)(2,1)S(1)}, bf16[2,128,1280]{2,1,0:T(8,128)(2,1)S(1)}, u32[]{:S(2)}, u32[]{:S(2)}) collective-permute-start(bf16[2,128,1280]{2,1,0:T(8,128)(2,1)S(1)} %get-tuple-element.27), channel_id=1, source_target_pairs={{0,4},{4,0},{8,12},{12,8},{16,20},{20,16},{24,28},{28,24},{1,5},{5... | collective-permute-start | bytes 1966088 | tf_op jit(solution)/shard_map/ppermute | solution.py:212
  65.0 16.1 %collective-permute-start.13 = (bf16[2,128,1280]{2,1,0:T(8,128)(2,1)S(1)}, bf16[2,128,1280]{2,1,0:T(8,128)(2,1)S(1)}, u32[]{:S(2)}, u32[]{:S(2)}) collective-permute-start(bf16[2,128,1280]{2,1,0:T(8,128)(2,1)S(1)} %inward.7.refs_5_), channel_id=1, source_target_pairs={{0,8},{4,12},{24,16},{28,20},{1,9},{5,13},{25,17},{29,21},{2,10},{... | collective-permute-start | bytes 1966088 | tf_op jit(solution)/shard_map/ppermute | solution.py:212
  67.2 16.1 %collective-permute-start.10 = (bf16[2,128,1280]{2,1,0:T(8,128)(2,1)S(1)}, bf16[2,128,1280]{2,1,0:T(8,128)(2,1)S(1)}, u32[]{:S(2)}, u32[]{:S(2)}) collective-permute-start(bf16[2,128,1280]{2,1,0:T(8,128)(2,1)S(1)} %get-tuple-element.26), channel_id=1, source_target_pairs={{0,4},{4,0},{8,12},{12,8},{16,20},{20,16},{24,28},{28,24},{1,5},{5... | collective-permute-start | bytes 1966088 | tf_op jit(solution)/shard_map/ppermute | solution.py:212
  68.8 6.2 %collective-permute-start.15 = (bf16[64,1280]{1,0:T(8,128)(2,1)S(1)}, bf16[64,1280]{1,0:T(8,128)(2,1)S(1)}, u32[]{:S(2)}, u32[]{:S(2)}) collective-permute-start(bf16[64,1280]{1,0:T(8,128)(2,1)S(1)} %activate.6.refs_3_.refs_0_), channel_id=1, source_target_pairs={{8,12},{12,8},{16,20},{20,16},{9,13},{13,9},{17,21},{21,17},{10,14... | collective-permute-start | bytes 491528 | tf_op jit(solution)/shard_map/ppermute | solution.py:212
  83.5 20.1 %collective-permute-start.16 = (bf16[2,128,1280]{2,1,0:T(8,128)(2,1)S(1)}, bf16[2,128,1280]{2,1,0:T(8,128)(2,1)S(1)}, u32[]{:S(2)}, u32[]{:S(2)}) collective-permute-start(bf16[2,128,1280]{2,1,0:T(8,128)(2,1)S(1)} %inward.8.refs_1_), channel_id=1, source_target_pairs={{0,8},{4,12},{24,16},{28,20},{1,9},{5,13},{25,17},{29,21},{2,10},{... | collective-permute-start | bytes 1966088 | tf_op jit(solution)/shard_map/ppermute | solution.py:212
  91.4 3.9 %collective-permute-start.17 = (bf16[2,64,1280]{2,1,0:T(8,128)(2,1)S(1)}, bf16[2,64,1280]{2,1,0:T(8,128)(2,1)S(1)}, u32[]{:S(2)}, u32[]{:S(2)}) collective-permute-start(bf16[2,64,1280]{2,1,0:T(8,128)(2,1)S(1)} %middle.7.refs_2_), channel_id=1, source_target_pairs={{8,16},{12,20},{16,8},{20,12},{9,17},{13,21},{17,9},{21,13},{10,18... | collective-permute-start | bytes 983048 | tf_op jit(solution)/shard_map/ppermute | solution.py:212
  92.1 23.0 %collective-permute-start.22 = (bf16[2,128,1024]{2,1,0:T(8,128)(2,1)S(1)}, bf16[2,128,1024]{2,1,0:T(8,128)(2,1)S(1)}, u32[]{:S(2)}, u32[]{:S(2)}) collective-permute-start(bf16[2,128,1024]{2,1,0:T(8,128)(2,1)S(1)} %get-tuple-element.31), channel_id=1, source_target_pairs={{0,4},{4,0},{8,12},{12,8},{16,20},{20,16},{24,28},{28,24},{1,5},{5... | collective-permute-start | bytes 1572872 | tf_op jit(solution)/shard_map/ppermute | solution.py:212
  92.7 13.7 %collective-permute-start.23 = (bf16[128,1280]{1,0:T(8,128)(2,1)S(1)}, bf16[128,1280]{1,0:T(8,128)(2,1)S(1)}, u32[]{:S(2)}, u32[]{:S(2)}) collective-permute-start(bf16[128,1280]{1,0:T(8,128)(2,1)S(1)} %join.6.refs_3_.refs_0_), channel_id=1, source_target_pairs={{8,0},{12,4},{16,24},{20,28},{9,1},{13,5},{17,25},{21,29},{10,2},{... | collective-permute-start | bytes 983048 | tf_op jit(solution)/shard_map/ppermute | solution.py:212
  94.0 16.6 %collective-permute-start.24 = (bf16[128,1280]{1,0:T(8,128)(2,1)S(1)}, bf16[128,1280]{1,0:T(8,128)(2,1)S(1)}, u32[]{:S(2)}, u32[]{:S(2)}) collective-permute-start(bf16[128,1280]{1,0:T(8,128)(2,1)S(1)} %pass.6.refs_5_.refs_1_), channel_id=1, source_target_pairs={{8,0},{12,4},{16,24},{20,28},{9,1},{13,5},{17,25},{21,29},{10,2},{... | collective-permute-start | bytes 983048 | tf_op jit(solution)/shard_map/ppermute | solution.py:212
  95.7 6.9 %collective-permute-start.19 = (bf16[64,1280]{1,0:T(8,128)(2,1)S(1)}, bf16[64,1280]{1,0:T(8,128)(2,1)S(1)}, u32[]{:S(2)}, u32[]{:S(2)}) collective-permute-start(bf16[64,1280]{1,0:T(8,128)(2,1)S(1)} %activate.7.refs_3_.refs_0_), channel_id=1, source_target_pairs={{8,12},{12,8},{16,20},{20,16},{9,13},{13,9},{17,21},{21,17},{10,14... | collective-permute-start | bytes 491528 | tf_op jit(solution)/shard_map/ppermute | solution.py:212
  102.5 29.2 %collective-permute-start.21 = (bf16[128,1280]{1,0:T(8,128)(2,1)S(1)}, bf16[128,1280]{1,0:T(8,128)(2,1)S(1)}, u32[]{:S(2)}, u32[]{:S(2)}) collective-permute-start(bf16[128,1280]{1,0:T(8,128)(2,1)S(1)} %join.7.refs_3_.refs_0_), channel_id=1, source_target_pairs={{8,16},{12,20},{16,8},{20,12},{9,17},{13,21},{17,9},{21,13},{10,18... | collective-permute-start | bytes 983048 | tf_op jit(solution)/shard_map/ppermute | solution.py:212
  103.7 29.4 %collective-permute-start.20 = (bf16[2,64,1280]{2,1,0:T(8,128)(2,1)S(1)}, bf16[2,64,1280]{2,1,0:T(8,128)(2,1)S(1)}, u32[]{:S(2)}, u32[]{:S(2)}) collective-permute-start(bf16[2,64,1280]{2,1,0:T(8,128)(2,1)S(1)} %middle.8.refs_5_), channel_id=1, source_target_pairs={{8,16},{12,20},{16,8},{20,12},{9,17},{13,21},{17,9},{21,13},{10,18... | collective-permute-start | bytes 983048 | tf_op jit(solution)/shard_map/ppermute | solution.py:212
  115.2 24.3 %collective-permute-start.31 = (bf16[2,128,1024]{2,1,0:T(8,128)(2,1)S(1)}, bf16[2,128,1024]{2,1,0:T(8,128)(2,1)S(1)}, u32[]{:S(2)}, u32[]{:S(2)}) collective-permute-start(bf16[2,128,1024]{2,1,0:T(8,128)(2,1)S(1)} %inward.9.refs_1_), channel_id=1, source_target_pairs={{0,8},{4,12},{24,16},{28,20},{1,9},{5,13},{25,17},{29,21},{2,10},{... | collective-permute-start | bytes 1572872 | tf_op jit(solution)/shard_map/ppermute | solution.py:212
  128.9 21.0 %collective-permute-start.28 = (bf16[2,128,1024]{2,1,0:T(8,128)(2,1)}, bf16[2,128,1024]{2,1,0:T(8,128)(2,1)S(1)}, u32[]{:S(2)}, u32[]{:S(2)}) collective-permute-start(bf16[2,128,1024]{2,1,0:T(8,128)(2,1)} %get-tuple-element.34), channel_id=1, source_target_pairs={{0,4},{4,0},{8,12},{12,8},{16,20},{20,16},{24,28},{28,24},{1,5},{5... | collective-permute-start | bytes 1572872 | tf_op jit(solution)/shard_map/ppermute | solution.py:212
  130.5 11.5 %collective-permute-start.29 = (bf16[128,1280]{1,0:T(8,128)(2,1)S(1)}, bf16[128,1280]{1,0:T(8,128)(2,1)S(1)}, u32[]{:S(2)}, u32[]{:S(2)}) collective-permute-start(bf16[128,1280]{1,0:T(8,128)(2,1)S(1)} %join.7.refs_3_.refs_0_), channel_id=1, source_target_pairs={{8,0},{12,4},{16,24},{20,28},{9,1},{13,5},{17,25},{21,29},{10,2},{... | collective-permute-start | bytes 983048 | tf_op jit(solution)/shard_map/ppermute | solution.py:212
  131.8 13.7 %collective-permute-start.30 = (bf16[128,1280]{1,0:T(8,128)(2,1)S(1)}, bf16[128,1280]{1,0:T(8,128)(2,1)S(1)}, u32[]{:S(2)}, u32[]{:S(2)}) collective-permute-start(bf16[128,1280]{1,0:T(8,128)(2,1)S(1)} %pass.7.refs_5_.refs_1_), channel_id=1, source_target_pairs={{8,0},{12,4},{16,24},{20,28},{9,1},{13,5},{17,25},{21,29},{10,2},{... | collective-permute-start | bytes 983048 | tf_op jit(solution)/shard_map/ppermute | solution.py:212
  133.3 5.4 %collective-permute-start.26 = (bf16[64,1280]{1,0:T(8,128)(2,1)S(1)}, bf16[64,1280]{1,0:T(8,128)(2,1)S(1)}, u32[]{:S(2)}, u32[]{:S(2)}) collective-permute-start(bf16[64,1280]{1,0:T(8,128)(2,1)S(1)} %activate.8.refs_3_.refs_0_), channel_id=1, source_target_pairs={{8,12},{12,8},{16,20},{20,16},{9,13},{13,9},{17,21},{21,17},{10,14... | collective-permute-start | bytes 491528 | tf_op jit(solution)/shard_map/ppermute | solution.py:212
  138.8 18.0 %collective-permute-start.27 = (bf16[128,1280]{1,0:T(8,128)(2,1)S(1)}, bf16[128,1280]{1,0:T(8,128)(2,1)S(1)}, u32[]{:S(2)}, u32[]{:S(2)}) collective-permute-start(bf16[128,1280]{1,0:T(8,128)(2,1)S(1)} %join.8.refs_3_.refs_0_), channel_id=1, source_target_pairs={{8,16},{12,20},{16,8},{20,12},{9,17},{13,21},{17,9},{21,13},{10,18... | collective-permute-start | bytes 983048 | tf_op jit(solution)/shard_map/ppermute | solution.py:212
  150.1 11.0 %collective-permute-start.34 = (bf16[2,128,1024]{2,1,0:T(8,128)(2,1)S(1)}, bf16[2,128,1024]{2,1,0:T(8,128)(2,1)S(1)}, u32[]{:S(2)}, u32[]{:S(2)}) collective-permute-start(bf16[2,128,1024]{2,1,0:T(8,128)(2,1)S(1)} %inward.10.refs_1_), channel_id=1, source_target_pairs={{0,8},{4,12},{24,16},{28,20},{1,9},{5,13},{25,17},{29,21},{2,10},{... | collective-permute-start | bytes 1572872 | tf_op jit(solution)/shard_map/ppermute | solution.py:212
  153.2 4.9 %collective-permute-start.35 = (bf16[2,64,1024]{2,1,0:T(8,128)(2,1)S(1)}, bf16[2,64,1024]{2,1,0:T(8,128)(2,1)S(1)}, u32[]{:S(2)}, u32[]{:S(2)}) collective-permute-start(bf16[2,64,1024]{2,1,0:T(8,128)(2,1)S(1)} %middle.9.refs_6_), channel_id=1, source_target_pairs={{8,16},{12,20},{16,8},{20,12},{9,17},{13,21},{17,9},{21,13},{10,18... | collective-permute-start | bytes 786440 | tf_op jit(solution)/shard_map/ppermute | solution.py:212
  153.9 19.6 %collective-permute-start.25 = (bf16[2,128,768]{2,1,0:T(8,128)(2,1)S(1)}, bf16[2,128,768]{2,1,0:T(8,128)(2,1)S(1)}, u32[]{:S(2)}, u32[]{:S(2)}) collective-permute-start(bf16[2,128,768]{2,1,0:T(8,128)(2,1)S(1)} %get-tuple-element.33), channel_id=1, source_target_pairs={{0,4},{4,0},{8,12},{12,8},{16,20},{20,16},{24,28},{28,24},{1,5},{5... | collective-permute-start | bytes 1179656 | tf_op jit(solution)/shard_map/ppermute | solution.py:212
  155.5 10.1 %collective-permute-start.32 = (bf16[128,1280]{1,0:T(8,128)(2,1)S(1)}, bf16[128,1280]{1,0:T(8,128)(2,1)S(1)}, u32[]{:S(2)}, u32[]{:S(2)}) collective-permute-start(bf16[128,1280]{1,0:T(8,128)(2,1)S(1)} %join.8.refs_3_.refs_0_), channel_id=1, source_target_pairs={{8,0},{12,4},{16,24},{20,28},{9,1},{13,5},{17,25},{21,29},{10,2},{... | collective-permute-start | bytes 983048 | tf_op jit(solution)/shard_map/ppermute | solution.py:212
  156.8 12.3 %collective-permute-start.33 = (bf16[128,1280]{1,0:T(8,128)(2,1)S(1)}, bf16[128,1280]{1,0:T(8,128)(2,1)S(1)}, u32[]{:S(2)}, u32[]{:S(2)}) collective-permute-start(bf16[128,1280]{1,0:T(8,128)(2,1)S(1)} %pass.8.refs_5_.refs_1_), channel_id=1, source_target_pairs={{8,0},{12,4},{16,24},{20,28},{9,1},{13,5},{17,25},{21,29},{10,2},{... | collective-permute-start | bytes 983048 | tf_op jit(solution)/shard_map/ppermute | solution.py:212
  159.0 21.5 %collective-permute-start.39 = (bf16[128,1024]{1,0:T(8,128)(2,1)S(1)}, bf16[128,1024]{1,0:T(8,128)(2,1)S(1)}, u32[]{:S(2)}, u32[]{:S(2)}) collective-permute-start(bf16[128,1024]{1,0:T(8,128)(2,1)S(1)} %join.9.refs_3_.refs_0_), channel_id=1, source_target_pairs={{8,16},{12,20},{16,8},{20,12},{9,17},{13,21},{17,9},{21,13},{10,18... | collective-permute-start | bytes 786440 | tf_op jit(solution)/shard_map/ppermute | solution.py:212
  161.2 19.3 %collective-permute-start.38 = (bf16[2,64,1024]{2,1,0:T(8,128)(2,1)S(1)}, bf16[2,64,1024]{2,1,0:T(8,128)(2,1)S(1)}, u32[]{:S(2)}, u32[]{:S(2)}) collective-permute-start(bf16[2,64,1024]{2,1,0:T(8,128)(2,1)S(1)} %middle.10.refs_6_), channel_id=1, source_target_pairs={{8,16},{12,20},{16,8},{20,12},{9,17},{13,21},{17,9},{21,13},{10,18... | collective-permute-start | bytes 786440 | tf_op jit(solution)/shard_map/ppermute | solution.py:212
  173.6 12.1 %collective-permute-start.37 = (bf16[2,128,768]{2,1,0:T(8,128)(2,1)S(1)}, bf16[2,128,768]{2,1,0:T(8,128)(2,1)S(1)}, u32[]{:S(2)}, u32[]{:S(2)}) collective-permute-start(bf16[2,128,768]{2,1,0:T(8,128)(2,1)S(1)} %inward.11.refs_1_), channel_id=1, source_target_pairs={{0,8},{4,12},{24,16},{28,20},{1,9},{5,13},{25,17},{29,21},{2,10},{... | collective-permute-start | bytes 1179656 | tf_op jit(solution)/shard_map/ppermute | solution.py:212
  180.7 3.3 %collective-permute-start.40 = (bf16[64,1024]{1,0:T(8,128)(2,1)S(1)}, bf16[64,1024]{1,0:T(8,128)(2,1)S(1)}, u32[]{:S(2)}, u32[]{:S(2)}) collective-permute-start(bf16[64,1024]{1,0:T(8,128)(2,1)S(1)} %activate.10.refs_0_.refs_2_), channel_id=1, source_target_pairs={{8,12},{12,8},{16,20},{20,16},{9,13},{13,9},{17,21},{21,17},{10,14... | collective-permute-start | bytes 393224 | tf_op jit(solution)/shard_map/ppermute | solution.py:212
  181.3 8.3 %collective-permute-start.43 = (bf16[128,1024]{1,0:T(8,128)(2,1)S(1)}, bf16[128,1024]{1,0:T(8,128)(2,1)S(1)}, u32[]{:S(2)}, u32[]{:S(2)}) collective-permute-start(bf16[128,1024]{1,0:T(8,128)(2,1)S(1)} %join.9.refs_3_.refs_0_), channel_id=1, source_target_pairs={{8,0},{12,4},{16,24},{20,28},{9,1},{13,5},{17,25},{21,29},{10,2},{... | collective-permute-start | bytes 786440 | tf_op jit(solution)/shard_map/ppermute | solution.py:212
  182.6 9.8 %collective-permute-start.44 = (bf16[128,1024]{1,0:T(8,128)(2,1)S(1)}, bf16[128,1024]{1,0:T(8,128)(2,1)S(1)}, u32[]{:S(2)}, u32[]{:S(2)}) collective-permute-start(bf16[128,1024]{1,0:T(8,128)(2,1)S(1)} %pass.9.refs_5_.refs_1_), channel_id=1, source_target_pairs={{8,0},{12,4},{16,24},{20,28},{9,1},{13,5},{17,25},{21,29},{10,2},{... | collective-permute-start | bytes 786440 | tf_op jit(solution)/shard_map/ppermute | solution.py:212
  184.0 12.5 %collective-permute-start.42 = (bf16[128,1024]{1,0:T(8,128)(2,1)S(1)}, bf16[128,1024]{1,0:T(8,128)(2,1)S(1)}, u32[]{:S(2)}, u32[]{:S(2)}) collective-permute-start(bf16[128,1024]{1,0:T(8,128)(2,1)S(1)} %join.10.refs_3_.refs_0_), channel_id=1, source_target_pairs={{8,16},{12,20},{16,8},{20,12},{9,17},{13,21},{17,9},{21,13},{10,18... | collective-permute-start | bytes 786440 | tf_op jit(solution)/shard_map/ppermute | solution.py:212
  185.8 10.8 %collective-permute-start.41 = (bf16[2,64,768]{2,1,0:T(8,128)(2,1)S(1)}, bf16[2,64,768]{2,1,0:T(8,128)(2,1)S(1)}, u32[]{:S(2)}, u32[]{:S(2)}) collective-permute-start(bf16[2,64,768]{2,1,0:T(8,128)(2,1)S(1)} %middle.11.refs_6_), channel_id=1, source_target_pairs={{8,16},{12,20},{16,8},{20,12},{9,17},{13,21},{17,9},{21,13},{10,18... | collective-permute-start | bytes 589832 | tf_op jit(solution)/shard_map/ppermute | solution.py:212
  197.4 9.3 %collective-permute-start.47 = (bf16[128,1024]{1,0:T(8,128)(2,1)S(1)}, bf16[128,1024]{1,0:T(8,128)(2,1)S(1)}, u32[]{:S(2)}, u32[]{:S(2)}) collective-permute-start(bf16[128,1024]{1,0:T(8,128)(2,1)S(1)} %join.10.refs_3_.refs_0_), channel_id=1, source_target_pairs={{8,0},{12,4},{16,24},{20,28},{9,1},{13,5},{17,25},{21,29},{10,2},{... | collective-permute-start | bytes 786440 | tf_op jit(solution)/shard_map/ppermute | solution.py:212
  198.7 10.8 %collective-permute-start.48 = (bf16[128,1024]{1,0:T(8,128)(2,1)S(1)}, bf16[128,1024]{1,0:T(8,128)(2,1)S(1)}, u32[]{:S(2)}, u32[]{:S(2)}) collective-permute-start(bf16[128,1024]{1,0:T(8,128)(2,1)S(1)} %pass.10.refs_5_.refs_1_), channel_id=1, source_target_pairs={{8,0},{12,4},{16,24},{20,28},{9,1},{13,5},{17,25},{21,29},{10,2},{... | collective-permute-start | bytes 786440 | tf_op jit(solution)/shard_map/ppermute | solution.py:212
  200.0 13.6 %collective-permute-start.46 = (bf16[128,768]{1,0:T(8,128)(2,1)S(1)}, bf16[128,768]{1,0:T(8,128)(2,1)S(1)}, u32[]{:S(2)}, u32[]{:S(2)}) collective-permute-start(bf16[128,768]{1,0:T(8,128)(2,1)S(1)} %join.11.refs_6_.refs_0_), channel_id=1, source_target_pairs={{8,16},{12,20},{16,8},{20,12},{9,17},{13,21},{17,9},{21,13},{10,18... | collective-permute-start | bytes 589832 | tf_op jit(solution)/shard_map/ppermute | solution.py:212
  200.7 14.2 %collective-permute-start.49 = (bf16[128,768]{1,0:T(8,128)(2,1)S(1)}, bf16[128,768]{1,0:T(8,128)(2,1)S(1)}, u32[]{:S(2)}, u32[]{:S(2)}) collective-permute-start(bf16[128,768]{1,0:T(8,128)(2,1)S(1)} %join.11.refs_6_.refs_0_), channel_id=1, source_target_pairs={{8,0},{12,4},{16,24},{20,28},{9,1},{13,5},{17,25},{21,29},{10,2},{... | collective-permute-start | bytes 589832 | tf_op jit(solution)/shard_map/ppermute | solution.py:212
  213.6 7.6 %collective-permute-start.50 = (bf16[128,768]{1,0:T(8,128)(2,1)S(1)}, bf16[128,768]{1,0:T(8,128)(2,1)S(1)}, u32[]{:S(2)}, u32[]{:S(2)}) collective-permute-start(bf16[128,768]{1,0:T(8,128)(2,1)S(1)} %pass.11.refs_1_.refs_6_), channel_id=1, source_target_pairs={{8,0},{12,4},{16,24},{20,28},{9,1},{13,5},{17,25},{21,29},{10,2},{... | collective-permute-start | bytes 589832 | tf_op jit(solution)/shard_map/ppermute | solution.py:212
  227.0 8.4 %collective-permute-start.52 = (bf16[64,2048]{1,0:T(8,128)(2,1)S(1)}, bf16[64,2048]{1,0:T(8,128)(2,1)S(1)}, u32[]{:S(2)}, u32[]{:S(2)}) collective-permute-start(bf16[64,2048]{1,0:T(8,128)(2,1)S(1)} %send_y.1.refs_3_), channel_id=1, source_target_pairs={{0,2},{1,3},{2,0},{3,1},{4,6},{5,7},{6,4},{7,5},{8,10},{9,11},{10,... | collective-permute-start | bytes 786440 | tf_op jit(solution)/shard_map/ppermute | solution.py:212
  (9 other events, 23.4 us)

commit v2 on v1

v2 whole, which is shorter than its diff:
```python
import functools

import jax
import jax.numpy as jnp
from jax import lax
from jax.experimental import pallas as pl
from jax.experimental.pallas import tpu as pltpu
from jax.sharding import PartitionSpec as P

F32, BF16 = jnp.float32, jnp.bfloat16
EPS = 1e-05
VMEM_LIMIT = 48 * 1024 * 1024

AXES = ("wa", "ha")
X, Z_LOW, Z_HIGH = 1, 2, 4


def swaps(wa_flips=(0, 0), ha_flip=0):
    return [(w * 4 + h, (w ^ wa_flips[h % 2]) * 4 + (h ^ ha_flip)) for w in range(8) for h in range(4)]


FIRST = swaps((X, Z_LOW))
SECOND = swaps((Z_LOW, X))
THIRD = swaps((Z_HIGH, Z_HIGH))
CORE_SWAP = swaps(ha_flip=1)
Y_SWAP = swaps(ha_flip=2)


def swap(a, pairs):
    return lax.ppermute(a, AXES, pairs)


def any_spec():
    return pl.BlockSpec(memory_space=pl.ANY)


class Chain:
    def __init__(self):
        self.token = None

    def call(self, kernel, args, out_shape, *, grid=(), in_specs=None, out_specs=None, scratch=(), aliases=None, flops=1, name=None):
        args = list(args)
        if in_specs is None:
            in_specs = [pl.BlockSpec(memory_space=pltpu.VMEM)] * len(args)
        if out_specs is None:
            out_specs = [pl.BlockSpec(memory_space=pltpu.VMEM)] * len(out_shape)
        n_in = len(args)
        extra = 0
        if self.token is not None:
            args.append(self.token)
            in_specs = list(in_specs) + [any_spec()]
            extra = 1

        def run(*refs):
            kernel(*refs[:n_in], *refs[n_in + extra:])

        outs = pl.pallas_call(
            run,
            out_shape=tuple(out_shape),
            grid=grid,
            in_specs=in_specs,
            out_specs=tuple(out_specs),
            scratch_shapes=scratch,
            input_output_aliases=aliases or {},
            compiler_params=pltpu.CompilerParams(vmem_limit_bytes=VMEM_LIMIT),
            cost_estimate=pl.CostEstimate(flops=flops, bytes_accessed=1024, transcendentals=0),
            name=name,
        )(*args)
        self.token = outs[0]
        return outs


def shape(dims, dtype):
    return jax.ShapeDtypeStruct(tuple(dims), dtype)


def own_block():
    place, core = lax.axis_index("wa"), lax.rem(lax.axis_index("ha"), 2)
    x, low, high = lax.rem(place, 2), lax.rem(place // 2, 2), place // 4
    return jnp.where(core == 0, 4 * x + 2 * low, 4 * low + 2 * x) + high


def token_rows(flip, part, rows):
    block = 2 * lax.bitwise_xor(lax.axis_index("ha"), flip) + part
    return pl.ds(pl.multiple_of(lax.bitwise_xor(block, own_block()) * rows, rows), rows)


def squares_kernel(t_ref, o_ref):
    v = t_ref[...].astype(F32)
    total = jnp.sum(v * v, axis=1, keepdims=True)
    o_ref[...] = jnp.broadcast_to(total, o_ref.shape)


def add_kernel(a_ref, b_ref, o_ref):
    o_ref[...] = a_ref[...] + b_ref[...]


def arrange_kernel(t0, t1, t2, t3, g_ref, o_ref):
    half = t0.shape[0] // 2
    for flip, t in enumerate((t0, t1, t2, t3)):
        v = (t[...].astype(F32) * g_ref[...]).astype(BF16)
        for part in range(2):
            o_ref[token_rows(flip, part, half), :] = v[part * half:(part + 1) * half]


def norm_kernel(width, t0, t1, t2, t3, s0, s1, s2, s3, g_ref, o_ref, r_ref):
    half = t0.shape[0] // 2
    for flip, (t, s) in enumerate(((t0, s0), (t1, s1), (t2, s2), (t3, s3))):
        factor = lax.rsqrt(s[...] / width + EPS)
        v = (t[...].astype(F32) * factor[:, :1] * g_ref[...]).astype(BF16)
        for part in range(2):
            at = token_rows(flip, part, half)
            o_ref[at, :] = v[part * half:(part + 1) * half]
            r_ref[at, :] = factor[part * half:(part + 1) * half]


def project_kernel(lhs_ref, g_ref, u_ref, keep_ref, send_ref):
    half = lhs_ref.shape[0] // 2
    for i, w in enumerate((g_ref, u_ref)):
        total = jnp.dot(lhs_ref[...], w[...], preferred_element_type=F32)
        keep_ref[i] = total[:half]
        send_ref[i] = total[half:].astype(BF16)


def sum_of(keep_ref, parts):
    total = keep_ref[...]
    for p in parts:
        total = total + p[...].astype(F32)
    return total


def add_up_kernel(keep_ref, *refs):
    refs[-1][...] = sum_of(keep_ref, refs[:-1]).astype(BF16)


def activate_kernel(scaled, keep_ref, p1_ref, p2_ref, p3_ref, r_ref, o_ref):
    total = sum_of(keep_ref, (p1_ref, p2_ref, p3_ref))
    if scaled:
        total = total * r_ref[...][None, :, :1]
    gate, up = total[0], total[1]
    o_ref[...] = (gate / (1.0 + jnp.exp(-gate)) * up).astype(BF16)


def join_kernel(a_ref, b_ref, o_ref):
    rows = a_ref.shape[0]
    o_ref[:rows, :] = a_ref[...]
    o_ref[rows:, :] = b_ref[...]


def pass_kernel(a_ref, o_ref):
    del a_ref, o_ref


def down_kernel(n_parts, first, last, *refs):
    refs = list(refs)
    parts, w_ref, refs = refs[:2 * n_parts], refs[2 * n_parts], refs[2 * n_parts + 1:]
    if not first:
        acc_ref = refs.pop(0)
    hid_ref = refs[-1]
    half = hid_ref.shape[0] // 2

    @pl.when(pl.program_id(0) == 0)
    def _():
        at = 0
        for i in range(n_parts):
            own, other = parts[2 * i:2 * i + 2]
            n = own.shape[1]
            hid_ref[:half, at:at + n] = own[...]
            hid_ref[half:, at:at + n] = other[...]
            at += n

    total = jnp.dot(hid_ref[...], w_ref[...], preferred_element_type=F32)
    if not first:
        total = total + acc_ref[...]
    if not last:
        refs[0][...] = total
        return
    keep_ref, send_ref, total_ref = refs[:3]
    total_ref[...] = total
    rows = half // 4
    for flip, ref, at in ((0, keep_ref, 0), (2, keep_ref, 2), (1, send_ref, 0), (3, send_ref, 2)):
        for part in range(2):
            v = total_ref[token_rows(flip, part, rows), :]
            ref[(at + part) * rows:(at + part + 1) * rows, :] = v.astype(ref.dtype)


def send_y_kernel(keep_ref, core_ref, o_ref):
    o_ref[...] = (keep_ref[...] + core_ref[...].astype(F32)).astype(BF16)


def final_kernel(keep_ref, core_ref, y_ref, o_ref):
    o_ref[...] = (keep_ref[...] + core_ref[...].astype(F32) + y_ref[...].astype(F32)).astype(BF16)


SHARES = (6, 4, 4, 6, 6)
GROUPS = ((0,), (1,), (2,), (3,), (4,),)
ORDER = (
    "q", "m0", "n", "m1", "a0", "m2", "a1", "m3", "b0", "a2", "b1", "m4",
    "a3", "c0", "b2", "c1", "a4", "b3", "d0", "c2", "d1", "b4", "c3", "e0",
    "d2", "e1", "c4", "d3", "e2", "w0", "d4", "e3", "w1", "e4", "w2", "w3",
    "w4",
)


def planned(tokens, norm_gain, gate_weight, up_weight, down_weight):
    rows, width = tokens.shape
    hidden = gate_weight.shape[1]
    out_width = down_weight.shape[1]
    unit = hidden // sum(SHARES)
    cuts = [unit * sum(SHARES[:k]) for k in range(len(SHARES) + 1)]
    gain = norm_gain[None, :]
    chain = Chain()

    t0 = tokens
    sq_shape = shape((rows, 128), F32)
    (sq,) = chain.call(squares_kernel, [t0], [sq_shape], name="squares")
    t2 = swap(t0, Y_SWAP)
    t1 = swap(t0, CORE_SWAP)
    (sq,) = chain.call(add_kernel, [sq, swap(sq, FIRST)], [sq_shape], name="squares_add")
    sq_second = swap(sq, SECOND)
    (t2,) = chain.call(
        pass_kernel, [t2], [shape(t2.shape, BF16)], in_specs=[any_spec()], out_specs=[any_spec()], aliases={0: 0}, name="pass",
    )
    t3 = swap(t2, CORE_SWAP)
    (sq,) = chain.call(add_kernel, [sq, sq_second], [sq_shape], name="squares_add")
    sq_third = swap(sq, THIRD)
    (raw,) = chain.call(arrange_kernel, [t0, t1, t2, t3, gain], [shape((4 * rows, width), BF16)], name="arrange")

    state = [dict() for _ in SHARES]
    env = {"lhs": raw, "acc": None}

    def stage_q(k):
        (s0,) = chain.call(add_kernel, [sq, sq_third], [sq_shape], name="squares_add")
        s2 = swap(s0, Y_SWAP)
        s1 = swap(s0, CORE_SWAP)
        env["s"] = (s0, s1, s2, swap(s2, CORE_SWAP))

    def stage_n(k):
        env["lhs"], env["r"] = chain.call(
            functools.partial(norm_kernel, width * lax.axis_size("wa")),
            [t0, t1, t2, t3, *env["s"], gain],
            [shape((4 * rows, width), BF16), shape((4 * rows, 128), F32)],
            name="norm",
        )

    def stage_m(k):
        s = state[k]
        n = s["n"] = cuts[k + 1] - cuts[k]
        s["scaled"] = "r" not in env
        tile = 512 if n % 512 == 0 and cuts[k] % 512 == 0 else 256
        first = cuts[k] // tile
        s["keep"], send = chain.call(
            project_kernel,
            [env["lhs"], gate_weight, up_weight],
            [shape((2, 2 * rows, n), F32), shape((2, 2 * rows, n), BF16)],
            grid=(n // tile,),
            in_specs=[
                pl.BlockSpec((4 * rows, width), lambda i: (0, 0)),
                pl.BlockSpec((width, tile), lambda i: (0, first + i)),
                pl.BlockSpec((width, tile), lambda i: (0, first + i)),
            ],
            out_specs=[pl.BlockSpec((2, 2 * rows, tile), lambda i: (0, 0, i))] * 2,
            name="project",
        )
        s["parts"] = [swap(send, FIRST)]

    def part(n, size, at):
        return pl.BlockSpec((2, size, n), lambda i: (0, at, 0))

    def add_up(k, size, pairs):
        s = state[k]
        n = s["n"]
        (send,) = chain.call(
            add_up_kernel, [s["keep"], *s["parts"]], [shape((2, size, n), BF16)],
            grid=(1,), in_specs=[part(n, size, 1)] * (1 + len(s["parts"])), out_specs=[part(n, size, 0)], name="add_up",
        )
        s["parts"].append(swap(send, pairs))

    def stage_a(k):
        add_up(k, rows, SECOND)

    def stage_b(k):
        add_up(k, rows // 2, THIRD)

    def stage_c(k):
        s = state[k]
        n, size = s["n"], rows // 2
        (s["h"],) = chain.call(
            functools.partial(activate_kernel, s["scaled"]),
            [s["keep"], *s["parts"], env["r"]],
            [shape((size, n), BF16)],
            grid=(1,),
            in_specs=[part(n, size, 0)] * 4 + [pl.BlockSpec((size, 128), lambda i: (0, 0))],
            out_specs=[pl.BlockSpec((size, n), lambda i: (0, 0))],
            name="activate",
        )
        s["got"] = swap(s["h"], THIRD)

    def join(k, pairs):
        s = state[k]
        (s["h"],) = chain.call(
            join_kernel, [s["h"], s["got"]], [shape((2 * s["h"].shape[0], s["n"]), BF16)], name="join"
        )
        s["got"] = swap(s["h"], pairs)

    def stage_d(k):
        join(k, SECOND)

    def stage_e(k):
        join(k, FIRST)

    def stage_w(k):
        group = GROUPS[k]
        first, last = k == 0, k == len(GROUPS) - 1
        at, n = cuts[group[0]], cuts[group[-1] + 1] - cuts[group[0]]
        cols = 512
        args, in_specs = [], []
        for j in group:
            args += [state[j]["h"], state[j]["got"]]
            in_specs += [pl.BlockSpec((2 * rows, state[j]["n"]), lambda i: (0, 0))] * 2
        args.append(down_weight)
        in_specs.append(pl.BlockSpec((pl.Element(n), pl.Element(cols)), lambda i: (at, i * cols)))
        if not first:
            args.append(env["acc"])
            in_specs.append(pl.BlockSpec((4 * rows, cols), lambda i: (0, i)))
        if last:
            out_shape = [shape((2 * rows, out_width), F32), shape((2 * rows, out_width), BF16)]
            out_specs = [pl.BlockSpec((2 * rows, cols), lambda i: (0, i))] * 2
            scratch = [pltpu.VMEM((4 * rows, cols), F32), pltpu.VMEM((4 * rows, n), BF16)]
        else:
            out_shape = [shape((4 * rows, out_width), F32)]
            out_specs = [pl.BlockSpec((4 * rows, cols), lambda i: (0, i))]
            scratch = [pltpu.VMEM((4 * rows, n), BF16)]
        env["last"] = chain.call(
            functools.partial(down_kernel, len(group), first, last), args, out_shape,
            grid=(out_width // cols,), in_specs=in_specs, out_specs=out_specs, scratch=scratch, name="down",
        )
        env["acc"] = env["last"][0]

    stages = dict(
        m=stage_m, a=stage_a, b=stage_b, c=stage_c, d=stage_d, e=stage_e, w=stage_w, q=stage_q, n=stage_n
    )
    for step in ORDER:
        stages[step[0]](int(step[1:] or 0))

    keep, send = env["last"]
    core = swap(send, CORE_SWAP)
    block = lambda at: pl.BlockSpec((rows, out_width), lambda i: (at, 0))
    (send_y,) = chain.call(
        send_y_kernel, [keep, core], [shape((rows, out_width), BF16)],
        grid=(1,), in_specs=[block(1), block(1)], out_specs=[block(0)], name="send_y",
    )
    y = swap(send_y, Y_SWAP)
    (out,) = chain.call(
        final_kernel, [keep, core, y], [shape((rows, out_width), BF16)],
        grid=(1,), in_specs=[block(0)] * 3, out_specs=[block(0)], name="final",
    )
    return out


def general(tokens, norm_gain, gate_weight, up_weight, down_weight):
    gathered = lax.all_gather(tokens, "ha", axis=0, tiled=True).astype(F32)
    squares = lax.psum(jnp.sum(gathered * gathered, axis=1), "wa")
    mean_square = squares[:, None] / (gathered.shape[1] * lax.axis_size("wa"))
    normed = (gathered * lax.rsqrt(mean_square + EPS) * norm_gain[None, :]).astype(BF16)
    hidden = gate_weight.shape[1]
    gate = jnp.dot(normed, gate_weight, preferred_element_type=F32)
    up = jnp.dot(normed, up_weight, preferred_element_type=F32)
    summed = lax.psum_scatter(jnp.concatenate([gate, up], axis=1), "wa", scatter_dimension=0, tiled=True)
    mixed = (jax.nn.silu(summed[:, :hidden]) * summed[:, hidden:]).astype(BF16)
    out = jnp.dot(lax.all_gather(mixed, "wa", axis=0, tiled=True), down_weight, preferred_element_type=F32)
    return lax.psum_scatter(out, "ha", scatter_dimension=0, tiled=True).astype(BF16)


def solution(mesh):
    body = planned if (mesh.shape["wa"], mesh.shape["ha"]) == (8, 4) else general
    placed = (P("ha", "wa"), P("wa"), P("wa", "ha"), P("wa", "ha"), P("ha", "wa"))
    return jax.shard_map(body, mesh=mesh, in_specs=placed, out_specs=P("ha", "wa"), check_vma=False)
```

time: 238 us -> 195 us (0.82)
  starting transfers between devices: 82.7 us -> 50.2 us
  Pallas kernels: 66.8 us -> 60 us
    ppermute x53 -> x41, starting transfers between devices: 82.7 us -> 50.2 us  [swap(): return lax.ppermute(a, AXES, pairs)]
    pallas_call x50 -> x44, Pallas kernels: 66.8 us -> 60 us  [call(): pl.pallas_call(run, out_shape=tuple(out_shape), grid=grid, in_specs=in_sp...]
    ppermute x53 -> x41, waiting for transfers between devices: 83.2 us -> 83.2 us  [swap(): return lax.ppermute(a, AXES, pairs)]
  transfers between devices with their start and end apart: 53 -> 41, of which waited for: 25 -> 22; matrix products, arithmetic and copies ran while one was open for 0% -> 0% of each run, Pallas kernels for 23% -> 24%
where the time goes in v2:
time: 195 us
  waiting for transfers between devices  83.2 us (43%)
  Pallas kernels  60 us (31%)
  starting transfers between devices  50.2 us (26%)
    ppermute x41, waiting for transfers between devices, swap(): return lax.ppermute(a, AXES, pairs)  83.2 us
    pallas_call x44, Pallas kernels, call(): pl.pallas_call(run, out_shape=tuple(out_shape), grid=grid, in_specs=in_sp...  60 us
    ppermute x41, starting transfers between devices, swap(): return lax.ppermute(a, AXES, pairs)  50.2 us
  transfers between devices with their start and end apart: 41, of which 22 were waited for; matrix products, arithmetic and copies ran while one was open for 0% of the time, Pallas kernels for 24%

profile of v2, /device:TPU:0, one launch (start us, length us, event | category | flops | bytes accessed | tf_op | source)
XLA Modules:
  0.0 194.5 jit_solution(16034726078452930604)
XLA Ops:
  0.0 3.0 %collective-permute-start.1 = (bf16[64,2048]{1,0:T(8,128)(2,1)}, bf16[64,2048]{1,0:T(8,128)(2,1)S(1)}, u32[]{:S(2)}, u32[]{:S(2)}) collective-permute-start(bf16[64,2048]{1,0:T(8,128)(2,1)} %refs_0_.5), channel_id=1, source_target_pairs={{0,2},{1,3},{2,0},{3,1},{4,6},{5,7},{6,4},{7,5},{8,10},{9,11},{10,... | collective-permute-start | bytes 786440 | tf_op jit(solution)/shard_map/ppermute | solution.py:30
  4.1 1.5 collective-permute-start.2
  5.6 2.4 %collective-permute-done.2.refs_1_ = f32[64,128]{1,0:T(8,128)S(1)} collective-permute-done((f32[64,128]{1,0:T(8,128)S(1)}, f32[64,128]{1,0:T(8,128)S(1)}, u32[]{:S(2)}, u32[]{:S(2)}) %collective-permute-start.2) | collective-permute-done | bytes 32800 | tf_op jit(solution)/shard_map/ppermute | solution.py:30
  8.0 1.5 collective-permute-done.1.refs_0_
  9.5 1.8 collective-permute-start.4
  11.3 2.1 %collective-permute-done.4.refs_1_ = f32[64,128]{1,0:T(8,128)S(1)} collective-permute-done((f32[64,128]{1,0:T(8,128)S(1)}, f32[64,128]{1,0:T(8,128)S(1)}, u32[]{:S(2)}, u32[]{:S(2)}) %collective-permute-start.4) | collective-permute-done | bytes 32800 | tf_op jit(solution)/shard_map/ppermute | solution.py:30
  13.4 2.8 %collective-permute-start.5 = (f32[64,128]{1,0:T(8,128)S(1)}, f32[64,128]{1,0:T(8,128)S(1)}, u32[]{:S(2)}, u32[]{:S(2)}) collective-permute-start(f32[64,128]{1,0:T(8,128)S(1)} %squares_add.4.refs_5_.refs_0_), channel_id=1, source_target_pairs={{0,16},{1,17},{2,18},{3,19},{4,20},{5,21},{6,22},{7,23},{8,24},{9,... | collective-permute-start | bytes 98312 | tf_op jit(solution)/shard_map/ppermute | solution.py:30
  18.2 7.3 %project.5 = (f32[2,128,1536]{2,1,0:T(8,128)S(1)}, bf16[2,128,1536]{2,1,0:T(8,128)(2,1)S(1)}) custom-call(bf16[256,2048]{1,0:T(8,128)(2,1)S(1)} %arrange.1.refs_2_.refs_0_, bf16[2048,6656]{1,0:T(8,128)(2,1)} %refs_1_.9, bf16[2048,6656]{1,0:T(8,128)(2,1)} %refs_2_.14, f32[64,128]{1,0:T(8,128)S(1)} %squares_add.5.refs_3_.refs_4_), custom_call_target="tpu_custom_call" | custom-call | flops 1 | bytes 1024 | tf_op jit(solution)/shard_map/project/pallas_call | solution.py:57
  25.5 1.8 collective-permute-start.10
  27.3 1.5 collective-permute-start.7
  28.8 2.4 %collective-permute-done.7.refs_6_ = f32[64,128]{1,0:T(8,128)S(1)} collective-permute-done((f32[64,128]{1,0:T(8,128)S(1)}, f32[64,128]{1,0:T(8,128)S(1)}, u32[]{:S(2)}, u32[]{:S(2)}) %collective-permute-start.7) | collective-permute-done | bytes 32800 | tf_op jit(solution)/shard_map/ppermute | solution.py:30
  33.7 4.9 %project.6 = (f32[2,128,1024]{2,1,0:T(8,128)S(1)}, bf16[2,128,1024]{2,1,0:T(8,128)(2,1)S(1)}) custom-call(bf16[256,2048]{1,0:T(8,128)(2,1)S(1)} %get-tuple-element.20.refs_0_.refs_3_, bf16[2048,6656]{1,0:T(8,128)(2,1)} %refs_1_.9, bf16[2048,6656]{1,0:T(8,128)(2,1)} %refs_2_.14, bf16[256,2048]{1,0:T(8,128)(2,1)S(1)} %get-tuple-element.20.refs_0_.refs_3_), custom_call_target="tpu_custom_call" | custom-call | flops 1 | bytes 1024 | tf_op jit(solution)/shard_map/project/pallas_call | solution.py:57
  39.0 4.9 %project.7 = (f32[2,128,1024]{2,1,0:T(8,128)S(1)}, bf16[2,128,1024]{2,1,0:T(8,128)(2,1)S(1)}) custom-call(bf16[256,2048]{1,0:T(8,128)(2,1)S(1)} %get-tuple-element.20.refs_0_.refs_3_, bf16[2048,6656]{1,0:T(8,128)(2,1)} %refs_1_.9, bf16[2048,6656]{1,0:T(8,128)(2,1)} %refs_2_.14, bf16[2,64,1536]{2,1,0:T(8,128)(2,1)S(1)} %add_up.10.refs_3_), custom_call_target="tpu_custom_call" | custom-call | flops 1 | bytes 1024 | tf_op jit(solution)/shard_map/project/pallas_call | solution.py:57
  43.9 1.8 collective-permute-start.12
  45.7 1.6 collective-permute-start.13
  47.8 1.6 collective-permute-start.11
  49.5 7.2 %project.8 = (f32[2,128,1536]{2,1,0:T(8,128)S(1)}, bf16[2,128,1536]{2,1,0:T(8,128)(2,1)S(1)}) custom-call(bf16[256,2048]{1,0:T(8,128)(2,1)S(1)} %get-tuple-element.20.refs_0_.refs_3_, bf16[2048,6656]{1,0:T(8,128)(2,1)} %refs_1_.9, bf16[2048,6656]{1,0:T(8,128)(2,1)} %refs_2_.14, bf16[2,64,1024]{2,1,0:T(8,128)(2,1)S(1)} %add_up.11.refs_3_), custom_call_target="tpu_custom_call" | custom-call | flops 1 | bytes 1024 | tf_op jit(solution)/shard_map/project/pallas_call | solution.py:57
  59.0 4.4 %collective-permute-done.11.refs_2_ = bf16[2,64,1024]{2,1,0:T(8,128)(2,1)S(1)} collective-permute-done((bf16[2,64,1024]{2,1,0:T(8,128)(2,1)S(1)}, bf16[2,64,1024]{2,1,0:T(8,128)(2,1)S(1)}, u32[]{:S(2)}, u32[]{:S(2)}) %collective-permute-start.11) | collective-permute-done | bytes 262176 | tf_op jit(solution)/shard_map/ppermute | solution.py:30
  63.4 7.1 %project.9 = (f32[2,128,1536]{2,1,0:T(8,128)S(1)}, bf16[2,128,1536]{2,1,0:T(8,128)(2,1)S(1)}) custom-call(bf16[256,2048]{1,0:T(8,128)(2,1)S(1)} %get-tuple-element.20.refs_0_.refs_3_, bf16[2048,6656]{1,0:T(8,128)(2,1)} %refs_1_.9, bf16[2048,6656]{1,0:T(8,128)(2,1)} %refs_2_.14, bf16[2,32,1024]{2,1,0:T(8,128)(2,1)S(1)} %add_up.14.refs_3_), custom_call_target="tpu_custom_call" | custom-call | flops 1 | bytes 1024 | tf_op jit(solution)/shard_map/project/pallas_call | solution.py:57
  70.8 2.8 %collective-permute-start.17 = (bf16[2,32,1536]{2,1,0:T(8,128)(2,1)S(1)}, bf16[2,32,1536]{2,1,0:T(8,128)(2,1)S(1)}, u32[]{:S(2)}, u32[]{:S(2)}) collective-permute-start(bf16[2,32,1536]{2,1,0:T(8,128)(2,1)S(1)} %add_up.12.refs_2_), channel_id=1, source_target_pairs={{0,16},{1,17},{2,18},{3,19},{4,20},{5,21},{6,22},{7,23},{8,24},{9,... | collective-permute-start | bytes 589832 | tf_op jit(solution)/shard_map/ppermute | solution.py:30
  73.7 1.7 collective-permute-start.23
  75.7 6.0 %collective-permute-done.17.refs_3_ = bf16[2,32,1536]{2,1,0:T(8,128)(2,1)S(1)} collective-permute-done((bf16[2,32,1536]{2,1,0:T(8,128)(2,1)S(1)}, bf16[2,32,1536]{2,1,0:T(8,128)(2,1)S(1)}, u32[]{:S(2)}, u32[]{:S(2)}) %collective-permute-start.17) | collective-permute-done | bytes 196640 | tf_op jit(solution)/shard_map/ppermute | solution.py:30
  81.9 5.0 %collective-permute-done.16.refs_2_ = bf16[2,64,1024]{2,1,0:T(8,128)(2,1)S(1)} collective-permute-done((bf16[2,64,1024]{2,1,0:T(8,128)(2,1)S(1)}, bf16[2,64,1024]{2,1,0:T(8,128)(2,1)S(1)}, u32[]{:S(2)}, u32[]{:S(2)}) %collective-permute-start.16) | collective-permute-done | bytes 262176 | tf_op jit(solution)/shard_map/ppermute | solution.py:30
  87.0 6.0 %collective-permute-done.15.refs_3_ = bf16[2,32,1024]{2,1,0:T(8,128)(2,1)S(1)} collective-permute-done((bf16[2,32,1024]{2,1,0:T(8,128)(2,1)S(1)}, bf16[2,32,1024]{2,1,0:T(8,128)(2,1)S(1)}, u32[]{:S(2)}, u32[]{:S(2)}) %collective-permute-start.15) | collective-permute-done | bytes 131104 | tf_op jit(solution)/shard_map/ppermute | solution.py:30
  93.1 4.1 %collective-permute-start.19 = (bf16[2,64,1536]{2,1,0:T(8,128)(2,1)S(1)}, bf16[2,64,1536]{2,1,0:T(8,128)(2,1)S(1)}, u32[]{:S(2)}, u32[]{:S(2)}) collective-permute-start(bf16[2,64,1536]{2,1,0:T(8,128)(2,1)S(1)} %add_up.17.refs_3_), channel_id=1, source_target_pairs={{0,8},{1,5},{2,10},{3,7},{4,12},{5,1},{6,14},{7,3},{8,0},{9,13},{1... | collective-permute-start | bytes 1179656 | tf_op jit(solution)/shard_map/ppermute | solution.py:30
  97.2 3.0 %collective-permute-start.28 = (bf16[2,32,1536]{2,1,0:T(8,128)(2,1)S(1)}, bf16[2,32,1536]{2,1,0:T(8,128)(2,1)S(1)}, u32[]{:S(2)}, u32[]{:S(2)}) collective-permute-start(bf16[2,32,1536]{2,1,0:T(8,128)(2,1)S(1)} %add_up.18.refs_2_), channel_id=1, source_target_pairs={{0,16},{1,17},{2,18},{3,19},{4,20},{5,21},{6,22},{7,23},{8,24},{9,... | collective-permute-start | bytes 589832 | tf_op jit(solution)/shard_map/ppermute | solution.py:30
  100.2 6.6 %collective-permute-done.22.refs_1_ = bf16[32,1536]{1,0:T(8,128)(2,1)S(1)} collective-permute-done((bf16[32,1536]{1,0:T(8,128)(2,1)S(1)}, bf16[32,1536]{1,0:T(8,128)(2,1)S(1)}, u32[]{:S(2)}, u32[]{:S(2)}) %collective-permute-start.22) | collective-permute-done | bytes 98336 | tf_op jit(solution)/shard_map/ppermute | solution.py:30
  106.9 1.6 collective-permute-start.27
  108.5 2.0 %collective-permute-start.21 = (bf16[2,32,1024]{2,1,0:T(8,128)(2,1)S(1)}, bf16[2,32,1024]{2,1,0:T(8,128)(2,1)S(1)}, u32[]{:S(2)}, u32[]{:S(2)}) collective-permute-start(bf16[2,32,1024]{2,1,0:T(8,128)(2,1)S(1)} %add_up.16.refs_5_), channel_id=1, source_target_pairs={{0,16},{1,17},{2,18},{3,19},{4,20},{5,21},{6,22},{7,23},{8,24},{9,... | collective-permute-start | bytes 393224 | tf_op jit(solution)/shard_map/ppermute | solution.py:30
  111.4 7.5 %collective-permute-done.21.refs_3_ = bf16[2,32,1024]{2,1,0:T(8,128)(2,1)S(1)} collective-permute-done((bf16[2,32,1024]{2,1,0:T(8,128)(2,1)S(1)}, bf16[2,32,1024]{2,1,0:T(8,128)(2,1)S(1)}, u32[]{:S(2)}, u32[]{:S(2)}) %collective-permute-start.21) | collective-permute-done | bytes 131104 | tf_op jit(solution)/shard_map/ppermute | solution.py:30
  119.9 1.7 collective-permute-start.30
  121.6 2.9 %collective-permute-start.25 = (bf16[64,1024]{1,0:T(8,128)(2,1)S(1)}, bf16[64,1024]{1,0:T(8,128)(2,1)S(1)}, u32[]{:S(2)}, u32[]{:S(2)}) collective-permute-start(bf16[64,1024]{1,0:T(8,128)(2,1)S(1)} %join.11.refs_3_.refs_0_), channel_id=1, source_target_pairs={{0,8},{1,5},{2,10},{3,7},{4,12},{5,1},{6,14},{7,3},{8,0},{9,13},{1... | collective-permute-start | bytes 393224 | tf_op jit(solution)/shard_map/ppermute | solution.py:30
  124.5 10.4 %collective-permute-done.26.refs_1_ = bf16[32,1024]{1,0:T(8,128)(2,1)S(1)} collective-permute-done((bf16[32,1024]{1,0:T(8,128)(2,1)S(1)}, bf16[32,1024]{1,0:T(8,128)(2,1)S(1)}, u32[]{:S(2)}, u32[]{:S(2)}) %collective-permute-start.26) | collective-permute-done | bytes 65568 | tf_op jit(solution)/shard_map/ppermute | solution.py:30
  135.1 2.9 %collective-permute-start.32 = (bf16[32,1536]{1,0:T(8,128)(2,1)S(1)}, bf16[32,1536]{1,0:T(8,128)(2,1)S(1)}, u32[]{:S(2)}, u32[]{:S(2)}) collective-permute-start(bf16[32,1536]{1,0:T(8,128)(2,1)S(1)} %activate.8.refs_2_.refs_0_), channel_id=1, source_target_pairs={{0,16},{1,17},{2,18},{3,19},{4,20},{5,21},{6,22},{7,23},{8,24},{9,... | collective-permute-start | bytes 294920 | tf_op jit(solution)/shard_map/ppermute | solution.py:30
  138.3 1.5 collective-permute-start.34
  139.8 5.8 %collective-permute-done.32.refs_1_ = bf16[32,1536]{1,0:T(8,128)(2,1)S(1)} collective-permute-done((bf16[32,1536]{1,0:T(8,128)(2,1)S(1)}, bf16[32,1536]{1,0:T(8,128)(2,1)S(1)}, u32[]{:S(2)}, u32[]{:S(2)}) %collective-permute-start.32) | collective-permute-done | bytes 98336 | tf_op jit(solution)/shard_map/ppermute | solution.py:30
  145.7 4.9 %down.5.refs_2_.refs_3_ = f32[256,2048]{1,0:T(8,128)S(1)} custom-call(bf16[128,1536]{1,0:T(8,128)(2,1)S(1)} %join.12.refs_2_.refs_0_, bf16[128,1536]{1,0:T(8,128)(2,1)S(1)} %collective-permute-done.30.refs_1_, bf16[6656,2048]{1,0:T(8,128)(2,1)} %refs_2_.19, bf16[128,1024]{1,0:T(8,128)(2,1)S(1)} %join.16.refs_3_.refs_0_), custom_call_target="tpu_custom_call" | custom-call | flops 1 | bytes 1024 | tf_op jit(solution)/shard_map/down/pallas_call | solution.py:57
  150.7 2.1 %collective-permute-start.33 = (bf16[64,1536]{1,0:T(8,128)(2,1)S(1)}, bf16[64,1536]{1,0:T(8,128)(2,1)S(1)}, u32[]{:S(2)}, u32[]{:S(2)}) collective-permute-start(bf16[64,1536]{1,0:T(8,128)(2,1)S(1)} %join.17.refs_2_.refs_0_), channel_id=1, source_target_pairs={{0,8},{1,5},{2,10},{3,7},{4,12},{5,1},{6,14},{7,3},{8,0},{9,13},{1... | collective-permute-start | bytes 589832 | tf_op jit(solution)/shard_map/ppermute | solution.py:30
  152.9 4.1 %down.6.refs_2_.refs_3_ = f32[256,2048]{1,0:T(8,128)S(1)} custom-call(bf16[128,1024]{1,0:T(8,128)(2,1)S(1)} %join.14.refs_5_.refs_0_, bf16[128,1024]{1,0:T(8,128)(2,1)S(1)} %collective-permute-done.34.refs_1_, bf16[6656,2048]{1,0:T(8,128)(2,1)} %refs_2_.19, f32[256,2048]{1,0:T(8,128)S(1)} %down.5.refs_2_.refs_3_, bf16[128,1536]{1,0:T(8,128)(2,1)S(1)} %join.18.refs_4_.refs_0_), custom_call_target="tpu_custom_call" | custom-call | flops 1 | bytes 1024 | tf_op jit(solution)/shard_map/down/pallas_call | solution.py:57
  156.9 1.6 collective-permute-done.33.refs_1_
  159.0 1.6 collective-permute-start.38
  160.7 8.6 %collective-permute-done.38.refs_1_ = bf16[128,1024]{1,0:T(8,128)(2,1)S(1)} collective-permute-done((bf16[128,1024]{1,0:T(8,128)(2,1)S(1)}, bf16[128,1024]{1,0:T(8,128)(2,1)S(1)}, u32[]{:S(2)}, u32[]{:S(2)}) %collective-permute-start.38) | collective-permute-done | bytes 262176 | tf_op jit(solution)/shard_map/ppermute | solution.py:30
  169.3 4.1 %down.7.refs_3_.refs_4_ = f32[256,2048]{1,0:T(8,128)S(1)} custom-call(bf16[128,1024]{1,0:T(8,128)(2,1)S(1)} %join.16.refs_3_.refs_0_, bf16[128,1024]{1,0:T(8,128)(2,1)S(1)} %collective-permute-done.38.refs_1_, bf16[6656,2048]{1,0:T(8,128)(2,1)} %refs_2_.19, f32[256,2048]{1,0:T(8,128)S(1)} %down.6.refs_2_.refs_3_, bf16[128,1536]{1,0:T(8,128)(2,1)S(1)} %join.19.refs_4_.refs_0_), custom_call_target="tpu_custom_call" | custom-call | flops 1 | bytes 1024 | tf_op jit(solution)/shard_map/down/pallas_call | solution.py:57
  173.3 4.9 %down.8.refs_3_.refs_4_ = f32[256,2048]{1,0:T(8,128)S(1)} custom-call(bf16[128,1536]{1,0:T(8,128)(2,1)S(1)} %join.18.refs_4_.refs_0_, bf16[128,1536]{1,0:T(8,128)(2,1)S(1)} %collective-permute-done.37.refs_1_, bf16[6656,2048]{1,0:T(8,128)(2,1)} %refs_2_.19, f32[256,2048]{1,0:T(8,128)S(1)} %down.7.refs_3_.refs_4_, f32[256,2048]{1,0:T(8,128)S(1)} %down.7.refs_3_.refs_4_), custom_call_target="tpu_custom_call" | custom-call | flops 1 | bytes 1024 | tf_op jit(solution)/shard_map/down/pallas_call | solution.py:57
  178.3 5.0 %down.9 = (f32[128,2048]{1,0:T(8,128)S(1)}, bf16[128,2048]{1,0:T(8,128)(2,1)S(1)}) custom-call(bf16[128,1536]{1,0:T(8,128)(2,1)S(1)} %join.19.refs_4_.refs_0_, bf16[128,1536]{1,0:T(8,128)(2,1)S(1)} %collective-permute-done.36.refs_1_, bf16[6656,2048]{1,0:T(8,128)(2,1)} %refs_2_.19, f32[256,2048]{1,0:T(8,128)S(1)} %down.8.refs_3_.refs_4_, ...), custom_call_target="tpu_custom_call" | custom-call | flops 1 | bytes 1024 | tf_op jit(solution)/shard_map/down/pallas_call | solution.py:57
  183.4 1.9 collective-permute-done.39.refs_1_
  185.3 1.6 collective-permute-start.40
  186.9 6.8 %collective-permute-done.40.refs_2_ = bf16[64,2048]{1,0:T(8,128)(2,1)S(1)} collective-permute-done((bf16[64,2048]{1,0:T(8,128)(2,1)S(1)}, bf16[64,2048]{1,0:T(8,128)(2,1)S(1)}, u32[]{:S(2)}, u32[]{:S(2)}) %collective-permute-start.40) | collective-permute-done | bytes 262176 | tf_op jit(solution)/shard_map/ppermute | solution.py:30
  (80 shorter events, 14.0 us)
Async XLA Ops:
  0.0 9.5 %collective-permute-start.1 = (bf16[64,2048]{1,0:T(8,128)(2,1)}, bf16[64,2048]{1,0:T(8,128)(2,1)S(1)}, u32[]{:S(2)}, u32[]{:S(2)}) collective-permute-start(bf16[64,2048]{1,0:T(8,128)(2,1)} %refs_0_.5), channel_id=1, source_target_pairs={{0,2},{1,3},{2,0},{3,1},{4,6},{5,7},{6,4},{7,5},{8,10},{9,11},{10,... | collective-permute-start | bytes 786440 | tf_op jit(solution)/shard_map/ppermute | solution.py:30
  4.1 3.9 %collective-permute-start.2 = (f32[64,128]{1,0:T(8,128)S(1)}, f32[64,128]{1,0:T(8,128)S(1)}, u32[]{:S(2)}, u32[]{:S(2)}) collective-permute-start(f32[64,128]{1,0:T(8,128)S(1)} %squares.1.refs_0_.refs_2_), channel_id=1, source_target_pairs={{0,4},{1,9},{2,6},{3,11},{4,0},{5,13},{6,2},{7,15},{8,12},{9,1},{1... | collective-permute-start | bytes 98312 | tf_op jit(solution)/shard_map/ppermute | solution.py:30
  5.6 10.6 %collective-permute-start = (bf16[64,2048]{1,0:T(8,128)(2,1)}, bf16[64,2048]{1,0:T(8,128)(2,1)S(1)}, u32[]{:S(2)}, u32[]{:S(2)}) collective-permute-start(bf16[64,2048]{1,0:T(8,128)(2,1)} %refs_0_.5), channel_id=1, source_target_pairs={{0,1},{1,0},{2,3},{3,2},{4,5},{5,4},{6,7},{7,6},{8,9},{9,8},{10,11... | collective-permute-start | bytes 786440 | tf_op jit(solution)/shard_map/ppermute | solution.py:30
  9.5 6.7 %collective-permute-start.3 = (bf16[64,2048]{1,0:T(8,128)(2,1)S(1)}, bf16[64,2048]{1,0:T(8,128)(2,1)S(1)}, u32[]{:S(2)}, u32[]{:S(2)}) collective-permute-start(bf16[64,2048]{1,0:T(8,128)(2,1)S(1)} %pass.1.refs_2_), channel_id=1, source_target_pairs={{0,1},{1,0},{2,3},{3,2},{4,5},{5,4},{6,7},{7,6},{8,9},{9,8},{10,11... | collective-permute-start | bytes 786440 | tf_op jit(solution)/shard_map/ppermute | solution.py:30
  9.5 3.9 %collective-permute-start.4 = (f32[64,128]{1,0:T(8,128)S(1)}, f32[64,128]{1,0:T(8,128)S(1)}, u32[]{:S(2)}, u32[]{:S(2)}) collective-permute-start(f32[64,128]{1,0:T(8,128)S(1)} %squares_add.3.refs_1_.refs_0_), channel_id=1, source_target_pairs={{0,8},{1,5},{2,10},{3,7},{4,12},{5,1},{6,14},{7,3},{8,0},{9,13},{1... | collective-permute-start | bytes 98312 | tf_op jit(solution)/shard_map/ppermute | solution.py:30
  13.4 4.8 %collective-permute-start.5 = (f32[64,128]{1,0:T(8,128)S(1)}, f32[64,128]{1,0:T(8,128)S(1)}, u32[]{:S(2)}, u32[]{:S(2)}) collective-permute-start(f32[64,128]{1,0:T(8,128)S(1)} %squares_add.4.refs_5_.refs_0_), channel_id=1, source_target_pairs={{0,16},{1,17},{2,18},{3,19},{4,20},{5,21},{6,22},{7,23},{8,24},{9,... | collective-permute-start | bytes 98312 | tf_op jit(solution)/shard_map/ppermute | solution.py:30
  16.2 0.7 copy-start
  25.5 13.4 %collective-permute-start.10 = (bf16[2,128,1536]{2,1,0:T(8,128)(2,1)S(1)}, bf16[2,128,1536]{2,1,0:T(8,128)(2,1)S(1)}, u32[]{:S(2)}, u32[]{:S(2)}) collective-permute-start(bf16[2,128,1536]{2,1,0:T(8,128)(2,1)S(1)} %get-tuple-element.23), channel_id=1, source_target_pairs={{0,4},{1,9},{2,6},{3,11},{4,0},{5,13},{6,2},{7,15},{8,12},{9,1},{1... | collective-permute-start | bytes 2359304 | tf_op jit(solution)/shard_map/ppermute | solution.py:30
  27.3 3.9 %collective-permute-start.7 = (f32[64,128]{1,0:T(8,128)S(1)}, f32[64,128]{1,0:T(8,128)S(1)}, u32[]{:S(2)}, u32[]{:S(2)}) collective-permute-start(f32[64,128]{1,0:T(8,128)S(1)} %squares_add.5.refs_3_.refs_4_), channel_id=1, source_target_pairs={{0,2},{1,3},{2,0},{3,1},{4,6},{5,7},{6,4},{7,5},{8,10},{9,11},{10,... | collective-permute-start | bytes 98312 | tf_op jit(solution)/shard_map/ppermute | solution.py:30
  28.8 2.4 %collective-permute-start.6 = (f32[64,128]{1,0:T(8,128)S(1)}, f32[64,128]{1,0:T(8,128)S(1)}, u32[]{:S(2)}, u32[]{:S(2)}) collective-permute-start(f32[64,128]{1,0:T(8,128)S(1)} %squares_add.5.refs_3_.refs_4_), channel_id=1, source_target_pairs={{0,1},{1,0},{2,3},{3,2},{4,5},{5,4},{6,7},{7,6},{8,9},{9,8},{10,11... | collective-permute-start | bytes 98312 | tf_op jit(solution)/shard_map/ppermute | solution.py:30
  31.2 1.2 collective-permute-start.8
  38.5 9.2 %collective-permute-start.9 = (bf16[2,128,1024]{2,1,0:T(8,128)(2,1)S(1)}, bf16[2,128,1024]{2,1,0:T(8,128)(2,1)S(1)}, u32[]{:S(2)}, u32[]{:S(2)}) collective-permute-start(bf16[2,128,1024]{2,1,0:T(8,128)(2,1)S(1)} %get-tuple-element.22), channel_id=1, source_target_pairs={{0,4},{1,9},{2,6},{3,11},{4,0},{5,13},{6,2},{7,15},{8,12},{9,1},{1... | collective-permute-start | bytes 1572872 | tf_op jit(solution)/shard_map/ppermute | solution.py:30
  43.9 15.0 %collective-permute-start.12 = (bf16[2,128,1024]{2,1,0:T(8,128)(2,1)S(1)}, bf16[2,128,1024]{2,1,0:T(8,128)(2,1)S(1)}, u32[]{:S(2)}, u32[]{:S(2)}) collective-permute-start(bf16[2,128,1024]{2,1,0:T(8,128)(2,1)S(1)} %get-tuple-element.25), channel_id=1, source_target_pairs={{0,4},{1,9},{2,6},{3,11},{4,0},{5,13},{6,2},{7,15},{8,12},{9,1},{1... | collective-permute-start | bytes 1572872 | tf_op jit(solution)/shard_map/ppermute | solution.py:30
  45.7 12.1 %collective-permute-start.13 = (bf16[2,64,1536]{2,1,0:T(8,128)(2,1)S(1)}, bf16[2,64,1536]{2,1,0:T(8,128)(2,1)S(1)}, u32[]{:S(2)}, u32[]{:S(2)}) collective-permute-start(bf16[2,64,1536]{2,1,0:T(8,128)(2,1)S(1)} %add_up.10.refs_3_), channel_id=1, source_target_pairs={{0,8},{1,5},{2,10},{3,7},{4,12},{5,1},{6,14},{7,3},{8,0},{9,13},{1... | collective-permute-start | bytes 1179656 | tf_op jit(solution)/shard_map/ppermute | solution.py:30
  47.8 15.5 %collective-permute-start.11 = (bf16[2,64,1024]{2,1,0:T(8,128)(2,1)S(1)}, bf16[2,64,1024]{2,1,0:T(8,128)(2,1)S(1)}, u32[]{:S(2)}, u32[]{:S(2)}) collective-permute-start(bf16[2,64,1024]{2,1,0:T(8,128)(2,1)S(1)} %add_up.11.refs_3_), channel_id=1, source_target_pairs={{0,8},{1,5},{2,10},{3,7},{4,12},{5,1},{6,14},{7,3},{8,0},{9,13},{1... | collective-permute-start | bytes 786440 | tf_op jit(solution)/shard_map/ppermute | solution.py:30
  56.7 16.9 %collective-permute-start.18 = (bf16[2,128,1536]{2,1,0:T(8,128)(2,1)S(1)}, bf16[2,128,1536]{2,1,0:T(8,128)(2,1)S(1)}, u32[]{:S(2)}, u32[]{:S(2)}) collective-permute-start(bf16[2,128,1536]{2,1,0:T(8,128)(2,1)S(1)} %get-tuple-element.30), channel_id=1, source_target_pairs={{0,4},{1,9},{2,6},{3,11},{4,0},{5,13},{6,2},{7,15},{8,12},{9,1},{1... | collective-permute-start | bytes 2359304 | tf_op jit(solution)/shard_map/ppermute | solution.py:30
  70.5 22.5 %collective-permute-start.14 = (bf16[2,128,1536]{2,1,0:T(8,128)(2,1)S(1)}, bf16[2,128,1536]{2,1,0:T(8,128)(2,1)S(1)}, u32[]{:S(2)}, u32[]{:S(2)}) collective-permute-start(bf16[2,128,1536]{2,1,0:T(8,128)(2,1)S(1)} %get-tuple-element.28), channel_id=1, source_target_pairs={{0,4},{1,9},{2,6},{3,11},{4,0},{5,13},{6,2},{7,15},{8,12},{9,1},{1... | collective-permute-start | bytes 2359304 | tf_op jit(solution)/shard_map/ppermute | solution.py:30
  70.6 16.3 %collective-permute-start.16 = (bf16[2,64,1024]{2,1,0:T(8,128)(2,1)S(1)}, bf16[2,64,1024]{2,1,0:T(8,128)(2,1)S(1)}, u32[]{:S(2)}, u32[]{:S(2)}) collective-permute-start(bf16[2,64,1024]{2,1,0:T(8,128)(2,1)S(1)} %add_up.13.refs_3_), channel_id=1, source_target_pairs={{0,8},{1,5},{2,10},{3,7},{4,12},{5,1},{6,14},{7,3},{8,0},{9,13},{1... | collective-permute-start | bytes 786440 | tf_op jit(solution)/shard_map/ppermute | solution.py:30
  70.8 10.9 %collective-permute-start.17 = (bf16[2,32,1536]{2,1,0:T(8,128)(2,1)S(1)}, bf16[2,32,1536]{2,1,0:T(8,128)(2,1)S(1)}, u32[]{:S(2)}, u32[]{:S(2)}) collective-permute-start(bf16[2,32,1536]{2,1,0:T(8,128)(2,1)S(1)} %add_up.12.refs_2_), channel_id=1, source_target_pairs={{0,16},{1,17},{2,18},{3,19},{4,20},{5,21},{6,22},{7,23},{8,24},{9,... | collective-permute-start | bytes 589832 | tf_op jit(solution)/shard_map/ppermute | solution.py:30
  73.7 23.5 %collective-permute-start.23 = (bf16[2,64,1536]{2,1,0:T(8,128)(2,1)S(1)}, bf16[2,64,1536]{2,1,0:T(8,128)(2,1)S(1)}, u32[]{:S(2)}, u32[]{:S(2)}) collective-permute-start(bf16[2,64,1536]{2,1,0:T(8,128)(2,1)S(1)} %add_up.15.refs_5_), channel_id=1, source_target_pairs={{0,8},{1,5},{2,10},{3,7},{4,12},{5,1},{6,14},{7,3},{8,0},{9,13},{1... | collective-permute-start | bytes 1179656 | tf_op jit(solution)/shard_map/ppermute | solution.py:30
  75.4 17.5 %collective-permute-start.15 = (bf16[2,32,1024]{2,1,0:T(8,128)(2,1)S(1)}, bf16[2,32,1024]{2,1,0:T(8,128)(2,1)S(1)}, u32[]{:S(2)}, u32[]{:S(2)}) collective-permute-start(bf16[2,32,1024]{2,1,0:T(8,128)(2,1)S(1)} %add_up.14.refs_3_), channel_id=1, source_target_pairs={{0,16},{1,17},{2,18},{3,19},{4,20},{5,21},{6,22},{7,23},{8,24},{9,... | collective-permute-start | bytes 393224 | tf_op jit(solution)/shard_map/ppermute | solution.py:30
  93.1 26.5 %collective-permute-start.19 = (bf16[2,64,1536]{2,1,0:T(8,128)(2,1)S(1)}, bf16[2,64,1536]{2,1,0:T(8,128)(2,1)S(1)}, u32[]{:S(2)}, u32[]{:S(2)}) collective-permute-start(bf16[2,64,1536]{2,1,0:T(8,128)(2,1)S(1)} %add_up.17.refs_3_), channel_id=1, source_target_pairs={{0,8},{1,5},{2,10},{3,7},{4,12},{5,1},{6,14},{7,3},{8,0},{9,13},{1... | collective-permute-start | bytes 1179656 | tf_op jit(solution)/shard_map/ppermute | solution.py:30
  97.2 9.7 %collective-permute-start.22 = (bf16[32,1536]{1,0:T(8,128)(2,1)S(1)}, bf16[32,1536]{1,0:T(8,128)(2,1)S(1)}, u32[]{:S(2)}, u32[]{:S(2)}) collective-permute-start(bf16[32,1536]{1,0:T(8,128)(2,1)S(1)} %activate.5.refs_3_.refs_0_), channel_id=1, source_target_pairs={{0,16},{1,17},{2,18},{3,19},{4,20},{5,21},{6,22},{7,23},{8,24},{9,... | collective-permute-start | bytes 294920 | tf_op jit(solution)/shard_map/ppermute | solution.py:30
  97.2 22.5 %collective-permute-start.28 = (bf16[2,32,1536]{2,1,0:T(8,128)(2,1)S(1)}, bf16[2,32,1536]{2,1,0:T(8,128)(2,1)S(1)}, u32[]{:S(2)}, u32[]{:S(2)}) collective-permute-start(bf16[2,32,1536]{2,1,0:T(8,128)(2,1)S(1)} %add_up.18.refs_2_), channel_id=1, source_target_pairs={{0,16},{1,17},{2,18},{3,19},{4,20},{5,21},{6,22},{7,23},{8,24},{9,... | collective-permute-start | bytes 589832 | tf_op jit(solution)/shard_map/ppermute | solution.py:30
  106.9 13.0 %collective-permute-start.27 = (bf16[64,1536]{1,0:T(8,128)(2,1)S(1)}, bf16[64,1536]{1,0:T(8,128)(2,1)S(1)}, u32[]{:S(2)}, u32[]{:S(2)}) collective-permute-start(bf16[64,1536]{1,0:T(8,128)(2,1)S(1)} %join.10.refs_5_.refs_0_), channel_id=1, source_target_pairs={{0,8},{1,5},{2,10},{3,7},{4,12},{5,1},{6,14},{7,3},{8,0},{9,13},{1... | collective-permute-start | bytes 589832 | tf_op jit(solution)/shard_map/ppermute | solution.py:30
  108.5 10.5 %collective-permute-start.21 = (bf16[2,32,1024]{2,1,0:T(8,128)(2,1)S(1)}, bf16[2,32,1024]{2,1,0:T(8,128)(2,1)S(1)}, u32[]{:S(2)}, u32[]{:S(2)}) collective-permute-start(bf16[2,32,1024]{2,1,0:T(8,128)(2,1)S(1)} %add_up.16.refs_5_), channel_id=1, source_target_pairs={{0,16},{1,17},{2,18},{3,19},{4,20},{5,21},{6,22},{7,23},{8,24},{9,... | collective-permute-start | bytes 393224 | tf_op jit(solution)/shard_map/ppermute | solution.py:30
  110.5 9.1 %collective-permute-start.20 = (bf16[32,1024]{1,0:T(8,128)(2,1)S(1)}, bf16[32,1024]{1,0:T(8,128)(2,1)S(1)}, u32[]{:S(2)}, u32[]{:S(2)}) collective-permute-start(bf16[32,1024]{1,0:T(8,128)(2,1)S(1)} %activate.6.refs_2_.refs_0_), channel_id=1, source_target_pairs={{0,16},{1,17},{2,18},{3,19},{4,20},{5,21},{6,22},{7,23},{8,24},{9,... | collective-permute-start | bytes 196616 | tf_op jit(solution)/shard_map/ppermute | solution.py:30
  119.9 25.8 %collective-permute-start.30 = (bf16[128,1536]{1,0:T(8,128)(2,1)S(1)}, bf16[128,1536]{1,0:T(8,128)(2,1)S(1)}, u32[]{:S(2)}, u32[]{:S(2)}) collective-permute-start(bf16[128,1536]{1,0:T(8,128)(2,1)S(1)} %join.12.refs_2_.refs_0_), channel_id=1, source_target_pairs={{0,4},{1,9},{2,6},{3,11},{4,0},{5,13},{6,2},{7,15},{8,12},{9,1},{1... | collective-permute-start | bytes 1179656 | tf_op jit(solution)/shard_map/ppermute | solution.py:30
  121.6 16.4 %collective-permute-start.24 = (bf16[2,32,1536]{2,1,0:T(8,128)(2,1)S(1)}, bf16[2,32,1536]{2,1,0:T(8,128)(2,1)S(1)}, u32[]{:S(2)}, u32[]{:S(2)}) collective-permute-start(bf16[2,32,1536]{2,1,0:T(8,128)(2,1)S(1)} %add_up.19.refs_5_), channel_id=1, source_target_pairs={{0,16},{1,17},{2,18},{3,19},{4,20},{5,21},{6,22},{7,23},{8,24},{9,... | collective-permute-start | bytes 589832 | tf_op jit(solution)/shard_map/ppermute | solution.py:30
  121.6 16.4 %collective-permute-start.25 = (bf16[64,1024]{1,0:T(8,128)(2,1)S(1)}, bf16[64,1024]{1,0:T(8,128)(2,1)S(1)}, u32[]{:S(2)}, u32[]{:S(2)}) collective-permute-start(bf16[64,1024]{1,0:T(8,128)(2,1)S(1)} %join.11.refs_3_.refs_0_), channel_id=1, source_target_pairs={{0,8},{1,5},{2,10},{3,7},{4,12},{5,1},{6,14},{7,3},{8,0},{9,13},{1... | collective-permute-start | bytes 393224 | tf_op jit(solution)/shard_map/ppermute | solution.py:30
  124.5 10.5 %collective-permute-start.26 = (bf16[32,1024]{1,0:T(8,128)(2,1)S(1)}, bf16[32,1024]{1,0:T(8,128)(2,1)S(1)}, u32[]{:S(2)}, u32[]{:S(2)}) collective-permute-start(bf16[32,1024]{1,0:T(8,128)(2,1)S(1)} %activate.7.refs_2_.refs_0_), channel_id=1, source_target_pairs={{0,16},{1,17},{2,18},{3,19},{4,20},{5,21},{6,22},{7,23},{8,24},{9,... | collective-permute-start | bytes 196616 | tf_op jit(solution)/shard_map/ppermute | solution.py:30
  135.0 10.7 %collective-permute-start.31 = (bf16[64,1024]{1,0:T(8,128)(2,1)S(1)}, bf16[64,1024]{1,0:T(8,128)(2,1)S(1)}, u32[]{:S(2)}, u32[]{:S(2)}) collective-permute-start(bf16[64,1024]{1,0:T(8,128)(2,1)S(1)} %join.13.refs_2_.refs_0_), channel_id=1, source_target_pairs={{0,8},{1,5},{2,10},{3,7},{4,12},{5,1},{6,14},{7,3},{8,0},{9,13},{1... | collective-permute-start | bytes 393224 | tf_op jit(solution)/shard_map/ppermute | solution.py:30
  135.1 10.5 %collective-permute-start.32 = (bf16[32,1536]{1,0:T(8,128)(2,1)S(1)}, bf16[32,1536]{1,0:T(8,128)(2,1)S(1)}, u32[]{:S(2)}, u32[]{:S(2)}) collective-permute-start(bf16[32,1536]{1,0:T(8,128)(2,1)S(1)} %activate.8.refs_2_.refs_0_), channel_id=1, source_target_pairs={{0,16},{1,17},{2,18},{3,19},{4,20},{5,21},{6,22},{7,23},{8,24},{9,... | collective-permute-start | bytes 294920 | tf_op jit(solution)/shard_map/ppermute | solution.py:30
  138.2 12.4 %collective-permute-start.29 = (bf16[32,1536]{1,0:T(8,128)(2,1)S(1)}, bf16[32,1536]{1,0:T(8,128)(2,1)S(1)}, u32[]{:S(2)}, u32[]{:S(2)}) collective-permute-start(bf16[32,1536]{1,0:T(8,128)(2,1)S(1)} %activate.9.refs_2_.refs_0_), channel_id=1, source_target_pairs={{0,16},{1,17},{2,18},{3,19},{4,20},{5,21},{6,22},{7,23},{8,24},{9,... | collective-permute-start | bytes 294920 | tf_op jit(solution)/shard_map/ppermute | solution.py:30
  138.3 14.5 %collective-permute-start.34 = (bf16[128,1024]{1,0:T(8,128)(2,1)S(1)}, bf16[128,1024]{1,0:T(8,128)(2,1)S(1)}, u32[]{:S(2)}, u32[]{:S(2)}) collective-permute-start(bf16[128,1024]{1,0:T(8,128)(2,1)S(1)} %join.14.refs_5_.refs_0_), channel_id=1, source_target_pairs={{0,4},{1,9},{2,6},{3,11},{4,0},{5,13},{6,2},{7,15},{8,12},{9,1},{1... | collective-permute-start | bytes 786440 | tf_op jit(solution)/shard_map/ppermute | solution.py:30
  145.6 7.1 %collective-permute-start.35 = (bf16[64,1536]{1,0:T(8,128)(2,1)S(1)}, bf16[64,1536]{1,0:T(8,128)(2,1)S(1)}, u32[]{:S(2)}, u32[]{:S(2)}) collective-permute-start(bf16[64,1536]{1,0:T(8,128)(2,1)S(1)} %join.15.refs_2_.refs_0_), channel_id=1, source_target_pairs={{0,8},{1,5},{2,10},{3,7},{4,12},{5,1},{6,14},{7,3},{8,0},{9,13},{1... | collective-permute-start | bytes 589832 | tf_op jit(solution)/shard_map/ppermute | solution.py:30
  150.7 7.9 %collective-permute-start.33 = (bf16[64,1536]{1,0:T(8,128)(2,1)S(1)}, bf16[64,1536]{1,0:T(8,128)(2,1)S(1)}, u32[]{:S(2)}, u32[]{:S(2)}) collective-permute-start(bf16[64,1536]{1,0:T(8,128)(2,1)S(1)} %join.17.refs_2_.refs_0_), channel_id=1, source_target_pairs={{0,8},{1,5},{2,10},{3,7},{4,12},{5,1},{6,14},{7,3},{8,0},{9,13},{1... | collective-permute-start | bytes 589832 | tf_op jit(solution)/shard_map/ppermute | solution.py:30
  152.8 20.6 %collective-permute-start.37 = (bf16[128,1536]{1,0:T(8,128)(2,1)S(1)}, bf16[128,1536]{1,0:T(8,128)(2,1)S(1)}, u32[]{:S(2)}, u32[]{:S(2)}) collective-permute-start(bf16[128,1536]{1,0:T(8,128)(2,1)S(1)} %join.18.refs_4_.refs_0_), channel_id=1, source_target_pairs={{0,4},{1,9},{2,6},{3,11},{4,0},{5,13},{6,2},{7,15},{8,12},{9,1},{1... | collective-permute-start | bytes 1179656 | tf_op jit(solution)/shard_map/ppermute | solution.py:30
  158.6 19.7 %collective-permute-start.36 = (bf16[128,1536]{1,0:T(8,128)(2,1)S(1)}, bf16[128,1536]{1,0:T(8,128)(2,1)S(1)}, u32[]{:S(2)}, u32[]{:S(2)}) collective-permute-start(bf16[128,1536]{1,0:T(8,128)(2,1)S(1)} %join.19.refs_4_.refs_0_), channel_id=1, source_target_pairs={{0,4},{1,9},{2,6},{3,11},{4,0},{5,13},{6,2},{7,15},{8,12},{9,1},{1... | collective-permute-start | bytes 1179656 | tf_op jit(solution)/shard_map/ppermute | solution.py:30
  159.0 10.2 %collective-permute-start.38 = (bf16[128,1024]{1,0:T(8,128)(2,1)S(1)}, bf16[128,1024]{1,0:T(8,128)(2,1)S(1)}, u32[]{:S(2)}, u32[]{:S(2)}) collective-permute-start(bf16[128,1024]{1,0:T(8,128)(2,1)S(1)} %join.16.refs_3_.refs_0_), channel_id=1, source_target_pairs={{0,4},{1,9},{2,6},{3,11},{4,0},{5,13},{6,2},{7,15},{8,12},{9,1},{1... | collective-permute-start | bytes 786440 | tf_op jit(solution)/shard_map/ppermute | solution.py:30
  183.3 2.0 %collective-permute-start.39 = (bf16[128,2048]{1,0:T(8,128)(2,1)S(1)}, bf16[128,2048]{1,0:T(8,128)(2,1)S(1)}, u32[]{:S(2)}, u32[]{:S(2)}) collective-permute-start(bf16[128,2048]{1,0:T(8,128)(2,1)S(1)} %get-tuple-element.32), channel_id=1, source_target_pairs={{0,1},{1,0},{2,3},{3,2},{4,5},{5,4},{6,7},{7,6},{8,9},{9,8},{10,11... | collective-permute-start | bytes 1572872 | tf_op jit(solution)/shard_map/ppermute | solution.py:30
  185.3 8.4 %collective-permute-start.40 = (bf16[64,2048]{1,0:T(8,128)(2,1)S(1)}, bf16[64,2048]{1,0:T(8,128)(2,1)S(1)}, u32[]{:S(2)}, u32[]{:S(2)}) collective-permute-start(bf16[64,2048]{1,0:T(8,128)(2,1)S(1)} %send_y.1.refs_3_), channel_id=1, source_target_pairs={{0,2},{1,3},{2,0},{3,1},{4,6},{5,7},{6,4},{7,5},{8,10},{9,11},{10,... | collective-permute-start | bytes 786440 | tf_op jit(solution)/shard_map/ppermute | solution.py:30

commit v3 on v2

--- a/solution.py
+++ b/solution.py
@@ -9,6 +9,7 @@
 
 F32, BF16 = jnp.float32, jnp.bfloat16
 EPS = 1e-05
+SMALL_FLOPS, UNIT_FLOPS = 4 * 10**9, 25 * 10**7
 VMEM_LIMIT = 48 * 1024 * 1024
 
 AXES = ("wa", "ha")
@@ -19,8 +20,9 @@
     return [(w * 4 + h, (w ^ wa_flips[h % 2]) * 4 + (h ^ ha_flip)) for w in range(8) for h in range(4)]
 
 
-FIRST = swaps((X, Z_LOW))
-SECOND = swaps((Z_LOW, X))
+MODES = {"m": (X, Z_LOW), "n": (Z_LOW, X), "x": (X, X), "z": (Z_LOW, Z_LOW)}
+FIRST = {mode: swaps(bits) for mode, bits in MODES.items()}
+SECOND = {mode: swaps([X + Z_LOW - b for b in bits]) for mode, bits in MODES.items()}
 THIRD = swaps((Z_HIGH, Z_HIGH))
 CORE_SWAP = swaps(ha_flip=1)
 Y_SWAP = swaps(ha_flip=2)
@@ -38,7 +40,7 @@
     def __init__(self):
         self.token = None
 
-    def call(self, kernel, args, out_shape, *, grid=(), in_specs=None, out_specs=None, scratch=(), aliases=None, flops=1, name=None):
+    def call(self, kernel, args, out_shape, *, grid=(), in_specs=None, out_specs=None, scratch=(), aliases=None, flops=SMALL_FLOPS, name=None):
         args = list(args)
         if in_specs is None:
             in_specs = [pl.BlockSpec(memory_space=pltpu.VMEM)] * len(args)
@@ -114,12 +116,26 @@
             r_ref[at, :] = factor[part * half:(part + 1) * half]
 
 
-def project_kernel(lhs_ref, g_ref, u_ref, keep_ref, send_ref):
-    half = lhs_ref.shape[0] // 2
+def crossed(mode, a, b):
+    differs = [p != q for p, q in zip(MODES[mode], MODES["m"])]
+    if all(differs):
+        return b, a
+    if not any(differs):
+        return a, b
+    swapped = lax.rem(lax.axis_index("ha"), 2) == differs.index(True)
+    return jnp.where(swapped, b, a), jnp.where(swapped, a, b)
+
+
+def project_kernel(mode, lhs_ref, g_ref, u_ref, keep_ref, send_ref):
+    quarter = lhs_ref.shape[0] // 4
+    half = 2 * quarter
     for i, w in enumerate((g_ref, u_ref)):
         total = jnp.dot(lhs_ref[...], w[...], preferred_element_type=F32)
-        keep_ref[i] = total[:half]
-        send_ref[i] = total[half:].astype(BF16)
+        second, third = crossed(mode, total[quarter:half], total[half:half + quarter])
+        keep_ref[i, :quarter] = total[:quarter]
+        keep_ref[i, quarter:] = second
+        send_ref[i, :quarter] = third.astype(BF16)
+        send_ref[i, quarter:] = total[half + quarter:].astype(BF16)
 
 
 def sum_of(keep_ref, parts):
@@ -151,8 +167,8 @@
     del a_ref, o_ref
 
 
-def down_kernel(n_parts, first, last, *refs):
-    refs = list(refs)
+def down_kernel(modes, first, last, *refs):
+    refs, n_parts = list(refs), len(modes)
     parts, w_ref, refs = refs[:2 * n_parts], refs[2 * n_parts], refs[2 * n_parts + 1:]
     if not first:
         acc_ref = refs.pop(0)
@@ -165,8 +181,12 @@
         for i in range(n_parts):
             own, other = parts[2 * i:2 * i + 2]
             n = own.shape[1]
-            hid_ref[:half, at:at + n] = own[...]
-            hid_ref[half:, at:at + n] = other[...]
+            quarter = half // 2
+            second, third = crossed(modes[i], own[quarter:], other[:quarter])
+            hid_ref[:quarter, at:at + n] = own[:quarter]
+            hid_ref[quarter:half, at:at + n] = second
+            hid_ref[half:half + quarter, at:at + n] = third
+            hid_ref[half + quarter:, at:at + n] = other[quarter:]
             at += n
 
     total = jnp.dot(hid_ref[...], w_ref[...], preferred_element_type=F32)
@@ -192,13 +212,13 @@
     o_ref[...] = (keep_ref[...] + core_ref[...].astype(F32) + y_ref[...].astype(F32)).astype(BF16)
 
 
-SHARES = (6, 4, 4, 6, 6)
-GROUPS = ((0,), (1,), (2,), (3,), (4,),)
+SHARES = (6, 6, 8, 6,)
+SUM, GATHER = "mmmm", "nnnn"
+GROUPS = ((0, 1,), (2,), (3,),)
 ORDER = (
-    "q", "m0", "n", "m1", "a0", "m2", "a1", "m3", "b0", "a2", "b1", "m4",
-    "a3", "c0", "b2", "c1", "a4", "b3", "d0", "c2", "d1", "b4", "c3", "e0",
-    "d2", "e1", "c4", "d3", "e2", "w0", "d4", "e3", "w1", "e4", "w2", "w3",
-    "w4",
+    "m0", "s", "m1", "a0", "q", "n", "m2", "b0", "a1", "m3", "c0", "b1",
+    "a2", "d0", "c1", "b2", "a3", "e0", "d1", "c2", "b3", "e1", "d2", "c3",
+    "w0", "e2", "d3", "e3", "w1", "w2",
 )
 
 
@@ -213,24 +233,27 @@
 
     t0 = tokens
     sq_shape = shape((rows, 128), F32)
-    (sq,) = chain.call(squares_kernel, [t0], [sq_shape], name="squares")
     t2 = swap(t0, Y_SWAP)
     t1 = swap(t0, CORE_SWAP)
-    (sq,) = chain.call(add_kernel, [sq, swap(sq, FIRST)], [sq_shape], name="squares_add")
-    sq_second = swap(sq, SECOND)
+    (sq,) = chain.call(squares_kernel, [t0], [sq_shape], name="squares")
+    squares = [sq, swap(sq, FIRST["m"])]
     (t2,) = chain.call(
         pass_kernel, [t2], [shape(t2.shape, BF16)], in_specs=[any_spec()], out_specs=[any_spec()], aliases={0: 0}, name="pass",
     )
     t3 = swap(t2, CORE_SWAP)
-    (sq,) = chain.call(add_kernel, [sq, sq_second], [sq_shape], name="squares_add")
-    sq_third = swap(sq, THIRD)
+    (sq,) = chain.call(add_kernel, squares, [sq_shape], name="squares_add")
+    squares = [sq, swap(sq, SECOND["m"])]
     (raw,) = chain.call(arrange_kernel, [t0, t1, t2, t3, gain], [shape((4 * rows, width), BF16)], name="arrange")
 
     state = [dict() for _ in SHARES]
     env = {"lhs": raw, "acc": None}
 
+    def stage_s(k):
+        (total,) = chain.call(add_kernel, squares, [sq_shape], name="squares_add")
+        squares[:] = total, swap(total, THIRD)
+
     def stage_q(k):
-        (s0,) = chain.call(add_kernel, [sq, sq_third], [sq_shape], name="squares_add")
+        (s0,) = chain.call(add_kernel, squares, [sq_shape], name="squares_add")
         s2 = swap(s0, Y_SWAP)
         s1 = swap(s0, CORE_SWAP)
         env["s"] = (s0, s1, s2, swap(s2, CORE_SWAP))
@@ -250,7 +273,7 @@
         tile = 512 if n % 512 == 0 and cuts[k] % 512 == 0 else 256
         first = cuts[k] // tile
         s["keep"], send = chain.call(
-            project_kernel,
+            functools.partial(project_kernel, SUM[k]),
             [env["lhs"], gate_weight, up_weight],
             [shape((2, 2 * rows, n), F32), shape((2, 2 * rows, n), BF16)],
             grid=(n // tile,),
@@ -260,9 +283,10 @@
                 pl.BlockSpec((width, tile), lambda i: (0, first + i)),
             ],
             out_specs=[pl.BlockSpec((2, 2 * rows, tile), lambda i: (0, 0, i))] * 2,
+            flops=UNIT_FLOPS * 5 * SHARES[k],
             name="project",
         )
-        s["parts"] = [swap(send, FIRST)]
+        s["parts"] = [swap(send, FIRST[SUM[k]])]
 
     def part(n, size, at):
         return pl.BlockSpec((2, size, n), lambda i: (0, at, 0))
@@ -277,7 +301,7 @@
         s["parts"].append(swap(send, pairs))
 
     def stage_a(k):
-        add_up(k, rows, SECOND)
+        add_up(k, rows, SECOND[SUM[k]])
 
     def stage_b(k):
         add_up(k, rows // 2, THIRD)
@@ -304,10 +328,10 @@
         s["got"] = swap(s["h"], pairs)
 
     def stage_d(k):
-        join(k, SECOND)
+        join(k, SECOND[GATHER[k]])
 
     def stage_e(k):
-        join(k, FIRST)
+        join(k, FIRST[GATHER[k]])
 
     def stage_w(k):
         group = GROUPS[k]
@@ -332,13 +356,14 @@
             out_specs = [pl.BlockSpec((4 * rows, cols), lambda i: (0, i))]
             scratch = [pltpu.VMEM((4 * rows, n), BF16)]
         env["last"] = chain.call(
-            functools.partial(down_kernel, len(group), first, last), args, out_shape,
-            grid=(out_width // cols,), in_specs=in_specs, out_specs=out_specs, scratch=scratch, name="down",
+            functools.partial(down_kernel, [GATHER[j] for j in group], first, last), args, out_shape,
+            grid=(out_width // cols,), in_specs=in_specs, out_specs=out_specs, scratch=scratch,
+            flops=UNIT_FLOPS * 2 * sum(SHARES[j] for j in group), name="down",
         )
         env["acc"] = env["last"][0]
 
     stages = dict(
-        m=stage_m, a=stage_a, b=stage_b, c=stage_c, d=stage_d, e=stage_e, w=stage_w, q=stage_q, n=stage_n
+        m=stage_m, a=stage_a, b=stage_b, c=stage_c, d=stage_d, e=stage_e, w=stage_w, s=stage_s, q=stage_q, n=stage_n
     )
     for step in ORDER:
         stages[step[0]](int(step[1:] or 0))

time: 195 us -> 164 us (0.84)
  waiting for transfers between devices: 83.2 us -> 64.3 us
  Pallas kernels: 60 us -> 51 us
  starting transfers between devices: 50.2 us -> 47.6 us
    ppermute x41 -> x35, waiting for transfers between devices: 83.2 us -> 64.3 us  [swap(): return lax.ppermute(a, AXES, pairs)]
    pallas_call x44 -> x36, Pallas kernels: 60 us -> 51 us  [call(): pl.pallas_call(run, out_shape=tuple(out_shape), grid=grid, in_specs=in_sp...]
    ppermute x41 -> x35, starting transfers between devices: 50.2 us -> 47.6 us  [swap(): return lax.ppermute(a, AXES, pairs)]
  transfers between devices with their start and end apart: 41 -> 35, of which waited for: 22 -> 15; matrix products, arithmetic and copies ran while one was open for 0% -> 0% of each run, Pallas kernels for 24% -> 28%
where the time goes in v3:
time: 164 us
  waiting for transfers between devices  64.3 us (39%)
  Pallas kernels  51 us (31%)
  starting transfers between devices  47.6 us (29%)
    ppermute x35, waiting for transfers between devices, swap(): return lax.ppermute(a, AXES, pairs)  64.3 us
    pallas_call x36, Pallas kernels, call(): pl.pallas_call(run, out_shape=tuple(out_shape), grid=grid, in_specs=in_sp...  51 us
    ppermute x35, starting transfers between devices, swap(): return lax.ppermute(a, AXES, pairs)  47.6 us
  transfers between devices with their start and end apart: 35, of which 15 were waited for; matrix products, arithmetic and copies ran while one was open for 0% of the time, Pallas kernels for 28%

profile of v3, /device:TPU:0, one launch (start us, length us, event | category | flops | bytes accessed | tf_op | source)
XLA Modules:
  0.0 164.2 jit_solution(13184042406439371922)
XLA Ops:
  0.0 3.0 %collective-permute-start.1 = (bf16[64,2048]{1,0:T(8,128)(2,1)}, bf16[64,2048]{1,0:T(8,128)(2,1)S(1)}, u32[]{:S(2)}, u32[]{:S(2)}) collective-permute-start(bf16[64,2048]{1,0:T(8,128)(2,1)} %refs_0_.5), channel_id=1, source_target_pairs={{0,2},{1,3},{2,0},{3,1},{4,6},{5,7},{6,4},{7,5},{8,10},{9,11},{10,... | collective-permute-start | bytes 786440 | tf_op jit(solution)/shard_map/ppermute | solution.py:32
  3.0 1.0 copy-done
  4.1 1.5 collective-permute-start.3
  5.6 3.9 %collective-permute-done.1.refs_0_ = bf16[64,2048]{1,0:T(8,128)(2,1)S(1)} collective-permute-done((bf16[64,2048]{1,0:T(8,128)(2,1)}, bf16[64,2048]{1,0:T(8,128)(2,1)S(1)}, u32[]{:S(2)}, u32[]{:S(2)}) %collective-permute-start.1) | collective-permute-done | bytes 262176 | tf_op jit(solution)/shard_map/ppermute | solution.py:32
  9.5 1.9 %collective-permute-start.4 = (f32[64,128]{1,0:T(8,128)S(1)}, f32[64,128]{1,0:T(8,128)S(1)}, u32[]{:S(2)}, u32[]{:S(2)}) collective-permute-start(f32[64,128]{1,0:T(8,128)S(1)} %squares_add.3.refs_5_.refs_0_), channel_id=1, source_target_pairs={{0,8},{1,5},{2,10},{3,7},{4,12},{5,1},{6,14},{7,3},{8,0},{9,13},{1... | collective-permute-start | bytes 98312 | tf_op jit(solution)/shard_map/ppermute | solution.py:32
  11.7 7.3 %project.4 = (f32[2,128,1536]{2,1,0:T(8,128)S(1)}, bf16[2,128,1536]{2,1,0:T(8,128)(2,1)S(1)}) custom-call(bf16[256,2048]{1,0:T(8,128)(2,1)S(1)} %arrange.1.refs_0_.refs_3_, bf16[2048,6656]{1,0:T(8,128)(2,1)} %refs_1_.7, bf16[2048,6656]{1,0:T(8,128)(2,1)} %refs_2_.9, bf16[256,2048]{1,0:T(8,128)(2,1)S(1)} %arrange.1.refs_0_.refs_3_), custom_call_target="tpu_custom_call" | custom-call | flops 7500000256 | bytes 1024 | tf_op jit(solution)/shard_map/project/pallas_call | solution.py:59
  19.0 1.6 collective-permute-start.6
  20.5 2.7 %collective-permute-start.5 = (f32[64,128]{1,0:T(8,128)S(1)}, f32[64,128]{1,0:T(8,128)S(1)}, u32[]{:S(2)}, u32[]{:S(2)}) collective-permute-start(f32[64,128]{1,0:T(8,128)S(1)} %squares_add.4.refs_3_.refs_0_), channel_id=1, source_target_pairs={{0,16},{1,17},{2,18},{3,19},{4,20},{5,21},{6,22},{7,23},{8,24},{9,... | collective-permute-start | bytes 98312 | tf_op jit(solution)/shard_map/ppermute | solution.py:32
  23.2 7.1 %project.5 = (f32[2,128,1536]{2,1,0:T(8,128)S(1)}, bf16[2,128,1536]{2,1,0:T(8,128)(2,1)S(1)}) custom-call(bf16[256,2048]{1,0:T(8,128)(2,1)S(1)} %arrange.1.refs_0_.refs_3_, bf16[2048,6656]{1,0:T(8,128)(2,1)} %refs_1_.7, bf16[2048,6656]{1,0:T(8,128)(2,1)} %refs_2_.9, f32[64,128]{1,0:T(8,128)S(1)} %squares_add.4.refs_3_.refs_0_), custom_call_target="tpu_custom_call" | custom-call | flops 7500000256 | bytes 1024 | tf_op jit(solution)/shard_map/project/pallas_call | solution.py:59
  31.1 1.6 collective-permute-start.8
  32.7 2.4 %collective-permute-done.8.refs_6_ = f32[64,128]{1,0:T(8,128)S(1)} collective-permute-done((f32[64,128]{1,0:T(8,128)S(1)}, f32[64,128]{1,0:T(8,128)S(1)}, u32[]{:S(2)}, u32[]{:S(2)}) %collective-permute-start.8) | collective-permute-done | bytes 32800 | tf_op jit(solution)/shard_map/ppermute | solution.py:32
  35.1 1.5 collective-permute-start.10
  36.6 1.4 collective-permute-start.11
  38.3 8.7 %project.6 = (f32[2,128,2048]{2,1,0:T(8,128)S(1)}, bf16[2,128,2048]{2,1,0:T(8,128)(2,1)S(1)}) custom-call(bf16[256,2048]{1,0:T(8,128)(2,1)S(1)} %get-tuple-element.20.refs_0_.refs_3_, bf16[2048,6656]{1,0:T(8,128)(2,1)} %refs_1_.7, bf16[2048,6656]{1,0:T(8,128)(2,1)} %refs_2_.9, bf16[256,2048]{1,0:T(8,128)(2,1)S(1)} %get-tuple-element.20.refs_0_.refs_3_), custom_call_target="tpu_custom_call" | custom-call | flops 10000000000 | bytes 1024 | tf_op jit(solution)/shard_map/project/pallas_call | solution.py:59
  47.7 1.0 collective-permute-done.11.refs_2_
  48.7 2.7 %collective-permute-start.15 = (bf16[2,32,1536]{2,1,0:T(8,128)(2,1)S(1)}, bf16[2,32,1536]{2,1,0:T(8,128)(2,1)S(1)}, u32[]{:S(2)}, u32[]{:S(2)}) collective-permute-start(bf16[2,32,1536]{2,1,0:T(8,128)(2,1)S(1)} %add_up.9.refs_2_), channel_id=1, source_target_pairs={{0,16},{1,17},{2,18},{3,19},{4,20},{5,21},{6,22},{7,23},{8,24},{9,... | collective-permute-start | bytes 589832 | tf_op jit(solution)/shard_map/ppermute | solution.py:32
  51.4 1.5 collective-permute-start.14
  52.9 7.1 %project.7 = (f32[2,128,1536]{2,1,0:T(8,128)S(1)}, bf16[2,128,1536]{2,1,0:T(8,128)(2,1)S(1)}) custom-call(bf16[256,2048]{1,0:T(8,128)(2,1)S(1)} %get-tuple-element.20.refs_0_.refs_3_, bf16[2048,6656]{1,0:T(8,128)(2,1)} %refs_1_.7, bf16[2048,6656]{1,0:T(8,128)(2,1)} %refs_2_.9, bf16[2,64,1536]{2,1,0:T(8,128)(2,1)S(1)} %add_up.10.refs_3_), custom_call_target="tpu_custom_call" | custom-call | flops 7500000256 | bytes 1024 | tf_op jit(solution)/shard_map/project/pallas_call | solution.py:59
  60.0 1.4 collective-permute-start.12
  61.6 2.7 %collective-permute-start.18 = (bf16[32,1536]{1,0:T(8,128)(2,1)S(1)}, bf16[32,1536]{1,0:T(8,128)(2,1)S(1)}, u32[]{:S(2)}, u32[]{:S(2)}) collective-permute-start(bf16[32,1536]{1,0:T(8,128)(2,1)S(1)} %activate.4.refs_3_.refs_0_), channel_id=1, source_target_pairs={{0,16},{1,17},{2,18},{3,19},{4,20},{5,21},{6,22},{7,23},{8,24},{9,... | collective-permute-start | bytes 294920 | tf_op jit(solution)/shard_map/ppermute | solution.py:32
  64.2 0.9 collective-permute-done.14.refs_2_
  65.2 2.3 %collective-permute-start.17 = (bf16[2,32,1536]{2,1,0:T(8,128)(2,1)S(1)}, bf16[2,32,1536]{2,1,0:T(8,128)(2,1)S(1)}, u32[]{:S(2)}, u32[]{:S(2)}) collective-permute-start(bf16[2,32,1536]{2,1,0:T(8,128)(2,1)S(1)} %add_up.11.refs_2_), channel_id=1, source_target_pairs={{0,16},{1,17},{2,18},{3,19},{4,20},{5,21},{6,22},{7,23},{8,24},{9,... | collective-permute-start | bytes 589832 | tf_op jit(solution)/shard_map/ppermute | solution.py:32
  67.6 1.3 collective-permute-start.16
  68.9 1.5 collective-permute-start.22
  70.5 5.8 %collective-permute-done.17.refs_3_ = bf16[2,32,1536]{2,1,0:T(8,128)(2,1)S(1)} collective-permute-done((bf16[2,32,1536]{2,1,0:T(8,128)(2,1)S(1)}, bf16[2,32,1536]{2,1,0:T(8,128)(2,1)S(1)}, u32[]{:S(2)}, u32[]{:S(2)}) %collective-permute-start.17) | collective-permute-done | bytes 196640 | tf_op jit(solution)/shard_map/ppermute | solution.py:32
  76.5 10.9 %collective-permute-done.16.refs_2_ = bf16[2,64,2048]{2,1,0:T(8,128)(2,1)S(1)} collective-permute-done((bf16[2,64,2048]{2,1,0:T(8,128)(2,1)S(1)}, bf16[2,64,2048]{2,1,0:T(8,128)(2,1)S(1)}, u32[]{:S(2)}, u32[]{:S(2)}) %collective-permute-start.16) | collective-permute-done | bytes 524320 | tf_op jit(solution)/shard_map/ppermute | solution.py:32
  87.5 1.9 %collective-permute-start.20 = (bf16[2,32,2048]{2,1,0:T(8,128)(2,1)S(1)}, bf16[2,32,2048]{2,1,0:T(8,128)(2,1)S(1)}, u32[]{:S(2)}, u32[]{:S(2)}) collective-permute-start(bf16[2,32,2048]{2,1,0:T(8,128)(2,1)S(1)} %add_up.13.refs_2_), channel_id=1, source_target_pairs={{0,16},{1,17},{2,18},{3,19},{4,20},{5,21},{6,22},{7,23},{8,24},{9,... | collective-permute-start | bytes 786440 | tf_op jit(solution)/shard_map/ppermute | solution.py:32
  89.6 2.5 %collective-permute-start.19 = (bf16[2,64,1536]{2,1,0:T(8,128)(2,1)S(1)}, bf16[2,64,1536]{2,1,0:T(8,128)(2,1)S(1)}, u32[]{:S(2)}, u32[]{:S(2)}) collective-permute-start(bf16[2,64,1536]{2,1,0:T(8,128)(2,1)S(1)} %add_up.14.refs_2_), channel_id=1, source_target_pairs={{0,8},{1,5},{2,10},{3,7},{4,12},{5,1},{6,14},{7,3},{8,0},{9,13},{1... | collective-permute-start | bytes 1179656 | tf_op jit(solution)/shard_map/ppermute | solution.py:32
  92.3 1.2 collective-permute-start.25
  93.5 11.0 %collective-permute-done.20.refs_3_ = bf16[2,32,2048]{2,1,0:T(8,128)(2,1)S(1)} collective-permute-done((bf16[2,32,2048]{2,1,0:T(8,128)(2,1)S(1)}, bf16[2,32,2048]{2,1,0:T(8,128)(2,1)S(1)}, u32[]{:S(2)}, u32[]{:S(2)}) %collective-permute-start.20) | collective-permute-done | bytes 262176 | tf_op jit(solution)/shard_map/ppermute | solution.py:32
  104.8 3.0 %collective-permute-start.23 = (bf16[2,32,1536]{2,1,0:T(8,128)(2,1)S(1)}, bf16[2,32,1536]{2,1,0:T(8,128)(2,1)S(1)}, u32[]{:S(2)}, u32[]{:S(2)}) collective-permute-start(bf16[2,32,1536]{2,1,0:T(8,128)(2,1)S(1)} %add_up.15.refs_2_), channel_id=1, source_target_pairs={{0,16},{1,17},{2,18},{3,19},{4,20},{5,21},{6,22},{7,23},{8,24},{9,... | collective-permute-start | bytes 589832 | tf_op jit(solution)/shard_map/ppermute | solution.py:32
  107.8 1.1 collective-permute-start.29
  109.0 5.8 %collective-permute-done.24.refs_1_ = bf16[32,2048]{1,0:T(8,128)(2,1)S(1)} collective-permute-done((bf16[32,2048]{1,0:T(8,128)(2,1)S(1)}, bf16[32,2048]{1,0:T(8,128)(2,1)S(1)}, u32[]{:S(2)}, u32[]{:S(2)}) %collective-permute-start.24) | collective-permute-done | bytes 131104 | tf_op jit(solution)/shard_map/ppermute | solution.py:32
  114.8 1.4 collective-permute-start.27
  116.2 5.4 %collective-permute-done.23.refs_3_ = bf16[2,32,1536]{2,1,0:T(8,128)(2,1)S(1)} collective-permute-done((bf16[2,32,1536]{2,1,0:T(8,128)(2,1)S(1)}, bf16[2,32,1536]{2,1,0:T(8,128)(2,1)S(1)}, u32[]{:S(2)}, u32[]{:S(2)}) %collective-permute-start.23) | collective-permute-done | bytes 196640 | tf_op jit(solution)/shard_map/ppermute | solution.py:32
  121.8 1.8 %collective-permute-done.29.refs_3_ = bf16[128,1536]{1,0:T(8,128)(2,1)S(1)} collective-permute-done((bf16[128,1536]{1,0:T(8,128)(2,1)S(1)}, bf16[128,1536]{1,0:T(8,128)(2,1)S(1)}, u32[]{:S(2)}, u32[]{:S(2)}) %collective-permute-start.29) | collective-permute-done | bytes 393248 | tf_op jit(solution)/shard_map/ppermute | solution.py:32
  123.7 7.2 %down.3.refs_2_.refs_3_ = f32[256,2048]{1,0:T(8,128)S(1)} custom-call(bf16[128,1536]{1,0:T(8,128)(2,1)S(1)} %join.9.refs_2_.refs_0_, bf16[128,1536]{1,0:T(8,128)(2,1)S(1)} %collective-permute-done.28.refs_1_, bf16[128,1536]{1,0:T(8,128)(2,1)S(1)} %join.11.refs_2_, bf16[128,1536]{1,0:T(8,128)(2,1)S(1)} %collective-permute-done.29.refs_3_, ...), custom_call_target="tpu_custom_call" | custom-call | flops 6000000000 | bytes 1024 | tf_op jit(solution)/shard_map/down/pallas_call | solution.py:59
  130.9 1.6 collective-permute-start.30
  132.5 1.4 collective-permute-start.32
  133.9 4.4 %collective-permute-done.30.refs_1_ = bf16[64,1536]{1,0:T(8,128)(2,1)S(1)} collective-permute-done((bf16[64,1536]{1,0:T(8,128)(2,1)S(1)}, bf16[64,1536]{1,0:T(8,128)(2,1)S(1)}, u32[]{:S(2)}, u32[]{:S(2)}) %collective-permute-start.30) | collective-permute-done | bytes 196640 | tf_op jit(solution)/shard_map/ppermute | solution.py:32
  138.3 1.7 %collective-permute-start.31 = (bf16[128,1536]{1,0:T(8,128)(2,1)S(1)}, bf16[128,1536]{1,0:T(8,128)(2,1)S(1)}, u32[]{:S(2)}, u32[]{:S(2)}) collective-permute-start(bf16[128,1536]{1,0:T(8,128)(2,1)S(1)} %join.15.refs_4_.refs_0_), channel_id=1, source_target_pairs={{0,8},{1,5},{2,10},{3,7},{4,12},{5,1},{6,14},{7,3},{8,0},{9,13},{1... | collective-permute-start | bytes 1179656 | tf_op jit(solution)/shard_map/ppermute | solution.py:32
  140.0 1.7 %collective-permute-done.32.refs_1_ = bf16[128,2048]{1,0:T(8,128)(2,1)S(1)} collective-permute-done((bf16[128,2048]{1,0:T(8,128)(2,1)S(1)}, bf16[128,2048]{1,0:T(8,128)(2,1)S(1)}, u32[]{:S(2)}, u32[]{:S(2)}) %collective-permute-start.32) | collective-permute-done | bytes 524320 | tf_op jit(solution)/shard_map/ppermute | solution.py:32
  141.7 5.7 %down.4.refs_3_.refs_4_ = f32[256,2048]{1,0:T(8,128)S(1)} custom-call(bf16[128,2048]{1,0:T(8,128)(2,1)S(1)} %join.13.refs_2_.refs_0_, bf16[128,2048]{1,0:T(8,128)(2,1)S(1)} %collective-permute-done.32.refs_1_, bf16[6656,2048]{1,0:T(8,128)(2,1)} %refs_2_.11, f32[256,2048]{1,0:T(8,128)S(1)} %down.3.refs_2_.refs_3_, bf16[128,1536]{1,0:T(8,128)(2,1)S(1)} %join.15.refs_4_.refs_0_), custom_call_target="tpu_custom_call" | custom-call | flops 4000000000 | bytes 1024 | tf_op jit(solution)/shard_map/down/pallas_call | solution.py:59
  147.4 5.0 %down.5 = (f32[128,2048]{1,0:T(8,128)S(1)}, bf16[128,2048]{1,0:T(8,128)(2,1)S(1)}) custom-call(bf16[128,1536]{1,0:T(8,128)(2,1)S(1)} %join.15.refs_4_.refs_0_, bf16[128,1536]{1,0:T(8,128)(2,1)S(1)} %collective-permute-done.31.refs_1_, bf16[6656,2048]{1,0:T(8,128)(2,1)} %refs_2_.11, f32[256,2048]{1,0:T(8,128)S(1)} %down.4.refs_3_.refs_4_, ...), custom_call_target="tpu_custom_call" | custom-call | flops 3000000000 | bytes 1024 | tf_op jit(solution)/shard_map/down/pallas_call | solution.py:59
  153.2 1.5 collective-permute-done.33.refs_1_
  154.8 1.6 collective-permute-start.34
  156.4 7.1 %collective-permute-done.34.refs_2_ = bf16[64,2048]{1,0:T(8,128)(2,1)S(1)} collective-permute-done((bf16[64,2048]{1,0:T(8,128)(2,1)S(1)}, bf16[64,2048]{1,0:T(8,128)(2,1)S(1)}, u32[]{:S(2)}, u32[]{:S(2)}) %collective-permute-start.34) | collective-permute-done | bytes 262176 | tf_op jit(solution)/shard_map/ppermute | solution.py:32
  163.5 0.8 final.1
  (64 shorter events, 4.8 us)
Async XLA Ops:
  0.0 9.5 %collective-permute-start.1 = (bf16[64,2048]{1,0:T(8,128)(2,1)}, bf16[64,2048]{1,0:T(8,128)(2,1)S(1)}, u32[]{:S(2)}, u32[]{:S(2)}) collective-permute-start(bf16[64,2048]{1,0:T(8,128)(2,1)} %refs_0_.5), channel_id=1, source_target_pairs={{0,2},{1,3},{2,0},{3,1},{4,6},{5,7},{6,4},{7,5},{8,10},{9,11},{10,... | collective-permute-start | bytes 786440 | tf_op jit(solution)/shard_map/ppermute | solution.py:32
  3.0 8.4 %collective-permute-start = (bf16[64,2048]{1,0:T(8,128)(2,1)}, bf16[64,2048]{1,0:T(8,128)(2,1)S(1)}, u32[]{:S(2)}, u32[]{:S(2)}) collective-permute-start(bf16[64,2048]{1,0:T(8,128)(2,1)} %refs_0_.5), channel_id=1, source_target_pairs={{0,1},{1,0},{2,3},{3,2},{4,5},{5,4},{6,7},{7,6},{8,9},{9,8},{10,11... | collective-permute-start | bytes 786440 | tf_op jit(solution)/shard_map/ppermute | solution.py:32
  3.0 1.0 copy-start
  4.1 5.4 %collective-permute-start.3 = (f32[64,128]{1,0:T(8,128)S(1)}, f32[64,128]{1,0:T(8,128)S(1)}, u32[]{:S(2)}, u32[]{:S(2)}) collective-permute-start(f32[64,128]{1,0:T(8,128)S(1)} %squares.1.refs_1_.refs_0_), channel_id=1, source_target_pairs={{0,4},{1,9},{2,6},{3,11},{4,0},{5,13},{6,2},{7,15},{8,12},{9,1},{1... | collective-permute-start | bytes 98312 | tf_op jit(solution)/shard_map/ppermute | solution.py:32
  9.5 1.9 %copy-start.1 = (bf16[64,2048]{1,0:T(8,128)(2,1)S(1)}, bf16[64,2048]{1,0:T(8,128)(2,1)}, u32[]{:S(2)}) copy-start(bf16[64,2048]{1,0:T(8,128)(2,1)} %refs_0_.5) | copy-start | bytes 786436
  9.5 1.9 %copy-start.2 = (f32[2048]{0:T(1024)S(1)}, f32[2048]{0:T(1024)}, u32[]{:S(2)}) copy-start(f32[2048]{0:T(1024)} %param.6) | copy-start | bytes 24580
  9.5 1.9 %collective-permute-start.2 = (bf16[64,2048]{1,0:T(8,128)(2,1)S(1)}, bf16[64,2048]{1,0:T(8,128)(2,1)S(1)}, u32[]{:S(2)}, u32[]{:S(2)}) collective-permute-start(bf16[64,2048]{1,0:T(8,128)(2,1)S(1)} %pass.1.refs_2_), channel_id=1, source_target_pairs={{0,1},{1,0},{2,3},{3,2},{4,5},{5,4},{6,7},{7,6},{8,9},{9,8},{10,11... | collective-permute-start | bytes 786440 | tf_op jit(solution)/shard_map/ppermute | solution.py:32
  9.5 11.0 %collective-permute-start.4 = (f32[64,128]{1,0:T(8,128)S(1)}, f32[64,128]{1,0:T(8,128)S(1)}, u32[]{:S(2)}, u32[]{:S(2)}) collective-permute-start(f32[64,128]{1,0:T(8,128)S(1)} %squares_add.3.refs_5_.refs_0_), channel_id=1, source_target_pairs={{0,8},{1,5},{2,10},{3,7},{4,12},{5,1},{6,14},{7,3},{8,0},{9,13},{1... | collective-permute-start | bytes 98312 | tf_op jit(solution)/shard_map/ppermute | solution.py:32
  19.0 12.1 %collective-permute-start.6 = (bf16[2,128,1536]{2,1,0:T(8,128)(2,1)S(1)}, bf16[2,128,1536]{2,1,0:T(8,128)(2,1)S(1)}, u32[]{:S(2)}, u32[]{:S(2)}) collective-permute-start(bf16[2,128,1536]{2,1,0:T(8,128)(2,1)S(1)} %get-tuple-element.18), channel_id=1, source_target_pairs={{0,4},{1,9},{2,6},{3,11},{4,0},{5,13},{6,2},{7,15},{8,12},{9,1},{1... | collective-permute-start | bytes 2359304 | tf_op jit(solution)/shard_map/ppermute | solution.py:32
  20.5 10.6 %collective-permute-start.5 = (f32[64,128]{1,0:T(8,128)S(1)}, f32[64,128]{1,0:T(8,128)S(1)}, u32[]{:S(2)}, u32[]{:S(2)}) collective-permute-start(f32[64,128]{1,0:T(8,128)S(1)} %squares_add.4.refs_3_.refs_0_), channel_id=1, source_target_pairs={{0,16},{1,17},{2,18},{3,19},{4,20},{5,21},{6,22},{7,23},{8,24},{9,... | collective-permute-start | bytes 98312 | tf_op jit(solution)/shard_map/ppermute | solution.py:32
  31.1 4.0 %collective-permute-start.8 = (f32[64,128]{1,0:T(8,128)S(1)}, f32[64,128]{1,0:T(8,128)S(1)}, u32[]{:S(2)}, u32[]{:S(2)}) collective-permute-start(f32[64,128]{1,0:T(8,128)S(1)} %squares_add.5.refs_4_.refs_9_), channel_id=1, source_target_pairs={{0,2},{1,3},{2,0},{3,1},{4,6},{5,7},{6,4},{7,5},{8,10},{9,11},{10,... | collective-permute-start | bytes 98312 | tf_op jit(solution)/shard_map/ppermute | solution.py:32
  32.7 5.3 %collective-permute-start.7 = (f32[64,128]{1,0:T(8,128)S(1)}, f32[64,128]{1,0:T(8,128)S(1)}, u32[]{:S(2)}, u32[]{:S(2)}) collective-permute-start(f32[64,128]{1,0:T(8,128)S(1)} %squares_add.5.refs_4_.refs_9_), channel_id=1, source_target_pairs={{0,1},{1,0},{2,3},{3,2},{4,5},{5,4},{6,7},{7,6},{8,9},{9,8},{10,11... | collective-permute-start | bytes 98312 | tf_op jit(solution)/shard_map/ppermute | solution.py:32
  35.1 2.9 %collective-permute-start.9 = (f32[64,128]{1,0:T(8,128)S(1)}, f32[64,128]{1,0:T(8,128)S(1)}, u32[]{:S(2)}, u32[]{:S(2)}) collective-permute-start(f32[64,128]{1,0:T(8,128)S(1)} %collective-permute-done.8.refs_6_), channel_id=1, source_target_pairs={{0,1},{1,0},{2,3},{3,2},{4,5},{5,4},{6,7},{7,6},{8,9},{9,8},{10,11... | collective-permute-start | bytes 98312 | tf_op jit(solution)/shard_map/ppermute | solution.py:32
  35.1 16.3 %collective-permute-start.10 = (bf16[2,128,1536]{2,1,0:T(8,128)(2,1)S(1)}, bf16[2,128,1536]{2,1,0:T(8,128)(2,1)S(1)}, u32[]{:S(2)}, u32[]{:S(2)}) collective-permute-start(bf16[2,128,1536]{2,1,0:T(8,128)(2,1)S(1)} %get-tuple-element.21), channel_id=1, source_target_pairs={{0,4},{1,9},{2,6},{3,11},{4,0},{5,13},{6,2},{7,15},{8,12},{9,1},{1... | collective-permute-start | bytes 2359304 | tf_op jit(solution)/shard_map/ppermute | solution.py:32
  36.6 12.1 %collective-permute-start.11 = (bf16[2,64,1536]{2,1,0:T(8,128)(2,1)S(1)}, bf16[2,64,1536]{2,1,0:T(8,128)(2,1)S(1)}, u32[]{:S(2)}, u32[]{:S(2)}) collective-permute-start(bf16[2,64,1536]{2,1,0:T(8,128)(2,1)S(1)} %add_up.8.refs_2_), channel_id=1, source_target_pairs={{0,8},{1,5},{2,10},{3,7},{4,12},{5,1},{6,14},{7,3},{8,0},{9,13},{1... | collective-permute-start | bytes 1179656 | tf_op jit(solution)/shard_map/ppermute | solution.py:32
  47.0 20.5 %collective-permute-start.13 = (bf16[2,128,2048]{2,1,0:T(8,128)(2,1)S(1)}, bf16[2,128,2048]{2,1,0:T(8,128)(2,1)S(1)}, u32[]{:S(2)}, u32[]{:S(2)}) collective-permute-start(bf16[2,128,2048]{2,1,0:T(8,128)(2,1)S(1)} %get-tuple-element.25), channel_id=1, source_target_pairs={{0,4},{1,9},{2,6},{3,11},{4,0},{5,13},{6,2},{7,15},{8,12},{9,1},{1... | collective-permute-start | bytes 3145736 | tf_op jit(solution)/shard_map/ppermute | solution.py:32
  48.7 12.7 %collective-permute-start.15 = (bf16[2,32,1536]{2,1,0:T(8,128)(2,1)S(1)}, bf16[2,32,1536]{2,1,0:T(8,128)(2,1)S(1)}, u32[]{:S(2)}, u32[]{:S(2)}) collective-permute-start(bf16[2,32,1536]{2,1,0:T(8,128)(2,1)S(1)} %add_up.9.refs_2_), channel_id=1, source_target_pairs={{0,16},{1,17},{2,18},{3,19},{4,20},{5,21},{6,22},{7,23},{8,24},{9,... | collective-permute-start | bytes 589832 | tf_op jit(solution)/shard_map/ppermute | solution.py:32
  51.4 13.7 %collective-permute-start.14 = (bf16[2,64,1536]{2,1,0:T(8,128)(2,1)S(1)}, bf16[2,64,1536]{2,1,0:T(8,128)(2,1)S(1)}, u32[]{:S(2)}, u32[]{:S(2)}) collective-permute-start(bf16[2,64,1536]{2,1,0:T(8,128)(2,1)S(1)} %add_up.10.refs_3_), channel_id=1, source_target_pairs={{0,8},{1,5},{2,10},{3,7},{4,12},{5,1},{6,14},{7,3},{8,0},{9,13},{1... | collective-permute-start | bytes 1179656 | tf_op jit(solution)/shard_map/ppermute | solution.py:32
  60.0 29.5 %collective-permute-start.12 = (bf16[2,128,1536]{2,1,0:T(8,128)(2,1)S(1)}, bf16[2,128,1536]{2,1,0:T(8,128)(2,1)S(1)}, u32[]{:S(2)}, u32[]{:S(2)}) collective-permute-start(bf16[2,128,1536]{2,1,0:T(8,128)(2,1)S(1)} %get-tuple-element.24), channel_id=1, source_target_pairs={{0,4},{1,9},{2,6},{3,11},{4,0},{5,13},{6,2},{7,15},{8,12},{9,1},{1... | collective-permute-start | bytes 2359304 | tf_op jit(solution)/shard_map/ppermute | solution.py:32
  61.6 7.3 %collective-permute-start.18 = (bf16[32,1536]{1,0:T(8,128)(2,1)S(1)}, bf16[32,1536]{1,0:T(8,128)(2,1)S(1)}, u32[]{:S(2)}, u32[]{:S(2)}) collective-permute-start(bf16[32,1536]{1,0:T(8,128)(2,1)S(1)} %activate.4.refs_3_.refs_0_), channel_id=1, source_target_pairs={{0,16},{1,17},{2,18},{3,19},{4,20},{5,21},{6,22},{7,23},{8,24},{9,... | collective-permute-start | bytes 294920 | tf_op jit(solution)/shard_map/ppermute | solution.py:32
  65.2 11.0 %collective-permute-start.17 = (bf16[2,32,1536]{2,1,0:T(8,128)(2,1)S(1)}, bf16[2,32,1536]{2,1,0:T(8,128)(2,1)S(1)}, u32[]{:S(2)}, u32[]{:S(2)}) collective-permute-start(bf16[2,32,1536]{2,1,0:T(8,128)(2,1)S(1)} %add_up.11.refs_2_), channel_id=1, source_target_pairs={{0,16},{1,17},{2,18},{3,19},{4,20},{5,21},{6,22},{7,23},{8,24},{9,... | collective-permute-start | bytes 589832 | tf_op jit(solution)/shard_map/ppermute | solution.py:32
  67.6 19.9 %collective-permute-start.16 = (bf16[2,64,2048]{2,1,0:T(8,128)(2,1)S(1)}, bf16[2,64,2048]{2,1,0:T(8,128)(2,1)S(1)}, u32[]{:S(2)}, u32[]{:S(2)}) collective-permute-start(bf16[2,64,2048]{2,1,0:T(8,128)(2,1)S(1)} %add_up.12.refs_2_), channel_id=1, source_target_pairs={{0,8},{1,5},{2,10},{3,7},{4,12},{5,1},{6,14},{7,3},{8,0},{9,13},{1... | collective-permute-start | bytes 1572872 | tf_op jit(solution)/shard_map/ppermute | solution.py:32
  68.9 23.2 %collective-permute-start.22 = (bf16[64,1536]{1,0:T(8,128)(2,1)S(1)}, bf16[64,1536]{1,0:T(8,128)(2,1)S(1)}, u32[]{:S(2)}, u32[]{:S(2)}) collective-permute-start(bf16[64,1536]{1,0:T(8,128)(2,1)S(1)} %join.8.refs_5_.refs_0_), channel_id=1, source_target_pairs={{0,4},{1,9},{2,6},{3,11},{4,0},{5,13},{6,2},{7,15},{8,12},{9,1},{1... | collective-permute-start | bytes 589832 | tf_op jit(solution)/shard_map/ppermute | solution.py:32
  76.4 15.8 %collective-permute-start.21 = (bf16[32,1536]{1,0:T(8,128)(2,1)S(1)}, bf16[32,1536]{1,0:T(8,128)(2,1)S(1)}, u32[]{:S(2)}, u32[]{:S(2)}) collective-permute-start(bf16[32,1536]{1,0:T(8,128)(2,1)S(1)} %activate.5.refs_3_.refs_0_), channel_id=1, source_target_pairs={{0,16},{1,17},{2,18},{3,19},{4,20},{5,21},{6,22},{7,23},{8,24},{9,... | collective-permute-start | bytes 294920 | tf_op jit(solution)/shard_map/ppermute | solution.py:32
  87.5 16.9 %collective-permute-start.20 = (bf16[2,32,2048]{2,1,0:T(8,128)(2,1)S(1)}, bf16[2,32,2048]{2,1,0:T(8,128)(2,1)S(1)}, u32[]{:S(2)}, u32[]{:S(2)}) collective-permute-start(bf16[2,32,2048]{2,1,0:T(8,128)(2,1)S(1)} %add_up.13.refs_2_), channel_id=1, source_target_pairs={{0,16},{1,17},{2,18},{3,19},{4,20},{5,21},{6,22},{7,23},{8,24},{9,... | collective-permute-start | bytes 786440 | tf_op jit(solution)/shard_map/ppermute | solution.py:32
  89.6 15.2 %collective-permute-start.19 = (bf16[2,64,1536]{2,1,0:T(8,128)(2,1)S(1)}, bf16[2,64,1536]{2,1,0:T(8,128)(2,1)S(1)}, u32[]{:S(2)}, u32[]{:S(2)}) collective-permute-start(bf16[2,64,1536]{2,1,0:T(8,128)(2,1)S(1)} %add_up.14.refs_2_), channel_id=1, source_target_pairs={{0,8},{1,5},{2,10},{3,7},{4,12},{5,1},{6,14},{7,3},{8,0},{9,13},{1... | collective-permute-start | bytes 1179656 | tf_op jit(solution)/shard_map/ppermute | solution.py:32
  92.1 29.7 %collective-permute-start.28 = (bf16[128,1536]{1,0:T(8,128)(2,1)S(1)}, bf16[128,1536]{1,0:T(8,128)(2,1)S(1)}, u32[]{:S(2)}, u32[]{:S(2)}) collective-permute-start(bf16[128,1536]{1,0:T(8,128)(2,1)S(1)} %join.9.refs_2_.refs_0_), channel_id=1, source_target_pairs={{0,8},{1,5},{2,10},{3,7},{4,12},{5,1},{6,14},{7,3},{8,0},{9,13},{1... | collective-permute-start | bytes 1179656 | tf_op jit(solution)/shard_map/ppermute | solution.py:32
  92.3 15.5 %collective-permute-start.25 = (bf16[64,1536]{1,0:T(8,128)(2,1)S(1)}, bf16[64,1536]{1,0:T(8,128)(2,1)S(1)}, u32[]{:S(2)}, u32[]{:S(2)}) collective-permute-start(bf16[64,1536]{1,0:T(8,128)(2,1)S(1)} %join.10.refs_5_.refs_0_), channel_id=1, source_target_pairs={{0,4},{1,9},{2,6},{3,11},{4,0},{5,13},{6,2},{7,15},{8,12},{9,1},{1... | collective-permute-start | bytes 589832 | tf_op jit(solution)/shard_map/ppermute | solution.py:32
  104.7 10.1 %collective-permute-start.24 = (bf16[32,2048]{1,0:T(8,128)(2,1)S(1)}, bf16[32,2048]{1,0:T(8,128)(2,1)S(1)}, u32[]{:S(2)}, u32[]{:S(2)}) collective-permute-start(bf16[32,2048]{1,0:T(8,128)(2,1)S(1)} %activate.6.refs_3_.refs_0_), channel_id=1, source_target_pairs={{0,16},{1,17},{2,18},{3,19},{4,20},{5,21},{6,22},{7,23},{8,24},{9,... | collective-permute-start | bytes 393224 | tf_op jit(solution)/shard_map/ppermute | solution.py:32
  104.8 16.8 %collective-permute-start.23 = (bf16[2,32,1536]{2,1,0:T(8,128)(2,1)S(1)}, bf16[2,32,1536]{2,1,0:T(8,128)(2,1)S(1)}, u32[]{:S(2)}, u32[]{:S(2)}) collective-permute-start(bf16[2,32,1536]{2,1,0:T(8,128)(2,1)S(1)} %add_up.15.refs_2_), channel_id=1, source_target_pairs={{0,16},{1,17},{2,18},{3,19},{4,20},{5,21},{6,22},{7,23},{8,24},{9,... | collective-permute-start | bytes 589832 | tf_op jit(solution)/shard_map/ppermute | solution.py:32
  107.8 15.8 %collective-permute-start.29 = (bf16[128,1536]{1,0:T(8,128)(2,1)S(1)}, bf16[128,1536]{1,0:T(8,128)(2,1)S(1)}, u32[]{:S(2)}, u32[]{:S(2)}) collective-permute-start(bf16[128,1536]{1,0:T(8,128)(2,1)S(1)} %join.11.refs_2_), channel_id=1, source_target_pairs={{0,8},{1,5},{2,10},{3,7},{4,12},{5,1},{6,14},{7,3},{8,0},{9,13},{1... | collective-permute-start | bytes 1179656 | tf_op jit(solution)/shard_map/ppermute | solution.py:32
  114.8 16.1 %collective-permute-start.27 = (bf16[64,2048]{1,0:T(8,128)(2,1)S(1)}, bf16[64,2048]{1,0:T(8,128)(2,1)S(1)}, u32[]{:S(2)}, u32[]{:S(2)}) collective-permute-start(bf16[64,2048]{1,0:T(8,128)(2,1)S(1)} %join.12.refs_5_.refs_0_), channel_id=1, source_target_pairs={{0,4},{1,9},{2,6},{3,11},{4,0},{5,13},{6,2},{7,15},{8,12},{9,1},{1... | collective-permute-start | bytes 786440 | tf_op jit(solution)/shard_map/ppermute | solution.py:32
  121.7 9.2 %collective-permute-start.26 = (bf16[32,1536]{1,0:T(8,128)(2,1)S(1)}, bf16[32,1536]{1,0:T(8,128)(2,1)S(1)}, u32[]{:S(2)}, u32[]{:S(2)}) collective-permute-start(bf16[32,1536]{1,0:T(8,128)(2,1)S(1)} %activate.7.refs_5_.refs_0_), channel_id=1, source_target_pairs={{0,16},{1,17},{2,18},{3,19},{4,20},{5,21},{6,22},{7,23},{8,24},{9,... | collective-permute-start | bytes 294920 | tf_op jit(solution)/shard_map/ppermute | solution.py:32
  130.9 7.4 %collective-permute-start.30 = (bf16[64,1536]{1,0:T(8,128)(2,1)S(1)}, bf16[64,1536]{1,0:T(8,128)(2,1)S(1)}, u32[]{:S(2)}, u32[]{:S(2)}) collective-permute-start(bf16[64,1536]{1,0:T(8,128)(2,1)S(1)} %join.14.refs_0_.refs_2_), channel_id=1, source_target_pairs={{0,4},{1,9},{2,6},{3,11},{4,0},{5,13},{6,2},{7,15},{8,12},{9,1},{1... | collective-permute-start | bytes 589832 | tf_op jit(solution)/shard_map/ppermute | solution.py:32
  132.5 9.2 %collective-permute-start.32 = (bf16[128,2048]{1,0:T(8,128)(2,1)S(1)}, bf16[128,2048]{1,0:T(8,128)(2,1)S(1)}, u32[]{:S(2)}, u32[]{:S(2)}) collective-permute-start(bf16[128,2048]{1,0:T(8,128)(2,1)S(1)} %join.13.refs_2_.refs_0_), channel_id=1, source_target_pairs={{0,8},{1,5},{2,10},{3,7},{4,12},{5,1},{6,14},{7,3},{8,0},{9,13},{1... | collective-permute-start | bytes 1572872 | tf_op jit(solution)/shard_map/ppermute | solution.py:32
  138.3 9.1 %collective-permute-start.31 = (bf16[128,1536]{1,0:T(8,128)(2,1)S(1)}, bf16[128,1536]{1,0:T(8,128)(2,1)S(1)}, u32[]{:S(2)}, u32[]{:S(2)}) collective-permute-start(bf16[128,1536]{1,0:T(8,128)(2,1)S(1)} %join.15.refs_4_.refs_0_), channel_id=1, source_target_pairs={{0,8},{1,5},{2,10},{3,7},{4,12},{5,1},{6,14},{7,3},{8,0},{9,13},{1... | collective-permute-start | bytes 1179656 | tf_op jit(solution)/shard_map/ppermute | solution.py:32
  152.4 2.3 %collective-permute-start.33 = (bf16[128,2048]{1,0:T(8,128)(2,1)S(1)}, bf16[128,2048]{1,0:T(8,128)(2,1)S(1)}, u32[]{:S(2)}, u32[]{:S(2)}) collective-permute-start(bf16[128,2048]{1,0:T(8,128)(2,1)S(1)} %get-tuple-element.28), channel_id=1, source_target_pairs={{0,1},{1,0},{2,3},{3,2},{4,5},{5,4},{6,7},{7,6},{8,9},{9,8},{10,11... | collective-permute-start | bytes 1572872 | tf_op jit(solution)/shard_map/ppermute | solution.py:32
  154.8 8.7 %collective-permute-start.34 = (bf16[64,2048]{1,0:T(8,128)(2,1)S(1)}, bf16[64,2048]{1,0:T(8,128)(2,1)S(1)}, u32[]{:S(2)}, u32[]{:S(2)}) collective-permute-start(bf16[64,2048]{1,0:T(8,128)(2,1)S(1)} %send_y.1.refs_3_), channel_id=1, source_target_pairs={{0,2},{1,3},{2,0},{3,1},{4,6},{5,7},{6,4},{7,5},{8,10},{9,11},{10,... | collective-permute-start | bytes 786440 | tf_op jit(solution)/shard_map/ppermute | solution.py:32

commit v4 on v3

--- a/solution.py
+++ b/solution.py
@@ -26,6 +26,7 @@
 THIRD = swaps((Z_HIGH, Z_HIGH))
 CORE_SWAP = swaps(ha_flip=1)
 Y_SWAP = swaps(ha_flip=2)
+BOTH_SWAP = swaps(ha_flip=3)
 
 
 def swap(a, pairs):
@@ -213,7 +214,7 @@
 
 
 SHARES = (6, 6, 8, 6,)
-SUM, GATHER = "mmmm", "nnnn"
+SUM, GATHER = "mmmm", "nnmm"
 GROUPS = ((0, 1,), (2,), (3,),)
 ORDER = (
     "m0", "s", "m1", "a0", "q", "n", "m2", "b0", "a1", "m3", "c0", "b1",
@@ -256,7 +257,7 @@
         (s0,) = chain.call(add_kernel, squares, [sq_shape], name="squares_add")
         s2 = swap(s0, Y_SWAP)
         s1 = swap(s0, CORE_SWAP)
-        env["s"] = (s0, s1, s2, swap(s2, CORE_SWAP))
+        env["s"] = (s0, s1, s2, swap(s0, BOTH_SWAP))
 
     def stage_n(k):
         env["lhs"], env["r"] = chain.call(
@@ -337,7 +338,7 @@
         group = GROUPS[k]
         first, last = k == 0, k == len(GROUPS) - 1
         at, n = cuts[group[0]], cuts[group[-1] + 1] - cuts[group[0]]
-        cols = 512
+        cols = 1024
         args, in_specs = [], []
         for j in group:
             args += [state[j]["h"], state[j]["got"]]

time: 164 us -> 160 us (0.976)
  waiting for transfers between devices: 64.3 us -> 59.8 us
  starting transfers between devices: 47.6 us -> 50.1 us
  Pallas kernels: 51 us -> 48.8 us
    ppermute x35, waiting for transfers between devices: 64.3 us -> 59.8 us  [swap(): return lax.ppermute(a, AXES, pairs)]
    ppermute x35, starting transfers between devices: 47.6 us -> 50.1 us  [swap(): return lax.ppermute(a, AXES, pairs)]
    pallas_call x36, Pallas kernels: 51 us -> 48.8 us  [call(): pl.pallas_call(run, out_shape=tuple(out_shape), grid=grid, in_specs=in_sp...]
  transfers between devices with their start and end apart: 35 -> 35, of which waited for: 15 -> 15; matrix products, arithmetic and copies ran while one was open for 0% -> 0% of each run, Pallas kernels for 28% -> 27%
where the time goes in v4:
time: 160 us
  waiting for transfers between devices  59.8 us (37%)
  starting transfers between devices  50.1 us (31%)
  Pallas kernels  48.8 us (30%)
    ppermute x35, waiting for transfers between devices, swap(): return lax.ppermute(a, AXES, pairs)  59.8 us
    ppermute x35, starting transfers between devices, swap(): return lax.ppermute(a, AXES, pairs)  50.1 us
    pallas_call x36, Pallas kernels, call(): pl.pallas_call(run, out_shape=tuple(out_shape), grid=grid, in_specs=in_sp...  48.8 us
  transfers between devices with their start and end apart: 35, of which 15 were waited for; matrix products, arithmetic and copies ran while one was open for 0% of the time, Pallas kernels for 27%

profile of v4, /device:TPU:0, one launch (start us, length us, event | category | flops | bytes accessed | tf_op | source)
XLA Modules:
  0.0 160.0 jit_solution(12906739674023382165)
XLA Ops:
  0.0 3.0 %collective-permute-start.1 = (bf16[64,2048]{1,0:T(8,128)(2,1)}, bf16[64,2048]{1,0:T(8,128)(2,1)S(1)}, u32[]{:S(2)}, u32[]{:S(2)}) collective-permute-start(bf16[64,2048]{1,0:T(8,128)(2,1)} %refs_0_.5), channel_id=1, source_target_pairs={{0,2},{1,3},{2,0},{3,1},{4,6},{5,7},{6,4},{7,5},{8,10},{9,11},{10,... | collective-permute-start | bytes 786440 | tf_op jit(solution)/shard_map/ppermute | solution.py:33
  3.0 1.0 copy-done
  4.1 1.5 collective-permute-start.3
  5.6 3.9 %collective-permute-done.1.refs_0_ = bf16[64,2048]{1,0:T(8,128)(2,1)S(1)} collective-permute-done((bf16[64,2048]{1,0:T(8,128)(2,1)}, bf16[64,2048]{1,0:T(8,128)(2,1)S(1)}, u32[]{:S(2)}, u32[]{:S(2)}) %collective-permute-start.1) | collective-permute-done | bytes 262176 | tf_op jit(solution)/shard_map/ppermute | solution.py:33
  9.5 1.9 %collective-permute-start.4 = (f32[64,128]{1,0:T(8,128)S(1)}, f32[64,128]{1,0:T(8,128)S(1)}, u32[]{:S(2)}, u32[]{:S(2)}) collective-permute-start(f32[64,128]{1,0:T(8,128)S(1)} %squares_add.3.refs_5_.refs_0_), channel_id=1, source_target_pairs={{0,8},{1,5},{2,10},{3,7},{4,12},{5,1},{6,14},{7,3},{8,0},{9,13},{1... | collective-permute-start | bytes 98312 | tf_op jit(solution)/shard_map/ppermute | solution.py:33
  11.7 7.3 %project.4 = (f32[2,128,1536]{2,1,0:T(8,128)S(1)}, bf16[2,128,1536]{2,1,0:T(8,128)(2,1)S(1)}) custom-call(bf16[256,2048]{1,0:T(8,128)(2,1)S(1)} %arrange.1.refs_0_.refs_3_, bf16[2048,6656]{1,0:T(8,128)(2,1)} %refs_1_.7, bf16[2048,6656]{1,0:T(8,128)(2,1)} %refs_2_.9, bf16[256,2048]{1,0:T(8,128)(2,1)S(1)} %arrange.1.refs_0_.refs_3_), custom_call_target="tpu_custom_call" | custom-call | flops 7500000256 | bytes 1024 | tf_op jit(solution)/shard_map/project/pallas_call | solution.py:60
  19.0 1.6 collective-permute-start.6
  20.5 2.7 %collective-permute-start.5 = (f32[64,128]{1,0:T(8,128)S(1)}, f32[64,128]{1,0:T(8,128)S(1)}, u32[]{:S(2)}, u32[]{:S(2)}) collective-permute-start(f32[64,128]{1,0:T(8,128)S(1)} %squares_add.4.refs_3_.refs_0_), channel_id=1, source_target_pairs={{0,16},{1,17},{2,18},{3,19},{4,20},{5,21},{6,22},{7,23},{8,24},{9,... | collective-permute-start | bytes 98312 | tf_op jit(solution)/shard_map/ppermute | solution.py:33
  23.2 7.1 %project.5 = (f32[2,128,1536]{2,1,0:T(8,128)S(1)}, bf16[2,128,1536]{2,1,0:T(8,128)(2,1)S(1)}) custom-call(bf16[256,2048]{1,0:T(8,128)(2,1)S(1)} %arrange.1.refs_0_.refs_3_, bf16[2048,6656]{1,0:T(8,128)(2,1)} %refs_1_.7, bf16[2048,6656]{1,0:T(8,128)(2,1)} %refs_2_.9, f32[64,128]{1,0:T(8,128)S(1)} %squares_add.4.refs_3_.refs_0_), custom_call_target="tpu_custom_call" | custom-call | flops 7500000256 | bytes 1024 | tf_op jit(solution)/shard_map/project/pallas_call | solution.py:60
  30.3 0.7 collective-permute-done.6.refs_1_
  31.2 1.6 collective-permute-start.8
  33.1 1.5 collective-permute-start.10
  34.5 1.6 %collective-permute-start.11 = (bf16[2,64,1536]{2,1,0:T(8,128)(2,1)S(1)}, bf16[2,64,1536]{2,1,0:T(8,128)(2,1)S(1)}, u32[]{:S(2)}, u32[]{:S(2)}) collective-permute-start(bf16[2,64,1536]{2,1,0:T(8,128)(2,1)S(1)} %add_up.8.refs_2_), channel_id=1, source_target_pairs={{0,8},{1,5},{2,10},{3,7},{4,12},{5,1},{6,14},{7,3},{8,0},{9,13},{1... | collective-permute-start | bytes 1179656 | tf_op jit(solution)/shard_map/ppermute | solution.py:33
  36.5 8.7 %project.6 = (f32[2,128,2048]{2,1,0:T(8,128)S(1)}, bf16[2,128,2048]{2,1,0:T(8,128)(2,1)S(1)}) custom-call(bf16[256,2048]{1,0:T(8,128)(2,1)S(1)} %get-tuple-element.20.refs_0_.refs_3_, bf16[2048,6656]{1,0:T(8,128)(2,1)} %refs_1_.7, bf16[2048,6656]{1,0:T(8,128)(2,1)} %refs_2_.9, bf16[256,2048]{1,0:T(8,128)(2,1)S(1)} %get-tuple-element.20.refs_0_.refs_3_), custom_call_target="tpu_custom_call" | custom-call | flops 10000000000 | bytes 1024 | tf_op jit(solution)/shard_map/project/pallas_call | solution.py:60
  45.2 1.5 collective-permute-start.13
  46.7 2.7 %collective-permute-start.15 = (bf16[2,32,1536]{2,1,0:T(8,128)(2,1)S(1)}, bf16[2,32,1536]{2,1,0:T(8,128)(2,1)S(1)}, u32[]{:S(2)}, u32[]{:S(2)}) collective-permute-start(bf16[2,32,1536]{2,1,0:T(8,128)(2,1)S(1)} %add_up.9.refs_2_), channel_id=1, source_target_pairs={{0,16},{1,17},{2,18},{3,19},{4,20},{5,21},{6,22},{7,23},{8,24},{9,... | collective-permute-start | bytes 589832 | tf_op jit(solution)/shard_map/ppermute | solution.py:33
  49.5 1.5 collective-permute-start.14
  51.0 7.1 %project.7 = (f32[2,128,1536]{2,1,0:T(8,128)S(1)}, bf16[2,128,1536]{2,1,0:T(8,128)(2,1)S(1)}) custom-call(bf16[256,2048]{1,0:T(8,128)(2,1)S(1)} %get-tuple-element.20.refs_0_.refs_3_, bf16[2048,6656]{1,0:T(8,128)(2,1)} %refs_1_.7, bf16[2048,6656]{1,0:T(8,128)(2,1)} %refs_2_.9, bf16[2,64,1536]{2,1,0:T(8,128)(2,1)S(1)} %add_up.10.refs_3_), custom_call_target="tpu_custom_call" | custom-call | flops 7500000256 | bytes 1024 | tf_op jit(solution)/shard_map/project/pallas_call | solution.py:60
  58.1 1.3 collective-permute-start.12
  59.5 2.5 %collective-permute-start.18 = (bf16[32,1536]{1,0:T(8,128)(2,1)S(1)}, bf16[32,1536]{1,0:T(8,128)(2,1)S(1)}, u32[]{:S(2)}, u32[]{:S(2)}) collective-permute-start(bf16[32,1536]{1,0:T(8,128)(2,1)S(1)} %activate.4.refs_3_.refs_0_), channel_id=1, source_target_pairs={{0,16},{1,17},{2,18},{3,19},{4,20},{5,21},{6,22},{7,23},{8,24},{9,... | collective-permute-start | bytes 294920 | tf_op jit(solution)/shard_map/ppermute | solution.py:33
  62.0 1.8 %collective-permute-done.14.refs_2_ = bf16[2,64,1536]{2,1,0:T(8,128)(2,1)S(1)} collective-permute-done((bf16[2,64,1536]{2,1,0:T(8,128)(2,1)S(1)}, bf16[2,64,1536]{2,1,0:T(8,128)(2,1)S(1)}, u32[]{:S(2)}, u32[]{:S(2)}) %collective-permute-start.14) | collective-permute-done | bytes 393248 | tf_op jit(solution)/shard_map/ppermute | solution.py:33
  63.8 2.5 %collective-permute-start.17 = (bf16[2,32,1536]{2,1,0:T(8,128)(2,1)S(1)}, bf16[2,32,1536]{2,1,0:T(8,128)(2,1)S(1)}, u32[]{:S(2)}, u32[]{:S(2)}) collective-permute-start(bf16[2,32,1536]{2,1,0:T(8,128)(2,1)S(1)} %add_up.11.refs_2_), channel_id=1, source_target_pairs={{0,16},{1,17},{2,18},{3,19},{4,20},{5,21},{6,22},{7,23},{8,24},{9,... | collective-permute-start | bytes 589832 | tf_op jit(solution)/shard_map/ppermute | solution.py:33
  67.0 3.1 %collective-permute-start.22 = (bf16[64,1536]{1,0:T(8,128)(2,1)S(1)}, bf16[64,1536]{1,0:T(8,128)(2,1)S(1)}, u32[]{:S(2)}, u32[]{:S(2)}) collective-permute-start(bf16[64,1536]{1,0:T(8,128)(2,1)S(1)} %join.8.refs_5_.refs_0_), channel_id=1, source_target_pairs={{0,4},{1,9},{2,6},{3,11},{4,0},{5,13},{6,2},{7,15},{8,12},{9,1},{1... | collective-permute-start | bytes 589832 | tf_op jit(solution)/shard_map/ppermute | solution.py:33
  70.1 4.7 %collective-permute-done.17.refs_3_ = bf16[2,32,1536]{2,1,0:T(8,128)(2,1)S(1)} collective-permute-done((bf16[2,32,1536]{2,1,0:T(8,128)(2,1)S(1)}, bf16[2,32,1536]{2,1,0:T(8,128)(2,1)S(1)}, u32[]{:S(2)}, u32[]{:S(2)}) %collective-permute-start.17) | collective-permute-done | bytes 196640 | tf_op jit(solution)/shard_map/ppermute | solution.py:33
  75.4 11.3 %collective-permute-done.16.refs_2_ = bf16[2,64,2048]{2,1,0:T(8,128)(2,1)S(1)} collective-permute-done((bf16[2,64,2048]{2,1,0:T(8,128)(2,1)S(1)}, bf16[2,64,2048]{2,1,0:T(8,128)(2,1)S(1)}, u32[]{:S(2)}, u32[]{:S(2)}) %collective-permute-start.16) | collective-permute-done | bytes 524320 | tf_op jit(solution)/shard_map/ppermute | solution.py:33
  87.3 2.5 %collective-permute-start.19 = (bf16[2,64,1536]{2,1,0:T(8,128)(2,1)S(1)}, bf16[2,64,1536]{2,1,0:T(8,128)(2,1)S(1)}, u32[]{:S(2)}, u32[]{:S(2)}) collective-permute-start(bf16[2,64,1536]{2,1,0:T(8,128)(2,1)S(1)} %add_up.14.refs_2_), channel_id=1, source_target_pairs={{0,8},{1,5},{2,10},{3,7},{4,12},{5,1},{6,14},{7,3},{8,0},{9,13},{1... | collective-permute-start | bytes 1179656 | tf_op jit(solution)/shard_map/ppermute | solution.py:33
  90.0 1.7 %collective-permute-start.25 = (bf16[64,1536]{1,0:T(8,128)(2,1)S(1)}, bf16[64,1536]{1,0:T(8,128)(2,1)S(1)}, u32[]{:S(2)}, u32[]{:S(2)}) collective-permute-start(bf16[64,1536]{1,0:T(8,128)(2,1)S(1)} %join.10.refs_5_.refs_0_), channel_id=1, source_target_pairs={{0,4},{1,9},{2,6},{3,11},{4,0},{5,13},{6,2},{7,15},{8,12},{9,1},{1... | collective-permute-start | bytes 589832 | tf_op jit(solution)/shard_map/ppermute | solution.py:33
  91.8 9.5 %collective-permute-done.20.refs_3_ = bf16[2,32,2048]{2,1,0:T(8,128)(2,1)S(1)} collective-permute-done((bf16[2,32,2048]{2,1,0:T(8,128)(2,1)S(1)}, bf16[2,32,2048]{2,1,0:T(8,128)(2,1)S(1)}, u32[]{:S(2)}, u32[]{:S(2)}) %collective-permute-start.20) | collective-permute-done | bytes 262176 | tf_op jit(solution)/shard_map/ppermute | solution.py:33
  101.5 1.8 %collective-permute-done.19.refs_2_ = bf16[2,64,1536]{2,1,0:T(8,128)(2,1)S(1)} collective-permute-done((bf16[2,64,1536]{2,1,0:T(8,128)(2,1)S(1)}, bf16[2,64,1536]{2,1,0:T(8,128)(2,1)S(1)}, u32[]{:S(2)}, u32[]{:S(2)}) %collective-permute-start.19) | collective-permute-done | bytes 393248 | tf_op jit(solution)/shard_map/ppermute | solution.py:33
  103.4 2.1 %collective-permute-start.23 = (bf16[2,32,1536]{2,1,0:T(8,128)(2,1)S(1)}, bf16[2,32,1536]{2,1,0:T(8,128)(2,1)S(1)}, u32[]{:S(2)}, u32[]{:S(2)}) collective-permute-start(bf16[2,32,1536]{2,1,0:T(8,128)(2,1)S(1)} %add_up.15.refs_2_), channel_id=1, source_target_pairs={{0,16},{1,17},{2,18},{3,19},{4,20},{5,21},{6,22},{7,23},{8,24},{9,... | collective-permute-start | bytes 589832 | tf_op jit(solution)/shard_map/ppermute | solution.py:33
  105.6 1.0 collective-permute-start.29
  106.6 7.0 %collective-permute-done.24.refs_1_ = bf16[32,2048]{1,0:T(8,128)(2,1)S(1)} collective-permute-done((bf16[32,2048]{1,0:T(8,128)(2,1)S(1)}, bf16[32,2048]{1,0:T(8,128)(2,1)S(1)}, u32[]{:S(2)}, u32[]{:S(2)}) %collective-permute-start.24) | collective-permute-done | bytes 131104 | tf_op jit(solution)/shard_map/ppermute | solution.py:33
  113.6 3.0 %collective-permute-start.27 = (bf16[64,2048]{1,0:T(8,128)(2,1)S(1)}, bf16[64,2048]{1,0:T(8,128)(2,1)S(1)}, u32[]{:S(2)}, u32[]{:S(2)}) collective-permute-start(bf16[64,2048]{1,0:T(8,128)(2,1)S(1)} %join.12.refs_5_.refs_0_), channel_id=1, source_target_pairs={{0,8},{1,5},{2,10},{3,7},{4,12},{5,1},{6,14},{7,3},{8,0},{9,13},{1... | collective-permute-start | bytes 786440 | tf_op jit(solution)/shard_map/ppermute | solution.py:33
  116.7 1.9 %collective-permute-done.23.refs_3_ = bf16[2,32,1536]{2,1,0:T(8,128)(2,1)S(1)} collective-permute-done((bf16[2,32,1536]{2,1,0:T(8,128)(2,1)S(1)}, bf16[2,32,1536]{2,1,0:T(8,128)(2,1)S(1)}, u32[]{:S(2)}, u32[]{:S(2)}) %collective-permute-start.23) | collective-permute-done | bytes 196640 | tf_op jit(solution)/shard_map/ppermute | solution.py:33
  119.3 2.2 %collective-permute-done.29.refs_3_ = bf16[128,1536]{1,0:T(8,128)(2,1)S(1)} collective-permute-done((bf16[128,1536]{1,0:T(8,128)(2,1)S(1)}, bf16[128,1536]{1,0:T(8,128)(2,1)S(1)}, u32[]{:S(2)}, u32[]{:S(2)}) %collective-permute-start.29) | collective-permute-done | bytes 393248 | tf_op jit(solution)/shard_map/ppermute | solution.py:33
  121.5 6.6 %down.3.refs_2_.refs_3_ = f32[256,2048]{1,0:T(8,128)S(1)} custom-call(bf16[128,1536]{1,0:T(8,128)(2,1)S(1)} %join.9.refs_2_.refs_0_, bf16[128,1536]{1,0:T(8,128)(2,1)S(1)} %collective-permute-done.28.refs_1_, bf16[128,1536]{1,0:T(8,128)(2,1)S(1)} %join.11.refs_2_, bf16[128,1536]{1,0:T(8,128)(2,1)S(1)} %collective-permute-done.29.refs_3_, ...), custom_call_target="tpu_custom_call" | custom-call | flops 6000000000 | bytes 1024 | tf_op jit(solution)/shard_map/down/pallas_call | solution.py:60
  128.3 0.9 collective-permute-start.30
  129.2 1.8 %collective-permute-start.32 = (bf16[128,2048]{1,0:T(8,128)(2,1)S(1)}, bf16[128,2048]{1,0:T(8,128)(2,1)S(1)}, u32[]{:S(2)}, u32[]{:S(2)}) collective-permute-start(bf16[128,2048]{1,0:T(8,128)(2,1)S(1)} %join.13.refs_2_.refs_0_), channel_id=1, source_target_pairs={{0,4},{1,9},{2,6},{3,11},{4,0},{5,13},{6,2},{7,15},{8,12},{9,1},{1... | collective-permute-start | bytes 1572872 | tf_op jit(solution)/shard_map/ppermute | solution.py:33
  131.0 4.8 %collective-permute-done.30.refs_1_ = bf16[64,1536]{1,0:T(8,128)(2,1)S(1)} collective-permute-done((bf16[64,1536]{1,0:T(8,128)(2,1)S(1)}, bf16[64,1536]{1,0:T(8,128)(2,1)S(1)}, u32[]{:S(2)}, u32[]{:S(2)}) %collective-permute-start.30) | collective-permute-done | bytes 196640 | tf_op jit(solution)/shard_map/ppermute | solution.py:33
  135.8 1.8 %collective-permute-start.31 = (bf16[128,1536]{1,0:T(8,128)(2,1)S(1)}, bf16[128,1536]{1,0:T(8,128)(2,1)S(1)}, u32[]{:S(2)}, u32[]{:S(2)}) collective-permute-start(bf16[128,1536]{1,0:T(8,128)(2,1)S(1)} %join.15.refs_4_.refs_0_), channel_id=1, source_target_pairs={{0,4},{1,9},{2,6},{3,11},{4,0},{5,13},{6,2},{7,15},{8,12},{9,1},{1... | collective-permute-start | bytes 1179656 | tf_op jit(solution)/shard_map/ppermute | solution.py:33
  137.6 0.7 collective-permute-done.32.refs_1_
  138.3 4.9 %down.4.refs_3_.refs_4_ = f32[256,2048]{1,0:T(8,128)S(1)} custom-call(bf16[128,2048]{1,0:T(8,128)(2,1)S(1)} %join.13.refs_2_.refs_0_, bf16[128,2048]{1,0:T(8,128)(2,1)S(1)} %collective-permute-done.32.refs_1_, bf16[6656,2048]{1,0:T(8,128)(2,1)} %refs_2_.11, f32[256,2048]{1,0:T(8,128)S(1)} %down.3.refs_2_.refs_3_, bf16[128,1536]{1,0:T(8,128)(2,1)S(1)} %join.15.refs_4_.refs_0_), custom_call_target="tpu_custom_call" | custom-call | flops 4000000000 | bytes 1024 | tf_op jit(solution)/shard_map/down/pallas_call | solution.py:60
  143.7 4.2 %down.5 = (f32[128,2048]{1,0:T(8,128)S(1)}, bf16[128,2048]{1,0:T(8,128)(2,1)S(1)}) custom-call(bf16[128,1536]{1,0:T(8,128)(2,1)S(1)} %join.15.refs_4_.refs_0_, bf16[128,1536]{1,0:T(8,128)(2,1)S(1)} %collective-permute-done.31.refs_1_, bf16[6656,2048]{1,0:T(8,128)(2,1)} %refs_2_.11, f32[256,2048]{1,0:T(8,128)S(1)} %down.4.refs_3_.refs_4_, ...), custom_call_target="tpu_custom_call" | custom-call | flops 3000000000 | bytes 1024 | tf_op jit(solution)/shard_map/down/pallas_call | solution.py:60
  147.9 1.1 collective-permute-start.33
  149.0 1.5 collective-permute-done.33.refs_1_
  150.5 1.2 collective-permute-start.34
  151.8 7.4 %collective-permute-done.34.refs_2_ = bf16[64,2048]{1,0:T(8,128)(2,1)S(1)} collective-permute-done((bf16[64,2048]{1,0:T(8,128)(2,1)S(1)}, bf16[64,2048]{1,0:T(8,128)(2,1)S(1)}, u32[]{:S(2)}, u32[]{:S(2)}) %collective-permute-start.34) | collective-permute-done | bytes 262176 | tf_op jit(solution)/shard_map/ppermute | solution.py:33
  159.2 0.8 final.1
  (64 shorter events, 5.3 us)
Async XLA Ops:
  0.0 9.5 %collective-permute-start.1 = (bf16[64,2048]{1,0:T(8,128)(2,1)}, bf16[64,2048]{1,0:T(8,128)(2,1)S(1)}, u32[]{:S(2)}, u32[]{:S(2)}) collective-permute-start(bf16[64,2048]{1,0:T(8,128)(2,1)} %refs_0_.5), channel_id=1, source_target_pairs={{0,2},{1,3},{2,0},{3,1},{4,6},{5,7},{6,4},{7,5},{8,10},{9,11},{10,... | collective-permute-start | bytes 786440 | tf_op jit(solution)/shard_map/ppermute | solution.py:33
  3.0 8.4 %collective-permute-start = (bf16[64,2048]{1,0:T(8,128)(2,1)}, bf16[64,2048]{1,0:T(8,128)(2,1)S(1)}, u32[]{:S(2)}, u32[]{:S(2)}) collective-permute-start(bf16[64,2048]{1,0:T(8,128)(2,1)} %refs_0_.5), channel_id=1, source_target_pairs={{0,1},{1,0},{2,3},{3,2},{4,5},{5,4},{6,7},{7,6},{8,9},{9,8},{10,11... | collective-permute-start | bytes 786440 | tf_op jit(solution)/shard_map/ppermute | solution.py:33
  3.0 1.0 copy-start
  4.1 5.4 %collective-permute-start.3 = (f32[64,128]{1,0:T(8,128)S(1)}, f32[64,128]{1,0:T(8,128)S(1)}, u32[]{:S(2)}, u32[]{:S(2)}) collective-permute-start(f32[64,128]{1,0:T(8,128)S(1)} %squares.1.refs_1_.refs_0_), channel_id=1, source_target_pairs={{0,4},{1,9},{2,6},{3,11},{4,0},{5,13},{6,2},{7,15},{8,12},{9,1},{1... | collective-permute-start | bytes 98312 | tf_op jit(solution)/shard_map/ppermute | solution.py:33
  9.5 1.9 %copy-start.1 = (bf16[64,2048]{1,0:T(8,128)(2,1)S(1)}, bf16[64,2048]{1,0:T(8,128)(2,1)}, u32[]{:S(2)}) copy-start(bf16[64,2048]{1,0:T(8,128)(2,1)} %refs_0_.5) | copy-start | bytes 786436
  9.5 1.9 %copy-start.2 = (f32[2048]{0:T(1024)S(1)}, f32[2048]{0:T(1024)}, u32[]{:S(2)}) copy-start(f32[2048]{0:T(1024)} %param.6) | copy-start | bytes 24580
  9.5 1.9 %collective-permute-start.2 = (bf16[64,2048]{1,0:T(8,128)(2,1)S(1)}, bf16[64,2048]{1,0:T(8,128)(2,1)S(1)}, u32[]{:S(2)}, u32[]{:S(2)}) collective-permute-start(bf16[64,2048]{1,0:T(8,128)(2,1)S(1)} %pass.1.refs_2_), channel_id=1, source_target_pairs={{0,1},{1,0},{2,3},{3,2},{4,5},{5,4},{6,7},{7,6},{8,9},{9,8},{10,11... | collective-permute-start | bytes 786440 | tf_op jit(solution)/shard_map/ppermute | solution.py:33
  9.5 11.0 %collective-permute-start.4 = (f32[64,128]{1,0:T(8,128)S(1)}, f32[64,128]{1,0:T(8,128)S(1)}, u32[]{:S(2)}, u32[]{:S(2)}) collective-permute-start(f32[64,128]{1,0:T(8,128)S(1)} %squares_add.3.refs_5_.refs_0_), channel_id=1, source_target_pairs={{0,8},{1,5},{2,10},{3,7},{4,12},{5,1},{6,14},{7,3},{8,0},{9,13},{1... | collective-permute-start | bytes 98312 | tf_op jit(solution)/shard_map/ppermute | solution.py:33
  19.0 12.1 %collective-permute-start.6 = (bf16[2,128,1536]{2,1,0:T(8,128)(2,1)S(1)}, bf16[2,128,1536]{2,1,0:T(8,128)(2,1)S(1)}, u32[]{:S(2)}, u32[]{:S(2)}) collective-permute-start(bf16[2,128,1536]{2,1,0:T(8,128)(2,1)S(1)} %get-tuple-element.18), channel_id=1, source_target_pairs={{0,4},{1,9},{2,6},{3,11},{4,0},{5,13},{6,2},{7,15},{8,12},{9,1},{1... | collective-permute-start | bytes 2359304 | tf_op jit(solution)/shard_map/ppermute | solution.py:33
  20.5 10.6 %collective-permute-start.5 = (f32[64,128]{1,0:T(8,128)S(1)}, f32[64,128]{1,0:T(8,128)S(1)}, u32[]{:S(2)}, u32[]{:S(2)}) collective-permute-start(f32[64,128]{1,0:T(8,128)S(1)} %squares_add.4.refs_3_.refs_0_), channel_id=1, source_target_pairs={{0,16},{1,17},{2,18},{3,19},{4,20},{5,21},{6,22},{7,23},{8,24},{9,... | collective-permute-start | bytes 98312 | tf_op jit(solution)/shard_map/ppermute | solution.py:33
  31.1 5.1 %collective-permute-start.7 = (f32[64,128]{1,0:T(8,128)S(1)}, f32[64,128]{1,0:T(8,128)S(1)}, u32[]{:S(2)}, u32[]{:S(2)}) collective-permute-start(f32[64,128]{1,0:T(8,128)S(1)} %squares_add.5.refs_4_.refs_9_), channel_id=1, source_target_pairs={{0,1},{1,0},{2,3},{3,2},{4,5},{5,4},{6,7},{7,6},{8,9},{9,8},{10,11... | collective-permute-start | bytes 98312 | tf_op jit(solution)/shard_map/ppermute | solution.py:33
  31.2 5.0 %collective-permute-start.8 = (f32[64,128]{1,0:T(8,128)S(1)}, f32[64,128]{1,0:T(8,128)S(1)}, u32[]{:S(2)}, u32[]{:S(2)}) collective-permute-start(f32[64,128]{1,0:T(8,128)S(1)} %squares_add.5.refs_4_.refs_9_), channel_id=1, source_target_pairs={{0,2},{1,3},{2,0},{3,1},{4,6},{5,7},{6,4},{7,5},{8,10},{9,11},{10,... | collective-permute-start | bytes 98312 | tf_op jit(solution)/shard_map/ppermute | solution.py:33
  32.8 3.4 %collective-permute-start.9 = (f32[64,128]{1,0:T(8,128)S(1)}, f32[64,128]{1,0:T(8,128)S(1)}, u32[]{:S(2)}, u32[]{:S(2)}) collective-permute-start(f32[64,128]{1,0:T(8,128)S(1)} %squares_add.5.refs_4_.refs_9_), channel_id=1, source_target_pairs={{0,3},{1,2},{2,1},{3,0},{4,7},{5,6},{6,5},{7,4},{8,11},{9,10},{10,... | collective-permute-start | bytes 98312 | tf_op jit(solution)/shard_map/ppermute | solution.py:33
  33.1 16.3 %collective-permute-start.10 = (bf16[2,128,1536]{2,1,0:T(8,128)(2,1)S(1)}, bf16[2,128,1536]{2,1,0:T(8,128)(2,1)S(1)}, u32[]{:S(2)}, u32[]{:S(2)}) collective-permute-start(bf16[2,128,1536]{2,1,0:T(8,128)(2,1)S(1)} %get-tuple-element.21), channel_id=1, source_target_pairs={{0,4},{1,9},{2,6},{3,11},{4,0},{5,13},{6,2},{7,15},{8,12},{9,1},{1... | collective-permute-start | bytes 2359304 | tf_op jit(solution)/shard_map/ppermute | solution.py:33
  34.5 12.1 %collective-permute-start.11 = (bf16[2,64,1536]{2,1,0:T(8,128)(2,1)S(1)}, bf16[2,64,1536]{2,1,0:T(8,128)(2,1)S(1)}, u32[]{:S(2)}, u32[]{:S(2)}) collective-permute-start(bf16[2,64,1536]{2,1,0:T(8,128)(2,1)S(1)} %add_up.8.refs_2_), channel_id=1, source_target_pairs={{0,8},{1,5},{2,10},{3,7},{4,12},{5,1},{6,14},{7,3},{8,0},{9,13},{1... | collective-permute-start | bytes 1179656 | tf_op jit(solution)/shard_map/ppermute | solution.py:33
  45.2 21.1 %collective-permute-start.13 = (bf16[2,128,2048]{2,1,0:T(8,128)(2,1)S(1)}, bf16[2,128,2048]{2,1,0:T(8,128)(2,1)S(1)}, u32[]{:S(2)}, u32[]{:S(2)}) collective-permute-start(bf16[2,128,2048]{2,1,0:T(8,128)(2,1)S(1)} %get-tuple-element.25), channel_id=1, source_target_pairs={{0,4},{1,9},{2,6},{3,11},{4,0},{5,13},{6,2},{7,15},{8,12},{9,1},{1... | collective-permute-start | bytes 3145736 | tf_op jit(solution)/shard_map/ppermute | solution.py:33
  46.7 12.6 %collective-permute-start.15 = (bf16[2,32,1536]{2,1,0:T(8,128)(2,1)S(1)}, bf16[2,32,1536]{2,1,0:T(8,128)(2,1)S(1)}, u32[]{:S(2)}, u32[]{:S(2)}) collective-permute-start(bf16[2,32,1536]{2,1,0:T(8,128)(2,1)S(1)} %add_up.9.refs_2_), channel_id=1, source_target_pairs={{0,16},{1,17},{2,18},{3,19},{4,20},{5,21},{6,22},{7,23},{8,24},{9,... | collective-permute-start | bytes 589832 | tf_op jit(solution)/shard_map/ppermute | solution.py:33
  49.5 14.3 %collective-permute-start.14 = (bf16[2,64,1536]{2,1,0:T(8,128)(2,1)S(1)}, bf16[2,64,1536]{2,1,0:T(8,128)(2,1)S(1)}, u32[]{:S(2)}, u32[]{:S(2)}) collective-permute-start(bf16[2,64,1536]{2,1,0:T(8,128)(2,1)S(1)} %add_up.10.refs_3_), channel_id=1, source_target_pairs={{0,8},{1,5},{2,10},{3,7},{4,12},{5,1},{6,14},{7,3},{8,0},{9,13},{1... | collective-permute-start | bytes 1179656 | tf_op jit(solution)/shard_map/ppermute | solution.py:33
  58.1 29.2 %collective-permute-start.12 = (bf16[2,128,1536]{2,1,0:T(8,128)(2,1)S(1)}, bf16[2,128,1536]{2,1,0:T(8,128)(2,1)S(1)}, u32[]{:S(2)}, u32[]{:S(2)}) collective-permute-start(bf16[2,128,1536]{2,1,0:T(8,128)(2,1)S(1)} %get-tuple-element.24), channel_id=1, source_target_pairs={{0,4},{1,9},{2,6},{3,11},{4,0},{5,13},{6,2},{7,15},{8,12},{9,1},{1... | collective-permute-start | bytes 2359304 | tf_op jit(solution)/shard_map/ppermute | solution.py:33
  59.5 7.5 %collective-permute-start.18 = (bf16[32,1536]{1,0:T(8,128)(2,1)S(1)}, bf16[32,1536]{1,0:T(8,128)(2,1)S(1)}, u32[]{:S(2)}, u32[]{:S(2)}) collective-permute-start(bf16[32,1536]{1,0:T(8,128)(2,1)S(1)} %activate.4.refs_3_.refs_0_), channel_id=1, source_target_pairs={{0,16},{1,17},{2,18},{3,19},{4,20},{5,21},{6,22},{7,23},{8,24},{9,... | collective-permute-start | bytes 294920 | tf_op jit(solution)/shard_map/ppermute | solution.py:33
  63.8 11.0 %collective-permute-start.17 = (bf16[2,32,1536]{2,1,0:T(8,128)(2,1)S(1)}, bf16[2,32,1536]{2,1,0:T(8,128)(2,1)S(1)}, u32[]{:S(2)}, u32[]{:S(2)}) collective-permute-start(bf16[2,32,1536]{2,1,0:T(8,128)(2,1)S(1)} %add_up.11.refs_2_), channel_id=1, source_target_pairs={{0,16},{1,17},{2,18},{3,19},{4,20},{5,21},{6,22},{7,23},{8,24},{9,... | collective-permute-start | bytes 589832 | tf_op jit(solution)/shard_map/ppermute | solution.py:33
  66.4 20.2 %collective-permute-start.16 = (bf16[2,64,2048]{2,1,0:T(8,128)(2,1)S(1)}, bf16[2,64,2048]{2,1,0:T(8,128)(2,1)S(1)}, u32[]{:S(2)}, u32[]{:S(2)}) collective-permute-start(bf16[2,64,2048]{2,1,0:T(8,128)(2,1)S(1)} %add_up.12.refs_2_), channel_id=1, source_target_pairs={{0,8},{1,5},{2,10},{3,7},{4,12},{5,1},{6,14},{7,3},{8,0},{9,13},{1... | collective-permute-start | bytes 1572872 | tf_op jit(solution)/shard_map/ppermute | solution.py:33
  67.0 22.9 %collective-permute-start.22 = (bf16[64,1536]{1,0:T(8,128)(2,1)S(1)}, bf16[64,1536]{1,0:T(8,128)(2,1)S(1)}, u32[]{:S(2)}, u32[]{:S(2)}) collective-permute-start(bf16[64,1536]{1,0:T(8,128)(2,1)S(1)} %join.8.refs_5_.refs_0_), channel_id=1, source_target_pairs={{0,4},{1,9},{2,6},{3,11},{4,0},{5,13},{6,2},{7,15},{8,12},{9,1},{1... | collective-permute-start | bytes 589832 | tf_op jit(solution)/shard_map/ppermute | solution.py:33
  75.0 15.0 %collective-permute-start.21 = (bf16[32,1536]{1,0:T(8,128)(2,1)S(1)}, bf16[32,1536]{1,0:T(8,128)(2,1)S(1)}, u32[]{:S(2)}, u32[]{:S(2)}) collective-permute-start(bf16[32,1536]{1,0:T(8,128)(2,1)S(1)} %activate.5.refs_3_.refs_0_), channel_id=1, source_target_pairs={{0,16},{1,17},{2,18},{3,19},{4,20},{5,21},{6,22},{7,23},{8,24},{9,... | collective-permute-start | bytes 294920 | tf_op jit(solution)/shard_map/ppermute | solution.py:33
  86.7 14.5 %collective-permute-start.20 = (bf16[2,32,2048]{2,1,0:T(8,128)(2,1)S(1)}, bf16[2,32,2048]{2,1,0:T(8,128)(2,1)S(1)}, u32[]{:S(2)}, u32[]{:S(2)}) collective-permute-start(bf16[2,32,2048]{2,1,0:T(8,128)(2,1)S(1)} %add_up.13.refs_2_), channel_id=1, source_target_pairs={{0,16},{1,17},{2,18},{3,19},{4,20},{5,21},{6,22},{7,23},{8,24},{9,... | collective-permute-start | bytes 786440 | tf_op jit(solution)/shard_map/ppermute | solution.py:33
  87.3 16.0 %collective-permute-start.19 = (bf16[2,64,1536]{2,1,0:T(8,128)(2,1)S(1)}, bf16[2,64,1536]{2,1,0:T(8,128)(2,1)S(1)}, u32[]{:S(2)}, u32[]{:S(2)}) collective-permute-start(bf16[2,64,1536]{2,1,0:T(8,128)(2,1)S(1)} %add_up.14.refs_2_), channel_id=1, source_target_pairs={{0,8},{1,5},{2,10},{3,7},{4,12},{5,1},{6,14},{7,3},{8,0},{9,13},{1... | collective-permute-start | bytes 1179656 | tf_op jit(solution)/shard_map/ppermute | solution.py:33
  89.9 29.4 %collective-permute-start.28 = (bf16[128,1536]{1,0:T(8,128)(2,1)S(1)}, bf16[128,1536]{1,0:T(8,128)(2,1)S(1)}, u32[]{:S(2)}, u32[]{:S(2)}) collective-permute-start(bf16[128,1536]{1,0:T(8,128)(2,1)S(1)} %join.9.refs_2_.refs_0_), channel_id=1, source_target_pairs={{0,8},{1,5},{2,10},{3,7},{4,12},{5,1},{6,14},{7,3},{8,0},{9,13},{1... | collective-permute-start | bytes 1179656 | tf_op jit(solution)/shard_map/ppermute | solution.py:33
  90.0 15.5 %collective-permute-start.25 = (bf16[64,1536]{1,0:T(8,128)(2,1)S(1)}, bf16[64,1536]{1,0:T(8,128)(2,1)S(1)}, u32[]{:S(2)}, u32[]{:S(2)}) collective-permute-start(bf16[64,1536]{1,0:T(8,128)(2,1)S(1)} %join.10.refs_5_.refs_0_), channel_id=1, source_target_pairs={{0,4},{1,9},{2,6},{3,11},{4,0},{5,13},{6,2},{7,15},{8,12},{9,1},{1... | collective-permute-start | bytes 589832 | tf_op jit(solution)/shard_map/ppermute | solution.py:33
  101.5 12.1 %collective-permute-start.24 = (bf16[32,2048]{1,0:T(8,128)(2,1)S(1)}, bf16[32,2048]{1,0:T(8,128)(2,1)S(1)}, u32[]{:S(2)}, u32[]{:S(2)}) collective-permute-start(bf16[32,2048]{1,0:T(8,128)(2,1)S(1)} %activate.6.refs_3_.refs_0_), channel_id=1, source_target_pairs={{0,16},{1,17},{2,18},{3,19},{4,20},{5,21},{6,22},{7,23},{8,24},{9,... | collective-permute-start | bytes 393224 | tf_op jit(solution)/shard_map/ppermute | solution.py:33
  103.4 15.1 %collective-permute-start.23 = (bf16[2,32,1536]{2,1,0:T(8,128)(2,1)S(1)}, bf16[2,32,1536]{2,1,0:T(8,128)(2,1)S(1)}, u32[]{:S(2)}, u32[]{:S(2)}) collective-permute-start(bf16[2,32,1536]{2,1,0:T(8,128)(2,1)S(1)} %add_up.15.refs_2_), channel_id=1, source_target_pairs={{0,16},{1,17},{2,18},{3,19},{4,20},{5,21},{6,22},{7,23},{8,24},{9,... | collective-permute-start | bytes 589832 | tf_op jit(solution)/shard_map/ppermute | solution.py:33
  105.6 16.0 %collective-permute-start.29 = (bf16[128,1536]{1,0:T(8,128)(2,1)S(1)}, bf16[128,1536]{1,0:T(8,128)(2,1)S(1)}, u32[]{:S(2)}, u32[]{:S(2)}) collective-permute-start(bf16[128,1536]{1,0:T(8,128)(2,1)S(1)} %join.11.refs_2_), channel_id=1, source_target_pairs={{0,8},{1,5},{2,10},{3,7},{4,12},{5,1},{6,14},{7,3},{8,0},{9,13},{1... | collective-permute-start | bytes 1179656 | tf_op jit(solution)/shard_map/ppermute | solution.py:33
  113.6 14.5 %collective-permute-start.27 = (bf16[64,2048]{1,0:T(8,128)(2,1)S(1)}, bf16[64,2048]{1,0:T(8,128)(2,1)S(1)}, u32[]{:S(2)}, u32[]{:S(2)}) collective-permute-start(bf16[64,2048]{1,0:T(8,128)(2,1)S(1)} %join.12.refs_5_.refs_0_), channel_id=1, source_target_pairs={{0,8},{1,5},{2,10},{3,7},{4,12},{5,1},{6,14},{7,3},{8,0},{9,13},{1... | collective-permute-start | bytes 786440 | tf_op jit(solution)/shard_map/ppermute | solution.py:33
  118.7 9.5 %collective-permute-start.26 = (bf16[32,1536]{1,0:T(8,128)(2,1)S(1)}, bf16[32,1536]{1,0:T(8,128)(2,1)S(1)}, u32[]{:S(2)}, u32[]{:S(2)}) collective-permute-start(bf16[32,1536]{1,0:T(8,128)(2,1)S(1)} %activate.7.refs_5_.refs_0_), channel_id=1, source_target_pairs={{0,16},{1,17},{2,18},{3,19},{4,20},{5,21},{6,22},{7,23},{8,24},{9,... | collective-permute-start | bytes 294920 | tf_op jit(solution)/shard_map/ppermute | solution.py:33
  128.3 7.5 %collective-permute-start.30 = (bf16[64,1536]{1,0:T(8,128)(2,1)S(1)}, bf16[64,1536]{1,0:T(8,128)(2,1)S(1)}, u32[]{:S(2)}, u32[]{:S(2)}) collective-permute-start(bf16[64,1536]{1,0:T(8,128)(2,1)S(1)} %join.14.refs_0_.refs_2_), channel_id=1, source_target_pairs={{0,8},{1,5},{2,10},{3,7},{4,12},{5,1},{6,14},{7,3},{8,0},{9,13},{1... | collective-permute-start | bytes 589832 | tf_op jit(solution)/shard_map/ppermute | solution.py:33
  129.2 9.2 %collective-permute-start.32 = (bf16[128,2048]{1,0:T(8,128)(2,1)S(1)}, bf16[128,2048]{1,0:T(8,128)(2,1)S(1)}, u32[]{:S(2)}, u32[]{:S(2)}) collective-permute-start(bf16[128,2048]{1,0:T(8,128)(2,1)S(1)} %join.13.refs_2_.refs_0_), channel_id=1, source_target_pairs={{0,4},{1,9},{2,6},{3,11},{4,0},{5,13},{6,2},{7,15},{8,12},{9,1},{1... | collective-permute-start | bytes 1572872 | tf_op jit(solution)/shard_map/ppermute | solution.py:33
  135.8 7.8 %collective-permute-start.31 = (bf16[128,1536]{1,0:T(8,128)(2,1)S(1)}, bf16[128,1536]{1,0:T(8,128)(2,1)S(1)}, u32[]{:S(2)}, u32[]{:S(2)}) collective-permute-start(bf16[128,1536]{1,0:T(8,128)(2,1)S(1)} %join.15.refs_4_.refs_0_), channel_id=1, source_target_pairs={{0,4},{1,9},{2,6},{3,11},{4,0},{5,13},{6,2},{7,15},{8,12},{9,1},{1... | collective-permute-start | bytes 1179656 | tf_op jit(solution)/shard_map/ppermute | solution.py:33
  147.9 2.6 %collective-permute-start.33 = (bf16[128,2048]{1,0:T(8,128)(2,1)S(1)}, bf16[128,2048]{1,0:T(8,128)(2,1)S(1)}, u32[]{:S(2)}, u32[]{:S(2)}) collective-permute-start(bf16[128,2048]{1,0:T(8,128)(2,1)S(1)} %get-tuple-element.28), channel_id=1, source_target_pairs={{0,1},{1,0},{2,3},{3,2},{4,5},{5,4},{6,7},{7,6},{8,9},{9,8},{10,11... | collective-permute-start | bytes 1572872 | tf_op jit(solution)/shard_map/ppermute | solution.py:33
  150.5 8.7 %collective-permute-start.34 = (bf16[64,2048]{1,0:T(8,128)(2,1)S(1)}, bf16[64,2048]{1,0:T(8,128)(2,1)S(1)}, u32[]{:S(2)}, u32[]{:S(2)}) collective-permute-start(bf16[64,2048]{1,0:T(8,128)(2,1)S(1)} %send_y.1.refs_3_), channel_id=1, source_target_pairs={{0,2},{1,3},{2,0},{3,1},{4,6},{5,7},{6,4},{7,5},{8,10},{9,11},{10,... | collective-permute-start | bytes 786440 | tf_op jit(solution)/shard_map/ppermute | solution.py:33

commit v5 on v4

--- a/solution.py
+++ b/solution.py
@@ -217,7 +217,7 @@
 SUM, GATHER = "mmmm", "nnmm"
 GROUPS = ((0, 1,), (2,), (3,),)
 ORDER = (
-    "m0", "s", "m1", "a0", "q", "n", "m2", "b0", "a1", "m3", "c0", "b1",
+    "m0", "m1", "s", "a0", "q", "b0", "n", "m2", "a1", "m3", "c0", "b1",
     "a2", "d0", "c1", "b2", "a3", "e0", "d1", "c2", "b3", "e1", "d2", "c3",
     "w0", "e2", "d3", "e3", "w1", "w2",
 )

time: 160 us -> 163 us (1.019)
  waiting for transfers between devices: 59.8 us -> 65.8 us
  starting transfers between devices: 50.1 us -> 47.2 us
    ppermute x35, waiting for transfers between devices: 59.8 us -> 65.8 us  [swap(): return lax.ppermute(a, AXES, pairs)]
    ppermute x35, starting transfers between devices: 50.1 us -> 47.2 us  [swap(): return lax.ppermute(a, AXES, pairs)]
  transfers between devices with their start and end apart: 35 -> 35, of which waited for: 15 -> 16; matrix products, arithmetic and copies ran while one was open for 0% -> 0% of each run, Pallas kernels for 27% -> 27%
where the time goes in v5:
time: 163 us
  waiting for transfers between devices  65.8 us (40%)
  Pallas kernels  48.9 us (30%)
  starting transfers between devices  47.2 us (29%)
    ppermute x35, waiting for transfers between devices, swap(): return lax.ppermute(a, AXES, pairs)  65.8 us
    pallas_call x36, Pallas kernels, call(): pl.pallas_call(run, out_shape=tuple(out_shape), grid=grid, in_specs=in_sp...  48.9 us
    ppermute x35, starting transfers between devices, swap(): return lax.ppermute(a, AXES, pairs)  47.2 us
  transfers between devices with their start and end apart: 35, of which 16 were waited for; matrix products, arithmetic and copies ran while one was open for 0% of the time, Pallas kernels for 27%

profile of v5, /device:TPU:0, one launch (start us, length us, event | category | flops | bytes accessed | tf_op | source)
XLA Modules:
  0.0 163.1 jit_solution(3000402460024729481)
XLA Ops:
  0.0 3.0 %collective-permute-start.1 = (bf16[64,2048]{1,0:T(8,128)(2,1)}, bf16[64,2048]{1,0:T(8,128)(2,1)S(1)}, u32[]{:S(2)}, u32[]{:S(2)}) collective-permute-start(bf16[64,2048]{1,0:T(8,128)(2,1)} %refs_0_.5), channel_id=1, source_target_pairs={{0,2},{1,3},{2,0},{3,1},{4,6},{5,7},{6,4},{7,5},{8,10},{9,11},{10,... | collective-permute-start | bytes 786440 | tf_op jit(solution)/shard_map/ppermute | solution.py:33
  3.0 1.0 copy-done
  4.1 1.5 collective-permute-start.3
  5.6 3.9 %collective-permute-done.1.refs_0_ = bf16[64,2048]{1,0:T(8,128)(2,1)S(1)} collective-permute-done((bf16[64,2048]{1,0:T(8,128)(2,1)}, bf16[64,2048]{1,0:T(8,128)(2,1)S(1)}, u32[]{:S(2)}, u32[]{:S(2)}) %collective-permute-start.1) | collective-permute-done | bytes 262176 | tf_op jit(solution)/shard_map/ppermute | solution.py:33
  9.5 1.9 %collective-permute-start.4 = (f32[64,128]{1,0:T(8,128)S(1)}, f32[64,128]{1,0:T(8,128)S(1)}, u32[]{:S(2)}, u32[]{:S(2)}) collective-permute-start(f32[64,128]{1,0:T(8,128)S(1)} %squares_add.3.refs_5_.refs_0_), channel_id=1, source_target_pairs={{0,8},{1,5},{2,10},{3,7},{4,12},{5,1},{6,14},{7,3},{8,0},{9,13},{1... | collective-permute-start | bytes 98312 | tf_op jit(solution)/shard_map/ppermute | solution.py:33
  11.7 7.3 %project.4 = (f32[2,128,1536]{2,1,0:T(8,128)S(1)}, bf16[2,128,1536]{2,1,0:T(8,128)(2,1)S(1)}) custom-call(bf16[256,2048]{1,0:T(8,128)(2,1)S(1)} %arrange.1.refs_0_.refs_3_, bf16[2048,6656]{1,0:T(8,128)(2,1)} %refs_1_.7, bf16[2048,6656]{1,0:T(8,128)(2,1)} %refs_2_.9, bf16[256,2048]{1,0:T(8,128)(2,1)S(1)} %arrange.1.refs_0_.refs_3_), custom_call_target="tpu_custom_call" | custom-call | flops 7500000256 | bytes 1024 | tf_op jit(solution)/shard_map/project/pallas_call | solution.py:60
  19.0 1.6 collective-permute-start.6
  20.5 7.1 %project.5 = (f32[2,128,1536]{2,1,0:T(8,128)S(1)}, bf16[2,128,1536]{2,1,0:T(8,128)(2,1)S(1)}) custom-call(bf16[256,2048]{1,0:T(8,128)(2,1)S(1)} %arrange.1.refs_0_.refs_3_, bf16[2048,6656]{1,0:T(8,128)(2,1)} %refs_1_.7, bf16[2048,6656]{1,0:T(8,128)(2,1)} %refs_2_.9, f32[2,128,1536]{2,1,0:T(8,128)S(1)} %get-tuple-element.17.refs_3_.refs_0_), custom_call_target="tpu_custom_call" | custom-call | flops 7500000256 | bytes 1024 | tf_op jit(solution)/shard_map/project/pallas_call | solution.py:60
  27.6 2.7 %collective-permute-start.5 = (f32[64,128]{1,0:T(8,128)S(1)}, f32[64,128]{1,0:T(8,128)S(1)}, u32[]{:S(2)}, u32[]{:S(2)}) collective-permute-start(f32[64,128]{1,0:T(8,128)S(1)} %squares_add.4.refs_2_.refs_0_), channel_id=1, source_target_pairs={{0,16},{1,17},{2,18},{3,19},{4,20},{5,21},{6,22},{7,23},{8,24},{9,... | collective-permute-start | bytes 98312 | tf_op jit(solution)/shard_map/ppermute | solution.py:33
  30.3 0.7 collective-permute-done.6.refs_1_
  31.1 1.5 collective-permute-start.10
  32.6 1.5 collective-permute-start.11
  34.2 1.6 collective-permute-start.8
  36.0 9.2 %collective-permute-done.10.refs_2_ = bf16[2,64,1536]{2,1,0:T(8,128)(2,1)S(1)} collective-permute-done((bf16[2,64,1536]{2,1,0:T(8,128)(2,1)S(1)}, bf16[2,64,1536]{2,1,0:T(8,128)(2,1)S(1)}, u32[]{:S(2)}, u32[]{:S(2)}) %collective-permute-start.10) | collective-permute-done | bytes 393248 | tf_op jit(solution)/shard_map/ppermute | solution.py:33
  46.1 8.7 %project.6 = (f32[2,128,2048]{2,1,0:T(8,128)S(1)}, bf16[2,128,2048]{2,1,0:T(8,128)(2,1)S(1)}) custom-call(bf16[256,2048]{1,0:T(8,128)(2,1)S(1)} %get-tuple-element.20.refs_0_.refs_3_, bf16[2048,6656]{1,0:T(8,128)(2,1)} %refs_1_.7, bf16[2048,6656]{1,0:T(8,128)(2,1)} %refs_2_.9, bf16[256,2048]{1,0:T(8,128)(2,1)S(1)} %get-tuple-element.20.refs_0_.refs_3_), custom_call_target="tpu_custom_call" | custom-call | flops 10000000000 | bytes 1024 | tf_op jit(solution)/shard_map/project/pallas_call | solution.py:60
  54.9 1.6 collective-permute-start.14
  56.4 1.5 collective-permute-start.13
  57.9 7.1 %project.7 = (f32[2,128,1536]{2,1,0:T(8,128)S(1)}, bf16[2,128,1536]{2,1,0:T(8,128)(2,1)S(1)}) custom-call(bf16[256,2048]{1,0:T(8,128)(2,1)S(1)} %get-tuple-element.20.refs_0_.refs_3_, bf16[2048,6656]{1,0:T(8,128)(2,1)} %refs_1_.7, bf16[2048,6656]{1,0:T(8,128)(2,1)} %refs_2_.9, bf16[2,64,1536]{2,1,0:T(8,128)(2,1)S(1)} %add_up.10.refs_3_), custom_call_target="tpu_custom_call" | custom-call | flops 7500000256 | bytes 1024 | tf_op jit(solution)/shard_map/project/pallas_call | solution.py:60
  65.0 0.6 collective-permute-start.12
  65.8 1.1 collective-permute-start.18
  67.0 3.2 %collective-permute-done.14.refs_2_ = bf16[2,64,1536]{2,1,0:T(8,128)(2,1)S(1)} collective-permute-done((bf16[2,64,1536]{2,1,0:T(8,128)(2,1)S(1)}, bf16[2,64,1536]{2,1,0:T(8,128)(2,1)S(1)}, u32[]{:S(2)}, u32[]{:S(2)}) %collective-permute-start.14) | collective-permute-done | bytes 393248 | tf_op jit(solution)/shard_map/ppermute | solution.py:33
  70.3 0.9 collective-permute-done.13.refs_1_
  71.3 1.6 collective-permute-start.16
  72.9 1.7 %collective-permute-start.22 = (bf16[64,1536]{1,0:T(8,128)(2,1)S(1)}, bf16[64,1536]{1,0:T(8,128)(2,1)S(1)}, u32[]{:S(2)}, u32[]{:S(2)}) collective-permute-start(bf16[64,1536]{1,0:T(8,128)(2,1)S(1)} %join.8.refs_5_.refs_0_), channel_id=1, source_target_pairs={{0,4},{1,9},{2,6},{3,11},{4,0},{5,13},{6,2},{7,15},{8,12},{9,1},{1... | collective-permute-start | bytes 589832 | tf_op jit(solution)/shard_map/ppermute | solution.py:33
  74.6 4.0 %collective-permute-done.17.refs_3_ = bf16[2,32,1536]{2,1,0:T(8,128)(2,1)S(1)} collective-permute-done((bf16[2,32,1536]{2,1,0:T(8,128)(2,1)S(1)}, bf16[2,32,1536]{2,1,0:T(8,128)(2,1)S(1)}, u32[]{:S(2)}, u32[]{:S(2)}) %collective-permute-start.17) | collective-permute-done | bytes 196640 | tf_op jit(solution)/shard_map/ppermute | solution.py:33
  79.3 10.0 %collective-permute-done.16.refs_2_ = bf16[2,64,2048]{2,1,0:T(8,128)(2,1)S(1)} collective-permute-done((bf16[2,64,2048]{2,1,0:T(8,128)(2,1)S(1)}, bf16[2,64,2048]{2,1,0:T(8,128)(2,1)S(1)}, u32[]{:S(2)}, u32[]{:S(2)}) %collective-permute-start.16) | collective-permute-done | bytes 524320 | tf_op jit(solution)/shard_map/ppermute | solution.py:33
  90.0 2.3 %collective-permute-start.19 = (bf16[2,64,1536]{2,1,0:T(8,128)(2,1)S(1)}, bf16[2,64,1536]{2,1,0:T(8,128)(2,1)S(1)}, u32[]{:S(2)}, u32[]{:S(2)}) collective-permute-start(bf16[2,64,1536]{2,1,0:T(8,128)(2,1)S(1)} %add_up.14.refs_2_), channel_id=1, source_target_pairs={{0,8},{1,5},{2,10},{3,7},{4,12},{5,1},{6,14},{7,3},{8,0},{9,13},{1... | collective-permute-start | bytes 1179656 | tf_op jit(solution)/shard_map/ppermute | solution.py:33
  92.5 1.7 %collective-permute-start.25 = (bf16[64,1536]{1,0:T(8,128)(2,1)S(1)}, bf16[64,1536]{1,0:T(8,128)(2,1)S(1)}, u32[]{:S(2)}, u32[]{:S(2)}) collective-permute-start(bf16[64,1536]{1,0:T(8,128)(2,1)S(1)} %join.10.refs_5_.refs_0_), channel_id=1, source_target_pairs={{0,4},{1,9},{2,6},{3,11},{4,0},{5,13},{6,2},{7,15},{8,12},{9,1},{1... | collective-permute-start | bytes 589832 | tf_op jit(solution)/shard_map/ppermute | solution.py:33
  94.2 9.6 %collective-permute-done.20.refs_3_ = bf16[2,32,2048]{2,1,0:T(8,128)(2,1)S(1)} collective-permute-done((bf16[2,32,2048]{2,1,0:T(8,128)(2,1)S(1)}, bf16[2,32,2048]{2,1,0:T(8,128)(2,1)S(1)}, u32[]{:S(2)}, u32[]{:S(2)}) %collective-permute-start.20) | collective-permute-done | bytes 262176 | tf_op jit(solution)/shard_map/ppermute | solution.py:33
  104.0 1.2 collective-permute-done.19.refs_2_
  105.3 1.8 %collective-permute-start.23 = (bf16[2,32,1536]{2,1,0:T(8,128)(2,1)S(1)}, bf16[2,32,1536]{2,1,0:T(8,128)(2,1)S(1)}, u32[]{:S(2)}, u32[]{:S(2)}) collective-permute-start(bf16[2,32,1536]{2,1,0:T(8,128)(2,1)S(1)} %add_up.15.refs_2_), channel_id=1, source_target_pairs={{0,16},{1,17},{2,18},{3,19},{4,20},{5,21},{6,22},{7,23},{8,24},{9,... | collective-permute-start | bytes 589832 | tf_op jit(solution)/shard_map/ppermute | solution.py:33
  107.1 1.2 collective-permute-start.29
  108.2 7.2 %collective-permute-done.24.refs_1_ = bf16[32,2048]{1,0:T(8,128)(2,1)S(1)} collective-permute-done((bf16[32,2048]{1,0:T(8,128)(2,1)S(1)}, bf16[32,2048]{1,0:T(8,128)(2,1)S(1)}, u32[]{:S(2)}, u32[]{:S(2)}) %collective-permute-start.24) | collective-permute-done | bytes 131104 | tf_op jit(solution)/shard_map/ppermute | solution.py:33
  115.5 2.8 %collective-permute-start.27 = (bf16[64,2048]{1,0:T(8,128)(2,1)S(1)}, bf16[64,2048]{1,0:T(8,128)(2,1)S(1)}, u32[]{:S(2)}, u32[]{:S(2)}) collective-permute-start(bf16[64,2048]{1,0:T(8,128)(2,1)S(1)} %join.12.refs_5_.refs_0_), channel_id=1, source_target_pairs={{0,8},{1,5},{2,10},{3,7},{4,12},{5,1},{6,14},{7,3},{8,0},{9,13},{1... | collective-permute-start | bytes 786440 | tf_op jit(solution)/shard_map/ppermute | solution.py:33
  118.2 2.4 %collective-permute-done.23.refs_3_ = bf16[2,32,1536]{2,1,0:T(8,128)(2,1)S(1)} collective-permute-done((bf16[2,32,1536]{2,1,0:T(8,128)(2,1)S(1)}, bf16[2,32,1536]{2,1,0:T(8,128)(2,1)S(1)}, u32[]{:S(2)}, u32[]{:S(2)}) %collective-permute-start.23) | collective-permute-done | bytes 196640 | tf_op jit(solution)/shard_map/ppermute | solution.py:33
  121.2 1.5 collective-permute-done.29.refs_3_
  122.7 6.6 %down.3.refs_2_.refs_3_ = f32[256,2048]{1,0:T(8,128)S(1)} custom-call(bf16[128,1536]{1,0:T(8,128)(2,1)S(1)} %join.9.refs_2_.refs_0_, bf16[128,1536]{1,0:T(8,128)(2,1)S(1)} %collective-permute-done.28.refs_1_, bf16[128,1536]{1,0:T(8,128)(2,1)S(1)} %join.11.refs_2_, bf16[128,1536]{1,0:T(8,128)(2,1)S(1)} %collective-permute-done.29.refs_3_, ...), custom_call_target="tpu_custom_call" | custom-call | flops 6000000000 | bytes 1024 | tf_op jit(solution)/shard_map/down/pallas_call | solution.py:60
  129.4 3.6 %collective-permute-start.30 = (bf16[64,1536]{1,0:T(8,128)(2,1)S(1)}, bf16[64,1536]{1,0:T(8,128)(2,1)S(1)}, u32[]{:S(2)}, u32[]{:S(2)}) collective-permute-start(bf16[64,1536]{1,0:T(8,128)(2,1)S(1)} %join.14.refs_0_.refs_2_), channel_id=1, source_target_pairs={{0,8},{1,5},{2,10},{3,7},{4,12},{5,1},{6,14},{7,3},{8,0},{9,13},{1... | collective-permute-start | bytes 589832 | tf_op jit(solution)/shard_map/ppermute | solution.py:33
  133.0 2.5 %collective-permute-start.32 = (bf16[128,2048]{1,0:T(8,128)(2,1)S(1)}, bf16[128,2048]{1,0:T(8,128)(2,1)S(1)}, u32[]{:S(2)}, u32[]{:S(2)}) collective-permute-start(bf16[128,2048]{1,0:T(8,128)(2,1)S(1)} %join.13.refs_2_.refs_0_), channel_id=1, source_target_pairs={{0,4},{1,9},{2,6},{3,11},{4,0},{5,13},{6,2},{7,15},{8,12},{9,1},{1... | collective-permute-start | bytes 1572872 | tf_op jit(solution)/shard_map/ppermute | solution.py:33
  135.5 1.9 %collective-permute-done.30.refs_1_ = bf16[64,1536]{1,0:T(8,128)(2,1)S(1)} collective-permute-done((bf16[64,1536]{1,0:T(8,128)(2,1)S(1)}, bf16[64,1536]{1,0:T(8,128)(2,1)S(1)}, u32[]{:S(2)}, u32[]{:S(2)}) %collective-permute-start.30) | collective-permute-done | bytes 196640 | tf_op jit(solution)/shard_map/ppermute | solution.py:33
  137.5 3.9 %collective-permute-start.31 = (bf16[128,1536]{1,0:T(8,128)(2,1)S(1)}, bf16[128,1536]{1,0:T(8,128)(2,1)S(1)}, u32[]{:S(2)}, u32[]{:S(2)}) collective-permute-start(bf16[128,1536]{1,0:T(8,128)(2,1)S(1)} %join.15.refs_4_.refs_0_), channel_id=1, source_target_pairs={{0,4},{1,9},{2,6},{3,11},{4,0},{5,13},{6,2},{7,15},{8,12},{9,1},{1... | collective-permute-start | bytes 1179656 | tf_op jit(solution)/shard_map/ppermute | solution.py:33
  141.4 1.3 collective-permute-done.32.refs_1_
  142.7 4.9 %down.4.refs_3_.refs_4_ = f32[256,2048]{1,0:T(8,128)S(1)} custom-call(bf16[128,2048]{1,0:T(8,128)(2,1)S(1)} %join.13.refs_2_.refs_0_, bf16[128,2048]{1,0:T(8,128)(2,1)S(1)} %collective-permute-done.32.refs_1_, bf16[6656,2048]{1,0:T(8,128)(2,1)} %refs_2_.11, f32[256,2048]{1,0:T(8,128)S(1)} %down.3.refs_2_.refs_3_, bf16[128,1536]{1,0:T(8,128)(2,1)S(1)} %join.15.refs_4_.refs_0_), custom_call_target="tpu_custom_call" | custom-call | flops 4000000000 | bytes 1024 | tf_op jit(solution)/shard_map/down/pallas_call | solution.py:60
  147.7 4.2 %down.5 = (f32[128,2048]{1,0:T(8,128)S(1)}, bf16[128,2048]{1,0:T(8,128)(2,1)S(1)}) custom-call(bf16[128,1536]{1,0:T(8,128)(2,1)S(1)} %join.15.refs_4_.refs_0_, bf16[128,1536]{1,0:T(8,128)(2,1)S(1)} %collective-permute-done.31.refs_1_, bf16[6656,2048]{1,0:T(8,128)(2,1)} %refs_2_.11, f32[256,2048]{1,0:T(8,128)S(1)} %down.4.refs_3_.refs_4_, ...), custom_call_target="tpu_custom_call" | custom-call | flops 3000000000 | bytes 1024 | tf_op jit(solution)/shard_map/down/pallas_call | solution.py:60
  152.0 1.9 %collective-permute-done.33.refs_1_ = bf16[128,2048]{1,0:T(8,128)(2,1)S(1)} collective-permute-done((bf16[128,2048]{1,0:T(8,128)(2,1)S(1)}, bf16[128,2048]{1,0:T(8,128)(2,1)S(1)}, u32[]{:S(2)}, u32[]{:S(2)}) %collective-permute-start.33) | collective-permute-done | bytes 524320 | tf_op jit(solution)/shard_map/ppermute | solution.py:33
  153.9 1.6 collective-permute-start.34
  155.5 6.8 %collective-permute-done.34.refs_2_ = bf16[64,2048]{1,0:T(8,128)(2,1)S(1)} collective-permute-done((bf16[64,2048]{1,0:T(8,128)(2,1)S(1)}, bf16[64,2048]{1,0:T(8,128)(2,1)S(1)}, u32[]{:S(2)}, u32[]{:S(2)}) %collective-permute-start.34) | collective-permute-done | bytes 262176 | tf_op jit(solution)/shard_map/ppermute | solution.py:33
  162.3 0.8 final.1
  (64 shorter events, 5.0 us)
Async XLA Ops:
  0.0 9.5 %collective-permute-start.1 = (bf16[64,2048]{1,0:T(8,128)(2,1)}, bf16[64,2048]{1,0:T(8,128)(2,1)S(1)}, u32[]{:S(2)}, u32[]{:S(2)}) collective-permute-start(bf16[64,2048]{1,0:T(8,128)(2,1)} %refs_0_.5), channel_id=1, source_target_pairs={{0,2},{1,3},{2,0},{3,1},{4,6},{5,7},{6,4},{7,5},{8,10},{9,11},{10,... | collective-permute-start | bytes 786440 | tf_op jit(solution)/shard_map/ppermute | solution.py:33
  3.0 8.4 %collective-permute-start = (bf16[64,2048]{1,0:T(8,128)(2,1)}, bf16[64,2048]{1,0:T(8,128)(2,1)S(1)}, u32[]{:S(2)}, u32[]{:S(2)}) collective-permute-start(bf16[64,2048]{1,0:T(8,128)(2,1)} %refs_0_.5), channel_id=1, source_target_pairs={{0,1},{1,0},{2,3},{3,2},{4,5},{5,4},{6,7},{7,6},{8,9},{9,8},{10,11... | collective-permute-start | bytes 786440 | tf_op jit(solution)/shard_map/ppermute | solution.py:33
  3.0 1.0 copy-start
  4.1 5.4 %collective-permute-start.3 = (f32[64,128]{1,0:T(8,128)S(1)}, f32[64,128]{1,0:T(8,128)S(1)}, u32[]{:S(2)}, u32[]{:S(2)}) collective-permute-start(f32[64,128]{1,0:T(8,128)S(1)} %squares.1.refs_1_.refs_0_), channel_id=1, source_target_pairs={{0,4},{1,9},{2,6},{3,11},{4,0},{5,13},{6,2},{7,15},{8,12},{9,1},{1... | collective-permute-start | bytes 98312 | tf_op jit(solution)/shard_map/ppermute | solution.py:33
  9.5 1.9 %copy-start.1 = (bf16[64,2048]{1,0:T(8,128)(2,1)S(1)}, bf16[64,2048]{1,0:T(8,128)(2,1)}, u32[]{:S(2)}) copy-start(bf16[64,2048]{1,0:T(8,128)(2,1)} %refs_0_.5) | copy-start | bytes 786436
  9.5 1.9 %copy-start.2 = (f32[2048]{0:T(1024)S(1)}, f32[2048]{0:T(1024)}, u32[]{:S(2)}) copy-start(f32[2048]{0:T(1024)} %param.6) | copy-start | bytes 24580
  9.5 1.9 %collective-permute-start.2 = (bf16[64,2048]{1,0:T(8,128)(2,1)S(1)}, bf16[64,2048]{1,0:T(8,128)(2,1)S(1)}, u32[]{:S(2)}, u32[]{:S(2)}) collective-permute-start(bf16[64,2048]{1,0:T(8,128)(2,1)S(1)} %pass.1.refs_2_), channel_id=1, source_target_pairs={{0,1},{1,0},{2,3},{3,2},{4,5},{5,4},{6,7},{7,6},{8,9},{9,8},{10,11... | collective-permute-start | bytes 786440 | tf_op jit(solution)/shard_map/ppermute | solution.py:33
  9.5 18.1 %collective-permute-start.4 = (f32[64,128]{1,0:T(8,128)S(1)}, f32[64,128]{1,0:T(8,128)S(1)}, u32[]{:S(2)}, u32[]{:S(2)}) collective-permute-start(f32[64,128]{1,0:T(8,128)S(1)} %squares_add.3.refs_5_.refs_0_), channel_id=1, source_target_pairs={{0,8},{1,5},{2,10},{3,7},{4,12},{5,1},{6,14},{7,3},{8,0},{9,13},{1... | collective-permute-start | bytes 98312 | tf_op jit(solution)/shard_map/ppermute | solution.py:33
  19.0 12.1 %collective-permute-start.6 = (bf16[2,128,1536]{2,1,0:T(8,128)(2,1)S(1)}, bf16[2,128,1536]{2,1,0:T(8,128)(2,1)S(1)}, u32[]{:S(2)}, u32[]{:S(2)}) collective-permute-start(bf16[2,128,1536]{2,1,0:T(8,128)(2,1)S(1)} %get-tuple-element.19), channel_id=1, source_target_pairs={{0,4},{1,9},{2,6},{3,11},{4,0},{5,13},{6,2},{7,15},{8,12},{9,1},{1... | collective-permute-start | bytes 2359304 | tf_op jit(solution)/shard_map/ppermute | solution.py:33
  27.6 6.4 %collective-permute-start.5 = (f32[64,128]{1,0:T(8,128)S(1)}, f32[64,128]{1,0:T(8,128)S(1)}, u32[]{:S(2)}, u32[]{:S(2)}) collective-permute-start(f32[64,128]{1,0:T(8,128)S(1)} %squares_add.4.refs_2_.refs_0_), channel_id=1, source_target_pairs={{0,16},{1,17},{2,18},{3,19},{4,20},{5,21},{6,22},{7,23},{8,24},{9,... | collective-permute-start | bytes 98312 | tf_op jit(solution)/shard_map/ppermute | solution.py:33
  31.1 14.1 %collective-permute-start.10 = (bf16[2,64,1536]{2,1,0:T(8,128)(2,1)S(1)}, bf16[2,64,1536]{2,1,0:T(8,128)(2,1)S(1)}, u32[]{:S(2)}, u32[]{:S(2)}) collective-permute-start(bf16[2,64,1536]{2,1,0:T(8,128)(2,1)S(1)} %add_up.8.refs_2_), channel_id=1, source_target_pairs={{0,8},{1,5},{2,10},{3,7},{4,12},{5,1},{6,14},{7,3},{8,0},{9,13},{1... | collective-permute-start | bytes 1179656 | tf_op jit(solution)/shard_map/ppermute | solution.py:33
  32.6 22.2 %collective-permute-start.11 = (bf16[2,128,1536]{2,1,0:T(8,128)(2,1)S(1)}, bf16[2,128,1536]{2,1,0:T(8,128)(2,1)S(1)}, u32[]{:S(2)}, u32[]{:S(2)}) collective-permute-start(bf16[2,128,1536]{2,1,0:T(8,128)(2,1)S(1)} %get-tuple-element.21), channel_id=1, source_target_pairs={{0,4},{1,9},{2,6},{3,11},{4,0},{5,13},{6,2},{7,15},{8,12},{9,1},{1... | collective-permute-start | bytes 2359304 | tf_op jit(solution)/shard_map/ppermute | solution.py:33
  34.1 11.7 %collective-permute-start.7 = (f32[64,128]{1,0:T(8,128)S(1)}, f32[64,128]{1,0:T(8,128)S(1)}, u32[]{:S(2)}, u32[]{:S(2)}) collective-permute-start(f32[64,128]{1,0:T(8,128)S(1)} %squares_add.5.refs_3_.refs_4_), channel_id=1, source_target_pairs={{0,1},{1,0},{2,3},{3,2},{4,5},{5,4},{6,7},{7,6},{8,9},{9,8},{10,11... | collective-permute-start | bytes 98312 | tf_op jit(solution)/shard_map/ppermute | solution.py:33
  34.2 11.6 %collective-permute-start.8 = (f32[64,128]{1,0:T(8,128)S(1)}, f32[64,128]{1,0:T(8,128)S(1)}, u32[]{:S(2)}, u32[]{:S(2)}) collective-permute-start(f32[64,128]{1,0:T(8,128)S(1)} %squares_add.5.refs_3_.refs_4_), channel_id=1, source_target_pairs={{0,2},{1,3},{2,0},{3,1},{4,6},{5,7},{6,4},{7,5},{8,10},{9,11},{10,... | collective-permute-start | bytes 98312 | tf_op jit(solution)/shard_map/ppermute | solution.py:33
  35.7 10.1 %collective-permute-start.9 = (f32[64,128]{1,0:T(8,128)S(1)}, f32[64,128]{1,0:T(8,128)S(1)}, u32[]{:S(2)}, u32[]{:S(2)}) collective-permute-start(f32[64,128]{1,0:T(8,128)S(1)} %squares_add.5.refs_3_.refs_4_), channel_id=1, source_target_pairs={{0,3},{1,2},{2,1},{3,0},{4,7},{5,6},{6,5},{7,4},{8,11},{9,10},{10,... | collective-permute-start | bytes 98312 | tf_op jit(solution)/shard_map/ppermute | solution.py:33
  45.3 20.4 %collective-permute-start.15 = (bf16[2,32,1536]{2,1,0:T(8,128)(2,1)S(1)}, bf16[2,32,1536]{2,1,0:T(8,128)(2,1)S(1)}, u32[]{:S(2)}, u32[]{:S(2)}) collective-permute-start(bf16[2,32,1536]{2,1,0:T(8,128)(2,1)S(1)} %add_up.9.refs_9_), channel_id=1, source_target_pairs={{0,16},{1,17},{2,18},{3,19},{4,20},{5,21},{6,22},{7,23},{8,24},{9,... | collective-permute-start | bytes 589832 | tf_op jit(solution)/shard_map/ppermute | solution.py:33
  54.9 15.3 %collective-permute-start.14 = (bf16[2,64,1536]{2,1,0:T(8,128)(2,1)S(1)}, bf16[2,64,1536]{2,1,0:T(8,128)(2,1)S(1)}, u32[]{:S(2)}, u32[]{:S(2)}) collective-permute-start(bf16[2,64,1536]{2,1,0:T(8,128)(2,1)S(1)} %add_up.10.refs_3_), channel_id=1, source_target_pairs={{0,8},{1,5},{2,10},{3,7},{4,12},{5,1},{6,14},{7,3},{8,0},{9,13},{1... | collective-permute-start | bytes 1179656 | tf_op jit(solution)/shard_map/ppermute | solution.py:33
  56.4 14.8 %collective-permute-start.13 = (bf16[2,128,2048]{2,1,0:T(8,128)(2,1)S(1)}, bf16[2,128,2048]{2,1,0:T(8,128)(2,1)S(1)}, u32[]{:S(2)}, u32[]{:S(2)}) collective-permute-start(bf16[2,128,2048]{2,1,0:T(8,128)(2,1)S(1)} %get-tuple-element.25), channel_id=1, source_target_pairs={{0,4},{1,9},{2,6},{3,11},{4,0},{5,13},{6,2},{7,15},{8,12},{9,1},{1... | collective-permute-start | bytes 3145736 | tf_op jit(solution)/shard_map/ppermute | solution.py:33
  65.0 24.9 %collective-permute-start.12 = (bf16[2,128,1536]{2,1,0:T(8,128)(2,1)S(1)}, bf16[2,128,1536]{2,1,0:T(8,128)(2,1)S(1)}, u32[]{:S(2)}, u32[]{:S(2)}) collective-permute-start(bf16[2,128,1536]{2,1,0:T(8,128)(2,1)S(1)} %get-tuple-element.24), channel_id=1, source_target_pairs={{0,4},{1,9},{2,6},{3,11},{4,0},{5,13},{6,2},{7,15},{8,12},{9,1},{1... | collective-permute-start | bytes 2359304 | tf_op jit(solution)/shard_map/ppermute | solution.py:33
  65.8 7.1 %collective-permute-start.18 = (bf16[32,1536]{1,0:T(8,128)(2,1)S(1)}, bf16[32,1536]{1,0:T(8,128)(2,1)S(1)}, u32[]{:S(2)}, u32[]{:S(2)}) collective-permute-start(bf16[32,1536]{1,0:T(8,128)(2,1)S(1)} %activate.4.refs_3_.refs_0_), channel_id=1, source_target_pairs={{0,16},{1,17},{2,18},{3,19},{4,20},{5,21},{6,22},{7,23},{8,24},{9,... | collective-permute-start | bytes 294920 | tf_op jit(solution)/shard_map/ppermute | solution.py:33
  70.2 8.4 %collective-permute-start.17 = (bf16[2,32,1536]{2,1,0:T(8,128)(2,1)S(1)}, bf16[2,32,1536]{2,1,0:T(8,128)(2,1)S(1)}, u32[]{:S(2)}, u32[]{:S(2)}) collective-permute-start(bf16[2,32,1536]{2,1,0:T(8,128)(2,1)S(1)} %add_up.11.refs_2_), channel_id=1, source_target_pairs={{0,16},{1,17},{2,18},{3,19},{4,20},{5,21},{6,22},{7,23},{8,24},{9,... | collective-permute-start | bytes 589832 | tf_op jit(solution)/shard_map/ppermute | solution.py:33
  71.3 18.0 %collective-permute-start.16 = (bf16[2,64,2048]{2,1,0:T(8,128)(2,1)S(1)}, bf16[2,64,2048]{2,1,0:T(8,128)(2,1)S(1)}, u32[]{:S(2)}, u32[]{:S(2)}) collective-permute-start(bf16[2,64,2048]{2,1,0:T(8,128)(2,1)S(1)} %add_up.12.refs_2_), channel_id=1, source_target_pairs={{0,8},{1,5},{2,10},{3,7},{4,12},{5,1},{6,14},{7,3},{8,0},{9,13},{1... | collective-permute-start | bytes 1572872 | tf_op jit(solution)/shard_map/ppermute | solution.py:33
  72.9 19.4 %collective-permute-start.22 = (bf16[64,1536]{1,0:T(8,128)(2,1)S(1)}, bf16[64,1536]{1,0:T(8,128)(2,1)S(1)}, u32[]{:S(2)}, u32[]{:S(2)}) collective-permute-start(bf16[64,1536]{1,0:T(8,128)(2,1)S(1)} %join.8.refs_5_.refs_0_), channel_id=1, source_target_pairs={{0,4},{1,9},{2,6},{3,11},{4,0},{5,13},{6,2},{7,15},{8,12},{9,1},{1... | collective-permute-start | bytes 589832 | tf_op jit(solution)/shard_map/ppermute | solution.py:33
  78.8 13.7 %collective-permute-start.21 = (bf16[32,1536]{1,0:T(8,128)(2,1)S(1)}, bf16[32,1536]{1,0:T(8,128)(2,1)S(1)}, u32[]{:S(2)}, u32[]{:S(2)}) collective-permute-start(bf16[32,1536]{1,0:T(8,128)(2,1)S(1)} %activate.5.refs_3_.refs_0_), channel_id=1, source_target_pairs={{0,16},{1,17},{2,18},{3,19},{4,20},{5,21},{6,22},{7,23},{8,24},{9,... | collective-permute-start | bytes 294920 | tf_op jit(solution)/shard_map/ppermute | solution.py:33
  89.4 14.3 %collective-permute-start.20 = (bf16[2,32,2048]{2,1,0:T(8,128)(2,1)S(1)}, bf16[2,32,2048]{2,1,0:T(8,128)(2,1)S(1)}, u32[]{:S(2)}, u32[]{:S(2)}) collective-permute-start(bf16[2,32,2048]{2,1,0:T(8,128)(2,1)S(1)} %add_up.13.refs_2_), channel_id=1, source_target_pairs={{0,16},{1,17},{2,18},{3,19},{4,20},{5,21},{6,22},{7,23},{8,24},{9,... | collective-permute-start | bytes 786440 | tf_op jit(solution)/shard_map/ppermute | solution.py:33
  90.0 15.2 %collective-permute-start.19 = (bf16[2,64,1536]{2,1,0:T(8,128)(2,1)S(1)}, bf16[2,64,1536]{2,1,0:T(8,128)(2,1)S(1)}, u32[]{:S(2)}, u32[]{:S(2)}) collective-permute-start(bf16[2,64,1536]{2,1,0:T(8,128)(2,1)S(1)} %add_up.14.refs_2_), channel_id=1, source_target_pairs={{0,8},{1,5},{2,10},{3,7},{4,12},{5,1},{6,14},{7,3},{8,0},{9,13},{1... | collective-permute-start | bytes 1179656 | tf_op jit(solution)/shard_map/ppermute | solution.py:33
  92.4 28.8 %collective-permute-start.28 = (bf16[128,1536]{1,0:T(8,128)(2,1)S(1)}, bf16[128,1536]{1,0:T(8,128)(2,1)S(1)}, u32[]{:S(2)}, u32[]{:S(2)}) collective-permute-start(bf16[128,1536]{1,0:T(8,128)(2,1)S(1)} %join.9.refs_2_.refs_0_), channel_id=1, source_target_pairs={{0,8},{1,5},{2,10},{3,7},{4,12},{5,1},{6,14},{7,3},{8,0},{9,13},{1... | collective-permute-start | bytes 1179656 | tf_op jit(solution)/shard_map/ppermute | solution.py:33
  92.5 14.5 %collective-permute-start.25 = (bf16[64,1536]{1,0:T(8,128)(2,1)S(1)}, bf16[64,1536]{1,0:T(8,128)(2,1)S(1)}, u32[]{:S(2)}, u32[]{:S(2)}) collective-permute-start(bf16[64,1536]{1,0:T(8,128)(2,1)S(1)} %join.10.refs_5_.refs_0_), channel_id=1, source_target_pairs={{0,4},{1,9},{2,6},{3,11},{4,0},{5,13},{6,2},{7,15},{8,12},{9,1},{1... | collective-permute-start | bytes 589832 | tf_op jit(solution)/shard_map/ppermute | solution.py:33
  103.9 11.5 %collective-permute-start.24 = (bf16[32,2048]{1,0:T(8,128)(2,1)S(1)}, bf16[32,2048]{1,0:T(8,128)(2,1)S(1)}, u32[]{:S(2)}, u32[]{:S(2)}) collective-permute-start(bf16[32,2048]{1,0:T(8,128)(2,1)S(1)} %activate.6.refs_3_.refs_0_), channel_id=1, source_target_pairs={{0,16},{1,17},{2,18},{3,19},{4,20},{5,21},{6,22},{7,23},{8,24},{9,... | collective-permute-start | bytes 393224 | tf_op jit(solution)/shard_map/ppermute | solution.py:33
  105.3 15.3 %collective-permute-start.23 = (bf16[2,32,1536]{2,1,0:T(8,128)(2,1)S(1)}, bf16[2,32,1536]{2,1,0:T(8,128)(2,1)S(1)}, u32[]{:S(2)}, u32[]{:S(2)}) collective-permute-start(bf16[2,32,1536]{2,1,0:T(8,128)(2,1)S(1)} %add_up.15.refs_2_), channel_id=1, source_target_pairs={{0,16},{1,17},{2,18},{3,19},{4,20},{5,21},{6,22},{7,23},{8,24},{9,... | collective-permute-start | bytes 589832 | tf_op jit(solution)/shard_map/ppermute | solution.py:33
  107.1 15.6 %collective-permute-start.29 = (bf16[128,1536]{1,0:T(8,128)(2,1)S(1)}, bf16[128,1536]{1,0:T(8,128)(2,1)S(1)}, u32[]{:S(2)}, u32[]{:S(2)}) collective-permute-start(bf16[128,1536]{1,0:T(8,128)(2,1)S(1)} %join.11.refs_2_), channel_id=1, source_target_pairs={{0,8},{1,5},{2,10},{3,7},{4,12},{5,1},{6,14},{7,3},{8,0},{9,13},{1... | collective-permute-start | bytes 1179656 | tf_op jit(solution)/shard_map/ppermute | solution.py:33
  115.5 13.8 %collective-permute-start.27 = (bf16[64,2048]{1,0:T(8,128)(2,1)S(1)}, bf16[64,2048]{1,0:T(8,128)(2,1)S(1)}, u32[]{:S(2)}, u32[]{:S(2)}) collective-permute-start(bf16[64,2048]{1,0:T(8,128)(2,1)S(1)} %join.12.refs_5_.refs_0_), channel_id=1, source_target_pairs={{0,8},{1,5},{2,10},{3,7},{4,12},{5,1},{6,14},{7,3},{8,0},{9,13},{1... | collective-permute-start | bytes 786440 | tf_op jit(solution)/shard_map/ppermute | solution.py:33
  120.7 8.6 %collective-permute-start.26 = (bf16[32,1536]{1,0:T(8,128)(2,1)S(1)}, bf16[32,1536]{1,0:T(8,128)(2,1)S(1)}, u32[]{:S(2)}, u32[]{:S(2)}) collective-permute-start(bf16[32,1536]{1,0:T(8,128)(2,1)S(1)} %activate.7.refs_5_.refs_0_), channel_id=1, source_target_pairs={{0,16},{1,17},{2,18},{3,19},{4,20},{5,21},{6,22},{7,23},{8,24},{9,... | collective-permute-start | bytes 294920 | tf_op jit(solution)/shard_map/ppermute | solution.py:33
  129.4 8.1 %collective-permute-start.30 = (bf16[64,1536]{1,0:T(8,128)(2,1)S(1)}, bf16[64,1536]{1,0:T(8,128)(2,1)S(1)}, u32[]{:S(2)}, u32[]{:S(2)}) collective-permute-start(bf16[64,1536]{1,0:T(8,128)(2,1)S(1)} %join.14.refs_0_.refs_2_), channel_id=1, source_target_pairs={{0,8},{1,5},{2,10},{3,7},{4,12},{5,1},{6,14},{7,3},{8,0},{9,13},{1... | collective-permute-start | bytes 589832 | tf_op jit(solution)/shard_map/ppermute | solution.py:33
  133.0 9.7 %collective-permute-start.32 = (bf16[128,2048]{1,0:T(8,128)(2,1)S(1)}, bf16[128,2048]{1,0:T(8,128)(2,1)S(1)}, u32[]{:S(2)}, u32[]{:S(2)}) collective-permute-start(bf16[128,2048]{1,0:T(8,128)(2,1)S(1)} %join.13.refs_2_.refs_0_), channel_id=1, source_target_pairs={{0,4},{1,9},{2,6},{3,11},{4,0},{5,13},{6,2},{7,15},{8,12},{9,1},{1... | collective-permute-start | bytes 1572872 | tf_op jit(solution)/shard_map/ppermute | solution.py:33
  137.5 10.2 %collective-permute-start.31 = (bf16[128,1536]{1,0:T(8,128)(2,1)S(1)}, bf16[128,1536]{1,0:T(8,128)(2,1)S(1)}, u32[]{:S(2)}, u32[]{:S(2)}) collective-permute-start(bf16[128,1536]{1,0:T(8,128)(2,1)S(1)} %join.15.refs_4_.refs_0_), channel_id=1, source_target_pairs={{0,4},{1,9},{2,6},{3,11},{4,0},{5,13},{6,2},{7,15},{8,12},{9,1},{1... | collective-permute-start | bytes 1179656 | tf_op jit(solution)/shard_map/ppermute | solution.py:33
  151.9 2.0 %collective-permute-start.33 = (bf16[128,2048]{1,0:T(8,128)(2,1)S(1)}, bf16[128,2048]{1,0:T(8,128)(2,1)S(1)}, u32[]{:S(2)}, u32[]{:S(2)}) collective-permute-start(bf16[128,2048]{1,0:T(8,128)(2,1)S(1)} %get-tuple-element.28), channel_id=1, source_target_pairs={{0,1},{1,0},{2,3},{3,2},{4,5},{5,4},{6,7},{7,6},{8,9},{9,8},{10,11... | collective-permute-start | bytes 1572872 | tf_op jit(solution)/shard_map/ppermute | solution.py:33
  153.9 8.4 %collective-permute-start.34 = (bf16[64,2048]{1,0:T(8,128)(2,1)S(1)}, bf16[64,2048]{1,0:T(8,128)(2,1)S(1)}, u32[]{:S(2)}, u32[]{:S(2)}) collective-permute-start(bf16[64,2048]{1,0:T(8,128)(2,1)S(1)} %send_y.1.refs_3_), channel_id=1, source_target_pairs={{0,2},{1,3},{2,0},{3,1},{4,6},{5,7},{6,4},{7,5},{8,10},{9,11},{10,... | collective-permute-start | bytes 786440 | tf_op jit(solution)/shard_map/ppermute | solution.py:33
